TPU v7x, 32 devices: a whole 2x2x4 slice. The times are simulated.
32 devices in a mesh: row: 4 (over x, core), col: 8 (over z, y).
Axes of the slice: x: 2, y: 2, z: 4, core: 2. Of those that a mesh axis runs over, the one named last changes fastest.
Arguments:
- stiffness: float32 [2048, 2048], P('row', 'col'), may hold values from -0.6 to 4.5
Outputs:
- factored: float32 [2048, 2048], P('row', 'col')
All inputs are finite; a program needn't handle non-finite values.
Results may differ from a plain program's by a relative error of at most 0.0001.
Values sent between devices are 32-bit elements; how exact they have to be, the bound alone decides.
No kernel may reach another device: no remote copies, remote signals or barrier semaphores. Data moves between devices by JAX's collectives and lax.ppermute only.
A program may use at most 64 MiB of HBM per device.

v0:
```python
import jax
import jax.numpy as jnp
from jax import lax
from jax.sharding import PartitionSpec as P

SNODES = 4


def broadcast(block, axis, source):
    block = jnp.where(lax.axis_index(axis) == source, block, jnp.zeros_like(block))
    return lax.psum(block, axis)


def solve_panel(columns, diag_block, global_rows, first_row):
    factor = jnp.linalg.cholesky(diag_block)
    solved = jax.scipy.linalg.solve_triangular(factor, columns.T, lower=True).T
    return jnp.where(global_rows[:, None] >= first_row, solved, jnp.zeros_like(solved))


def on_device(stiffness):
    rows_dev, width = stiffness.shape
    row_index = lax.axis_index("row")
    col_index = lax.axis_index("col")
    global_rows = row_index * rows_dev + lax.broadcasted_iota(jnp.int32, (rows_dev,), 0)
    work_tile = stiffness
    for section in range(SNODES):
        first_row = section * width
        diag_root = first_row // rows_dev
        diag_off = first_row % rows_dev
        own_block = work_tile[diag_off : diag_off + width]
        diag_block = broadcast(own_block, "row", diag_root)
        col_panel = lax.cond(
            col_index == section,
            lambda current: solve_panel(current, diag_block, global_rows, first_row),
            lambda current: jnp.zeros_like(current),
            work_tile,
        )
        col_panel = broadcast(col_panel, "col", section)
        cross_first = col_index * width
        cross_root = cross_first // rows_dev
        cross_off = cross_first % rows_dev
        my_slice = lax.dynamic_slice_in_dim(col_panel, cross_off, width, 0)
        cross_block = broadcast(my_slice, "row", cross_root)
        low_panel = jnp.where(
            global_rows[:, None] >= first_row + width, col_panel, jnp.zeros_like(col_panel)
        )

        def apply_update(current):
            update = lax.dot_general(
                low_panel, cross_block, (((1,), (1,)), ((), ())), precision=lax.Precision.HIGHEST
            )
            return current - update

        work_tile = lax.cond(col_index > section, apply_update, lambda current: current, work_tile)
        work_tile = jnp.where(col_index == section, col_panel, work_tile)
    global_cols = col_index * width + lax.broadcasted_iota(jnp.int32, (width,), 0)
    window = SNODES * width
    keep = jnp.where(
        global_cols[None, :] < window,
        global_rows[:, None] >= global_cols[None, :],
        global_rows[:, None] >= window,
    )
    return jnp.where(keep, work_tile, jnp.zeros_like(work_tile))


def solution(mesh):
    placed = (P("row", "col"),)
    return jax.shard_map(
        on_device, mesh=mesh, in_specs=placed, out_specs=P("row", "col"), check_vma=False
    )
```

profile of v0, /device:TPU:19, one launch (start us, length us, event | category | flops | bytes accessed | tf_op | source)
XLA Modules:
  0.0 822.9 jit_solution(17191251707258830042)
XLA Ops:
  6.5 1.0 copy.95
  7.6 0.7 slice_select_fusion.3
  8.3 0.0 all-reduce.16.cloned.1.call-start
  8.4 32.6 %all-reduce.14.cloned.1.call-done = f32[256,256]{1,0:T(8,128)} async-done(((f32[256,256]{1,0:T(8,128)}), f32[256,256]{1,0:T(8,128)}) %all-reduce.14.cloned.1.call-update) | async-done | bytes 262160 | tf_op jit(solution)/shard_map/psum | solution.py:11
  41.0 8.4 %conditional.8 = (f32[512,256]{1,0:T(8,128)S(1)}) conditional(s32[]{:T(128)} %convert_element_type.27, () %tuple.61, (s32[512]{0:T(512)S(1)}, f32[256,256]{1,0:T(8,128)}, f32[512,256]{1,0:T(8,128)S(1)}) %tuple.62), branch_computations={%region_1.2_spmd, %region_2.9_spmd} | conditional | flops 353190656 | bytes 8393963 | solution.py:32
  49.4 0.8 broadcast_select_fusion.3
  50.2 0.0 all-reduce.18.cloned.1.call-start
  50.3 121.6 %all-reduce.16.cloned.1.call-done = f32[512,256]{1,0:T(8,128)} async-done(((f32[512,256]{1,0:T(8,128)}), f32[512,256]{1,0:T(8,128)}) %all-reduce.16.cloned.1.call-update) | async-done | bytes 524304 | tf_op jit(solution)/shard_map/psum | solution.py:11
  171.9 1.7 dynamic-slice_select_fusion.3
  173.6 0.0 all-reduce.20.cloned.1.call-start
  173.7 32.9 %all-reduce.18.cloned.1.call-done = f32[256,256]{1,0:T(8,128)} async-done(((f32[256,256]{1,0:T(8,128)}), f32[256,256]{1,0:T(8,128)}) %all-reduce.18.cloned.1.call-update) | async-done | bytes 262160 | tf_op jit(solution)/shard_map/psum | solution.py:11
  206.6 0.9 copy-done.8
  207.5 0.8 conditional.9
  207.6 0.8 convolution_subtract_fusion.9
  208.3 0.1 broadcast_select_fusion.4
  208.4 0.7 slice_select_fusion.2
  209.2 32.1 %all-reduce.20.cloned.1.call-done = f32[256,256]{1,0:T(8,128)} async-done(((f32[256,256]{1,0:T(8,128)}), f32[256,256]{1,0:T(8,128)}) %all-reduce.20.cloned.1.call-update) | async-done | bytes 262160 | tf_op jit(solution)/shard_map/psum | solution.py:11
  241.3 8.5 %conditional.10 = (f32[512,256]{1,0:T(8,128)S(1)}) conditional(s32[]{:T(128)} %convert_element_type.26, () %tuple.60, (s32[512]{0:T(512)S(1)}, f32[256,256]{1,0:T(8,128)}, f32[512,256]{1,0:T(8,128)S(1)}) %tuple.64), branch_computations={%region_12.15_spmd, %region_13.16_spmd} | conditional | flops 353190656 | bytes 8393963 | solution.py:32
  249.8 0.8 broadcast_select_fusion.2
  250.6 0.0 all-reduce.24.cloned.1.call-start
  250.7 123.0 %all-reduce.22.cloned.1.call-done = f32[512,256]{1,0:T(8,128)} async-done(((f32[512,256]{1,0:T(8,128)}), f32[512,256]{1,0:T(8,128)}) %all-reduce.22.cloned.1.call-update) | async-done | bytes 524304 | tf_op jit(solution)/shard_map/psum | solution.py:11
  373.7 1.7 dynamic-slice_select_fusion.2
  375.5 32.8 %all-reduce.24.cloned.1.call-done = f32[256,256]{1,0:T(8,128)} async-done(((f32[256,256]{1,0:T(8,128)}), f32[256,256]{1,0:T(8,128)}) %all-reduce.24.cloned.1.call-update) | async-done | bytes 262160 | tf_op jit(solution)/shard_map/psum | solution.py:11
  408.3 1.7 conditional.11
  408.4 1.7 convolution_subtract_fusion.10
  410.1 0.1 broadcast_select_fusion.5
  410.2 0.7 slice_select_fusion.1
  411.0 32.1 %all-reduce.26.cloned.1.call-done = f32[256,256]{1,0:T(8,128)} async-done(((f32[256,256]{1,0:T(8,128)}), f32[256,256]{1,0:T(8,128)}) %all-reduce.26.cloned.1.call-update) | async-done | bytes 262160 | tf_op jit(solution)/shard_map/psum | solution.py:11
  443.0 8.3 %conditional.12 = (f32[512,256]{1,0:T(8,128)S(1)}) conditional(s32[]{:T(128)} %convert_element_type.25, () %tuple.59, (s32[512]{0:T(512)S(1)}, f32[256,256]{1,0:T(8,128)}, f32[512,256]{1,0:T(8,128)S(1)}) %tuple.66), branch_computations={%region_19.22_spmd, %region_20.23_spmd} | conditional | flops 353190656 | bytes 8393963 | solution.py:32
  451.4 0.8 broadcast_select_fusion.1
  452.2 0.0 all-reduce.30.cloned.1.call-start
  452.3 123.1 %all-reduce.28.cloned.1.call-done = f32[512,256]{1,0:T(8,128)} async-done(((f32[512,256]{1,0:T(8,128)}), f32[512,256]{1,0:T(8,128)}) %all-reduce.28.cloned.1.call-update) | async-done | bytes 524304 | tf_op jit(solution)/shard_map/psum | solution.py:11
  575.3 1.7 dynamic-slice_select_fusion.1
  577.2 32.9 %all-reduce.30.cloned.1.call-done = f32[256,256]{1,0:T(8,128)} async-done(((f32[256,256]{1,0:T(8,128)}), f32[256,256]{1,0:T(8,128)}) %all-reduce.30.cloned.1.call-update) | async-done | bytes 262160 | tf_op jit(solution)/shard_map/psum | solution.py:11
  610.0 1.7 conditional.13
  610.1 1.7 convolution_subtract_fusion.11
  611.8 0.1 broadcast_select_fusion.6
  611.8 0.7 slice_select_fusion
  612.6 32.1 %all-reduce.32.cloned.1.call-done = f32[256,256]{1,0:T(8,128)} async-done(((f32[256,256]{1,0:T(8,128)}), f32[256,256]{1,0:T(8,128)}) %all-reduce.32.cloned.1.call-update) | async-done | bytes 262160 | tf_op jit(solution)/shard_map/psum | solution.py:11
  644.7 1.9 conditional.14
  646.6 0.8 broadcast_select_fusion
  647.5 0.0 all-reduce.36.cloned.1.call-start
  647.5 130.6 %all-reduce.34.cloned.1.call-done = f32[512,256]{1,0:T(8,128)} async-done(((f32[512,256]{1,0:T(8,128)}), f32[512,256]{1,0:T(8,128)}) %all-reduce.34.cloned.1.call-update) | async-done | bytes 524304 | tf_op jit(solution)/shard_map/psum | solution.py:11
  778.1 1.7 dynamic-slice_select_fusion
  779.9 32.8 %all-reduce.36.cloned.1.call-done = f32[256,256]{1,0:T(8,128)} async-done(((f32[256,256]{1,0:T(8,128)}), f32[256,256]{1,0:T(8,128)}) %all-reduce.36.cloned.1.call-update) | async-done | bytes 262160 | tf_op jit(solution)/shard_map/psum | solution.py:11
  812.8 1.7 conditional.15
  812.8 1.7 convolution_subtract_fusion
  814.5 1.0 select_select_fusion.4
  (40 shorter events, 0.7 us)
Async XLA Ops:
  6.5 34.5 %all-reduce.14.cloned.1.call-start = ((), (), s32[]{:S(2)}) async-start(), calls=%async_computation | async-start | bytes 524288 | tf_op jit(solution)/shard_map/psum | solution.py:11
  8.3 163.6 %all-reduce.16.cloned.1.call-start = ((), (), s32[]{:S(2)}) async-start(), calls=%async_computation.1 | async-start | bytes 1048576 | tf_op jit(solution)/shard_map/psum | solution.py:11
  50.2 156.4 %all-reduce.18.cloned.1.call-start = ((), (), s32[]{:S(2)}) async-start(), calls=%async_computation.2 | async-start | bytes 524288 | tf_op jit(solution)/shard_map/psum | solution.py:11
  173.6 33.1 %copy-start = (f32[512,256]{1,0:T(8,128)S(1)}, f32[512,256]{1,0:T(8,128)}, u32[]{:S(2)}) copy-start(f32[512,256]{1,0:T(8,128)} %all-reduce.16.cloned.1.call-done) | copy-start | bytes 1572868
  173.6 67.7 %all-reduce.20.cloned.1.call-start = ((), (), s32[]{:S(2)}) async-start(), calls=%async_computation.3 | async-start | bytes 524288 | tf_op jit(solution)/shard_map/psum | solution.py:11
  206.6 0.9 copy-start.8
  209.2 164.5 %all-reduce.22.cloned.1.call-start = ((), (), s32[]{:S(2)}) async-start(), calls=%async_computation.4 | async-start | bytes 1048576 | tf_op jit(solution)/shard_map/psum | solution.py:11
  250.6 157.7 %all-reduce.24.cloned.1.call-start = ((), (), s32[]{:S(2)}) async-start(), calls=%async_computation.5 | async-start | bytes 524288 | tf_op jit(solution)/shard_map/psum | solution.py:11
  373.7 34.6 %copy-start.2 = (f32[512,256]{1,0:T(8,128)S(1)}, f32[512,256]{1,0:T(8,128)}, u32[]{:S(2)}) copy-start(f32[512,256]{1,0:T(8,128)} %all-reduce.22.cloned.1.call-done) | copy-start | bytes 1572868
  375.5 67.6 %all-reduce.26.cloned.1.call-start = ((), (), s32[]{:S(2)}) async-start(), calls=%async_computation.6 | async-start | bytes 524288 | tf_op jit(solution)/shard_map/psum | solution.py:11
  410.9 164.4 %all-reduce.28.cloned.1.call-start = ((), (), s32[]{:S(2)}) async-start(), calls=%async_computation.7 | async-start | bytes 1048576 | tf_op jit(solution)/shard_map/psum | solution.py:11
  452.2 157.8 %all-reduce.30.cloned.1.call-start = ((), (), s32[]{:S(2)}) async-start(), calls=%async_computation.8 | async-start | bytes 524288 | tf_op jit(solution)/shard_map/psum | solution.py:11
  575.3 34.7 %copy-start.3 = (f32[512,256]{1,0:T(8,128)S(1)}, f32[512,256]{1,0:T(8,128)}, u32[]{:S(2)}) copy-start(f32[512,256]{1,0:T(8,128)} %all-reduce.28.cloned.1.call-done) | copy-start | bytes 1572868
  577.1 67.6 %all-reduce.32.cloned.1.call-start = ((), (), s32[]{:S(2)}) async-start(), calls=%async_computation.9 | async-start | bytes 524288 | tf_op jit(solution)/shard_map/psum | solution.py:11
  612.6 165.5 %all-reduce.34.cloned.1.call-start = ((), (), s32[]{:S(2)}) async-start(), calls=%async_computation.10 | async-start | bytes 1048576 | tf_op jit(solution)/shard_map/psum | solution.py:11
  647.5 165.3 %all-reduce.36.cloned.1.call-start = ((), (), s32[]{:S(2)}) async-start(), calls=%async_computation.11 | async-start | bytes 524288 | tf_op jit(solution)/shard_map/psum | solution.py:11
  778.1 34.6 %copy-start.1 = (f32[512,256]{1,0:T(8,128)S(1)}, f32[512,256]{1,0:T(8,128)}, u32[]{:S(2)}) copy-start(f32[512,256]{1,0:T(8,128)} %all-reduce.34.cloned.1.call-done) | copy-start | bytes 1572868
Sparse Core Ops, SparseCore 0:
  9.7 31.2 all-reduce.13
  50.4 121.5 all-reduce.15
  174.2 32.3 all-reduce.17
  209.3 31.9 all-reduce.19
  250.8 122.8 all-reduce.21
  376.0 32.2 all-reduce.23
  411.0 31.9 all-reduce.25
  452.3 122.9 all-reduce.27
  577.7 32.3 all-reduce.29
  612.7 31.9 all-reduce.31
  648.1 129.9 all-reduce.33
  780.4 32.2 all-reduce.35
where the time goes:
time: 833 us; the launch traced here: 823 us
  waiting for transfers between devices  759 us (91%)
  loops' own time  26.9 us (3%)
  other arithmetic  14.4 us (2%)
  between operations  14.4 us (2%)
    psum x12, waiting for transfers between devices, broadcast(): return lax.psum(block, axis)  759 us
    another operation x4, loops' own time, on_device(): lax.cond(col_index == section, lambda current: solve_panel(current, diag_...  26.9 us
  transfers between devices with their start and end apart: 12, of which 12 were waited for; matrix products, arithmetic and copies ran while one was open for 0% of the time, Pallas kernels for 0%

commit v1 on v0

v1 whole, which is shorter than its diff:
```python
import functools

import jax
import jax.numpy as jnp
from jax import lax
from jax.experimental import pallas as pl
from jax.experimental.pallas import tpu as pltpu
from jax.sharding import PartitionSpec as P

SNODES = 4
LANES = 128
SUB = 8
f32 = jnp.float32
bf16 = jnp.bfloat16
VMEM = pl.BlockSpec(memory_space=pltpu.VMEM)
SMEM = pl.BlockSpec(memory_space=pltpu.SMEM)
PARAMS = pltpu.CompilerParams(vmem_limit_bytes=56 * 2**20)


def lane_copy(tile, lane):
    return jnp.broadcast_to(tile[:, lane : lane + 1], (SUB, LANES))


def row_copy(tile, row):
    return jnp.broadcast_to(tile[row : row + 1, :], (SUB, LANES))


def factor_half(block):
    lane = lax.broadcasted_iota(jnp.int32, (SUB, LANES), 1)
    sub = lax.broadcasted_iota(jnp.int32, (SUB, LANES), 0)
    n = LANES // SUB
    tiles = [block[SUB * t : SUB * t + SUB, :] for t in range(n)]
    upper, inverse = [], []
    diag = [lane_copy(tiles[0], k) for k in range(SUB)]
    for p in range(n):
        rows, base = tiles[p], SUB * p
        up = jnp.zeros((SUB, LANES), f32)
        inv = up
        pivot_rows, scales, roots = [], [], []
        for j in range(SUB):
            at = base + j
            root = lax.rsqrt(row_copy(diag[j], j))
            column = diag[j] * root
            up_row = row_copy(rows, j) * root
            inv_row = jnp.where(lane == at, root, up_row)
            rows = jnp.where(lane == at, 0.0, rows) - column * inv_row
            scale = [None] * SUB
            for k in range(j + 1, SUB):
                scale[k] = row_copy(column, k)
                diag[k] = diag[k] - column * scale[k]
            up = jnp.where(sub == j, up_row, up)
            inv = jnp.where(sub == j, inv_row, inv)
            pivot_rows.append(jnp.where((lane > at) & (lane < base + SUB), 0.0, inv_row))
            scales.append(scale)
            roots.append(root)
        upper.append(up)
        inverse.append(inv)
        ahead = None
        for t in range(p + 1, n):
            left = [lane_copy(tiles[t], base + k) for k in range(SUB)]
            if t == p + 1:
                ahead = [lane_copy(tiles[t], base + SUB + k) for k in range(SUB)]
            rest = jnp.where((lane >= base) & (lane < base + SUB), 0.0, tiles[t])
            for j in range(SUB):
                column = left[j] * roots[j]
                rest = rest - column * pivot_rows[j]
                for k in range(j + 1, SUB):
                    left[k] = left[k] - column * scales[j][k]
                if t == p + 1:
                    for k in range(SUB):
                        ahead[k] = ahead[k] - column * row_copy(column, k)
            tiles[t] = rest
        diag = ahead
    return jnp.concatenate(upper, 0), jnp.concatenate(inverse, 0)


def split(x):
    high = x.astype(bf16)
    return high, (x - high.astype(f32)).astype(bf16)


def as_left(x):
    high, low = split(x)
    return jnp.concatenate([high, high, low], axis=1)


def as_right(x):
    high, low = split(x)
    return jnp.concatenate([high, low, high], axis=1)


def dot_t(left, right):
    return lax.dot_general(left, right, (((1,), (1,)), ((), ())), preferred_element_type=f32)


def dot_plain(a, b):
    def dot(x, y):
        return lax.dot_general(x, y, (((1,), (0,)), ((), ())), preferred_element_type=f32)

    (ah, al), (bh, bl) = split(a), split(b)
    return dot(ah, bh) + dot(ah, bl) + dot(al, bh)


def lower(x):
    row = lax.broadcasted_iota(jnp.int32, x.shape, 0)
    col = lax.broadcasted_iota(jnp.int32, x.shape, 1)
    return jnp.where(row >= col, x, 0.0)


def factor_block(block, factor_ref, inv_ref, col):
    h = LANES
    up_a, inv_a = factor_half(block[:h, :h])
    inv_a = lower(inv_a)
    low = dot_t(as_left(block[h:, :h]), as_right(inv_a))
    up_b, inv_b = factor_half(block[h:, h:] - dot_t(as_left(low), as_right(low)))
    inv_b = lower(inv_b)
    inv_low = -dot_plain(inv_b, dot_plain(low, inv_a))
    zero = jnp.zeros((h, h), f32)
    factor_ref[:h, col : col + h] = lower(up_a.T)
    factor_ref[:h, col + h : col + 2 * h] = zero
    factor_ref[h:, col : col + h] = low
    factor_ref[h:, col + h : col + 2 * h] = lower(up_b.T)
    inv = jnp.concatenate([jnp.concatenate([inv_a, zero], 1), jnp.concatenate([inv_low, inv_b], 1)], 0)
    inv_ref[...] = as_right(inv)


def chain_body(take, k, width, refs):
    inv_refs, right_refs = refs[:k], refs[k : 2 * k]
    factor_ref, inv_ref, right_ref, left = refs[2 * k :]
    w = width
    for j in range(k):
        rest = take(j)
        if j > 0:
            rest = rest - dot_t(left[:, : 3 * w * j], right_refs[j][:, : 3 * w * j])
        row = dot_t(as_left(rest), inv_refs[j][...])
        factor_ref[:, w * j : w * j + w] = row
        left[:, 3 * w * j : 3 * w * (j + 1)] = as_left(row)
        right_ref[:, 3 * w * j : 3 * w * (j + 1)] = as_right(row)
    block = take(k)
    if k > 0:
        block = block - dot_t(left[:, : 3 * w * k], right_ref[:, : 3 * w * k])
    else:
        right_ref[...] = jnp.zeros_like(right_ref)
    factor_block(block, factor_ref, inv_ref, w * k)


def chain_call(kernel, k, width, inputs, specs, state):
    invs, rights = state
    wide = 3 * width * max(1, k)
    factor, inv, right = pl.pallas_call(
        kernel,
        out_shape=[
            jax.ShapeDtypeStruct((width, (k + 1) * width), f32),
            jax.ShapeDtypeStruct((width, 3 * width), bf16),
            jax.ShapeDtypeStruct((width, wide), bf16),
        ],
        in_specs=specs + [VMEM] * (2 * k),
        out_specs=[VMEM] * 3,
        scratch_shapes=[pltpu.VMEM((width, wide), bf16)],
        compiler_params=PARAMS,
        name=f"chain{k}",
    )(*inputs, *invs, *rights)
    return factor, (invs + [inv], rights + [right])


def solve_rows(take, rows, extra, inv_refs, right_refs, left, right, factor_rows, width):
    w = width
    for k in range(SNODES):
        rest = take(k)
        if k > 0:
            rest = rest - dot_t(left[:, : 3 * w * k], right_refs[k][:, : 3 * w * k])
        row = dot_t(as_left(rest), inv_refs[k][...])
        left[:, 3 * w * k : 3 * w * (k + 1)] = as_left(row)
        right[:, 3 * w * k : 3 * w * (k + 1)] = as_right(row[rows:])
        factor_rows(k, row[:rows])


def write_tile(pos_ref, take, tile_ref, inv_refs, right_refs, factor_refs, out_ref, left, right, width):
    row_index, col_index = pos_ref[0], pos_ref[1]
    rows = out_ref.shape[0]
    blocks = rows // width
    inside = SNODES * width // rows
    top = row_index < inside

    @pl.when(jnp.logical_not(top))
    def _():
        def factor_rows(k, value):
            @pl.when(col_index == k)
            def _():
                out_ref[...] = value

        solve_rows(take, rows, width, inv_refs, right_refs, left, right, factor_rows, width)

        @pl.when(col_index >= SNODES)
        def _():
            out_ref[...] = tile_ref[...] - dot_t(left[:rows], right[...])

    @pl.when(top)
    def _():
        out_ref[...] = jnp.zeros_like(out_ref)
        for i in range(SNODES):
            for j in range(i + 1):

                @pl.when((row_index == i // blocks) & (col_index == j))
                def _():
                    at = (i % blocks) * width
                    out_ref[at : at + width, :] = factor_refs[i][:, j * width : (j + 1) * width]


def plain_chain(k, width, *refs):
    block_ref = refs[0]
    chain_body(lambda j: block_ref[:, j * width : (j + 1) * width], k, width, refs[1:])


def plain_tile(width, *refs):
    pos_ref, below_ref, tile_ref = refs[:3]
    n = SNODES
    inv_refs, right_refs, factor_refs = refs[3 : 3 + n], refs[3 + n : 3 + 2 * n], refs[3 + 2 * n : 3 + 3 * n]
    out_ref, left, right = refs[3 + 3 * n :]
    write_tile(
        pos_ref,
        lambda k: below_ref[:, k * width : (k + 1) * width],
        tile_ref, inv_refs, right_refs, factor_refs, out_ref, left, right, width,
    )


def tile_call(kernel, inputs, state, factors, rows, width):
    invs, rights = state
    wide = 3 * width * SNODES
    return pl.pallas_call(
        kernel,
        out_shape=jax.ShapeDtypeStruct((rows, width), f32),
        in_specs=[SMEM] + [VMEM] * (len(inputs) - 1 + 3 * SNODES),
        out_specs=VMEM,
        scratch_shapes=[pltpu.VMEM((rows + width, wide), bf16), pltpu.VMEM((width, wide), bf16)],
        compiler_params=PARAMS,
        name="tile",
    )(*inputs, *invs, *rights, *factors)


def any_mesh(stiffness):
    rows, width = stiffness.shape
    row_index, col_index = lax.axis_index("row"), lax.axis_index("col")
    inside = SNODES * width // rows
    zero = jnp.zeros_like(stiffness)
    own_rows = lax.psum(
        jnp.concatenate([jnp.where(col_index == j, stiffness, zero) for j in range(SNODES)], 1), "col"
    )
    window = lax.psum(
        jnp.concatenate([jnp.where(row_index == i, own_rows, jnp.zeros_like(own_rows)) for i in range(inside)], 0), "row"
    )
    own_cols = lax.psum(jnp.concatenate([jnp.where(row_index == i, stiffness, zero) for i in range(inside)], 0), "row")
    state, factors = ([], []), []
    for k in range(SNODES):
        block = window[k * width : (k + 1) * width, : (k + 1) * width]
        factor, state = chain_call(functools.partial(plain_chain, k, width), k, width, [block], [VMEM], state)
        factors.append(factor)
    below = jnp.concatenate([own_rows, own_cols.T], 0)
    pos = jnp.stack([row_index, col_index]).astype(jnp.int32)
    return tile_call(
        functools.partial(plain_tile, width), [pos, below, stiffness], state, factors, rows, width
    )


def chain_first(width, pos_ref, a_ref, b_ref, *refs):
    even = (pos_ref[0] % 2) == 0
    chain_body(lambda j: jnp.where(even, a_ref[...], b_ref[...]), 0, width, refs)


def chain_second(width, pos_ref, a_ref, b_ref, *refs):
    even = (pos_ref[0] % 2) == 0
    chain_body(lambda j: jnp.where(even, a_ref[j], b_ref[j]), 1, width, refs)


def chain_later(k, width, pos_ref, a_ref, b_ref, a_other, b_other, *refs):
    core = pos_ref[0] % 2
    first = (pos_ref[1] % 2) == k % 2

    def take(j):
        own = core == j // 2
        mine = jnp.where(own, a_ref[j % 2], a_other[j % 2])
        other = jnp.where(own, b_ref[j % 2], b_other[j % 2])
        return jnp.where(first, mine, other)

    chain_body(take, k, width, refs)


def box_tile(width, *refs):
    pos_ref, tile_ref = refs[:2]
    below, crossed, other = refs[2:6], refs[6:10], refs[10:14]
    rest = refs[14:]
    n = SNODES
    inv_refs, right_refs, factor_refs = rest[:n], rest[n : 2 * n], rest[2 * n : 3 * n]
    out_ref, left, right, work = rest[3 * n :]
    row_index, col_index = pos_ref[0], pos_ref[1]
    core = row_index % 2
    w = width

    @pl.when((row_index >= 2) & (col_index < n))
    def _():
        for m in range(4):
            for k in range(n):

                @pl.when((col_index ^ m) == k)
                def _():
                    work[k, :w, :] = below[m][0]
                    work[k, w : 2 * w, :] = below[m][1]

    @pl.when((row_index >= 2) & (col_index >= n))
    def _():
        for k in range(n):
            for place in range(3):
                want = col_index if place == 2 else n + 2 * core + place
                for m in range(4):

                    @pl.when((col_index ^ m) == want)
                    def _():
                        work[k, place * w : (place + 1) * w, :] = jnp.where(
                            core == k // 2, crossed[m][k % 2], other[m][k % 2]
                        )

    write_tile(
        pos_ref, lambda k: work[k], tile_ref, inv_refs, right_refs, factor_refs, out_ref, left, right, width
    )


def swap(x, pair):
    perm = []
    for r in range(4):
        for c in range(8):
            pr, pc = pair(r, c)
            perm.append((r * 8 + c, pr * 8 + pc))
    return lax.ppermute(x, ("row", "col"), perm)


def across(members):
    def pair(r, c):
        if r < 2 and c < 4 and members(r, c):
            return r + 2, c + 4
        if r >= 2 and c >= 4 and members(r - 2, c - 4):
            return r - 2, c - 4
        return r, c

    return pair


def core_pair(r, c):
    return r ^ 1, c


def x_pair(r, c):
    return r ^ 2, c


def y_pair(r, c):
    return r, c ^ 1


def z_pair(r, c):
    return r, c ^ 2


def mixed(r, c):
    return (r >= 2) != (c >= 4)


def some(pair, members):
    return lambda r, c: pair(r, c) if members(r, c) else (r, c)


def box_mesh(stiffness):
    rows, width = stiffness.shape
    r, c = lax.axis_index("row"), lax.axis_index("col")
    pos = jnp.stack([r, c]).astype(jnp.int32)
    blocks = stiffness.reshape(2, width, width)
    first = (r == 0) & (c == 0)

    d = blocks[0]
    d = jnp.where((r == 2) & (c == 4), swap(d, across(lambda r, c: (r, c) == (0, 0))), d)
    q = jnp.where(r < 2, blocks.transpose(0, 2, 1), blocks)
    d = jnp.where(c % 2 == 0, d, swap(d, y_pair))
    d = jnp.where((c // 2) % 2 == 0, d, swap(d, z_pair))
    d = jnp.where((r >= 2) & (c < 4), swap(d, x_pair), d)
    d_other = swap(d, core_pair)

    xq = swap(q, x_pair)
    e = swap(q, across(lambda r, c: (r, c) == (0, 1)))
    e = jnp.where(r < 2, q, jnp.where(c < 4, xq, e))
    e = jnp.where(c % 2 == 1, e, swap(e, y_pair))
    e = jnp.where((c // 2) % 2 == 0, e, swap(e, z_pair))
    e_other = swap(e, core_pair)

    g = swap(q, across(lambda r, c: c >= 2))
    g = jnp.where(r < 2, q, jnp.where(c < 4, xq, g))
    gy = swap(g, y_pair)
    odd = (c // 2) % 2 == 1
    g = jnp.where(odd, g, swap(g, z_pair))
    gy = jnp.where(odd, gy, swap(gy, z_pair))
    g_other, gy_other = swap(g, core_pair), swap(gy, core_pair)

    yq, zq = swap(q, some(y_pair, mixed)), swap(q, some(z_pair, mixed))
    yzq = swap(zq, some(y_pair, mixed))
    xzq, xyq = swap(zq, x_pair), swap(yq, x_pair)
    xyzq = swap(xzq, y_pair)
    crossed = [xq, xyq, xzq, xyzq]
    other = [swap(v, core_pair) for v in crossed]

    state, factors = ([], []), []
    for k in range(SNODES):
        if k == 0:
            kernel, inputs = chain_first, [pos, d, d_other]
        elif k == 1:
            kernel, inputs = chain_second, [pos, e, e_other]
        else:
            kernel, inputs = functools.partial(chain_later, k), [pos, g, gy, g_other, gy_other]
        factor, state = chain_call(
            functools.partial(kernel, width), k, width, inputs, [SMEM] + [VMEM] * (len(inputs) - 1), state
        )
        factors.append(factor)
    invs, rights = state
    wide = 3 * width * SNODES
    inputs = [pos, stiffness, q, yq, zq, yzq, *crossed, *other]
    return pl.pallas_call(
        functools.partial(box_tile, width),
        out_shape=jax.ShapeDtypeStruct((rows, width), f32),
        in_specs=[SMEM] + [VMEM] * (len(inputs) - 1 + 3 * SNODES),
        out_specs=VMEM,
        scratch_shapes=[
            pltpu.VMEM((rows + width, wide), bf16),
            pltpu.VMEM((width, wide), bf16),
            pltpu.VMEM((SNODES, rows + width, width), f32),
        ],
        compiler_params=PARAMS,
        name="tile",
    )(*inputs, *invs, *rights, *factors)


def solution(mesh):
    box = (mesh.shape["row"], mesh.shape["col"]) == (4, 8)

    def on_device(stiffness):
        rows, width = stiffness.shape
        return box_mesh(stiffness) if box and rows == 2 * width else any_mesh(stiffness)

    return jax.shard_map(
        on_device, mesh=mesh, in_specs=(P("row", "col"),), out_specs=P("row", "col"), check_vma=False
    )
```

time: 833 us -> 141 us (0.17); the launches traced: 823 us -> 140 us
  waiting for transfers between devices: 759 us -> 41.1 us
  Pallas kernels: 0 us -> 52.3 us
  starting transfers between devices: 0.46 us -> 38.9 us
  loops' own time: 26.9 us -> 0 us
  between operations: 14.4 us -> 0.37 us
  other arithmetic: 14.4 us -> 4.42 us
    psum x12 -> x0, waiting for transfers between devices: 759 us -> none  [broadcast(): return lax.psum(block, axis)]
    pallas_call x0 -> x5, Pallas kernels: none -> 52.3 us  [the longest x4 38.5 us: chain_call(): pl.pallas_call(kernel, out_shape=[jax.ShapeDtypeStruct((width, (k + 1) *...]
    ppermute x0 -> x26, waiting for transfers between devices: none -> 41.1 us  [swap(): return lax.ppermute(x, ('row', 'col'), perm)]
    ppermute x0 -> x26, starting transfers between devices: none -> 38.9 us  [swap(): return lax.ppermute(x, ('row', 'col'), perm)]
    another operation x8 -> x0, loops' own time: 26.9 us -> none  [the longest x4 26.9 us: on_device(): lax.cond(col_index == section, lambda current: solve_panel(current, diag_...]
    select_n x16 -> x10, other arithmetic: 14.3 us -> 3.76 us  [the longest x1 1.18 us: box_mesh(): g = jnp.where(r < 2, q, jnp.where(c < 4, xq, g))]
  transfers between devices with their start and end apart: 12 -> 26, of which waited for: 12 -> 7; matrix products, arithmetic and copies ran while one was open for 0% -> 3% of each run, Pallas kernels for 0% -> 27%
where the time goes in v1:
time: 141 us; the launch traced here: 140 us
  Pallas kernels  52.3 us (37%)
  waiting for transfers between devices  41.1 us (29%)
  starting transfers between devices  38.9 us (28%)
  other arithmetic  4.42 us (3%)
  local copies, waits for them, and re-layouts  2.87 us (2%)
    ppermute x26, waiting for transfers between devices, swap(): return lax.ppermute(x, ('row', 'col'), perm)  41.1 us
    ppermute x26, starting transfers between devices, swap(): return lax.ppermute(x, ('row', 'col'), perm)  38.9 us
    pallas_call x4, Pallas kernels, chain_call(): pl.pallas_call(kernel, out_shape=[jax.ShapeDtypeStruct((width, (k + 1) *...  38.5 us
    pallas_call x1, Pallas kernels, box_mesh(): pl.pallas_call(functools.partial(box_tile, width), out_shape=jax.ShapeDty...  13.8 us
  transfers between devices with their start and end apart: 26, of which 7 were waited for; matrix products, arithmetic and copies ran while one was open for 3% of the time, Pallas kernels for 27%

profile of v1, /device:TPU:19, one launch (start us, length us, event | category | flops | bytes accessed | tf_op | source)
XLA Modules:
  0.0 140.0 jit_solution(11470623211710284787)
XLA Ops:
  0.0 1.3 copy.2
  1.3 0.1 broadcast_select_fusion.4.refs_2_
  1.4 0.3 collective-permute-start.3
  1.7 0.7 collective-permute-start.16
  2.4 1.5 %collective-permute-start.20 = (f32[2,256,256]{2,1,0:T(8,128)S(1)}, f32[2,256,256]{2,1,0:T(8,128)}, u32[]{:S(2)}, u32[]{:S(2)}) collective-permute-start(f32[2,256,256]{2,1,0:T(8,128)S(1)} %broadcast_select_fusion.4.refs_2_), channel_id=1, source_target_pairs={{0,0},{1,1},{2,22},{3,23},{4,4},{5,5},{6,6},{7,7},{8,8},{9,9},{10,... | collective-permute-start | bytes 1572872 | tf_op jit(solution)/shard_map/ppermute | solution.py:333
  3.9 0.7 collective-permute-start.11
  4.6 0.7 collective-permute-start.1
  5.3 1.4 %collective-permute-start = (f32[2,256,256]{2,1,0:T(8,128)S(1)}, f32[2,256,256]{2,1,0:T(8,128)}, u32[]{:S(2)}, u32[]{:S(2)}) collective-permute-start(f32[2,256,256]{2,1,0:T(8,128)S(1)} %broadcast_select_fusion.4.refs_2_), channel_id=1, source_target_pairs={{0,0},{1,1},{2,2},{3,3},{4,5},{5,4},{6,7},{7,6},{8,8},{9,9},{10,10... | collective-permute-start | bytes 1572872 | tf_op jit(solution)/shard_map/ppermute | solution.py:333
  6.8 10.3 %collective-permute-done.3.refs_6_ = f32[2,256,256]{2,1,0:T(8,128)S(1)} collective-permute-done((f32[2,256,256]{2,1,0:T(8,128)S(1)}, f32[2,256,256]{2,1,0:T(8,128)S(1)}, u32[]{:S(2)}, u32[]{:S(2)}) %collective-permute-start.3) | collective-permute-done | bytes 524320 | tf_op jit(solution)/shard_map/ppermute | solution.py:333
  17.1 4.0 %collective-permute-start.12 = (f32[256,256]{1,0:T(8,128)S(1)}, f32[256,256]{1,0:T(8,128)S(1)}, u32[]{:S(2)}, u32[]{:S(2)}) collective-permute-start(f32[256,256]{1,0:T(8,128)S(1)} %broadcast_select_fusion.5), channel_id=1, source_target_pairs={{0,1},{1,0},{2,3},{3,2},{4,5},{5,4},{6,7},{7,6},{8,9},{9,8},{10,11... | collective-permute-start | bytes 786440 | tf_op jit(solution)/shard_map/ppermute | solution.py:333
  21.1 1.2 select_select_fusion
  22.3 0.3 collective-permute-start.22
  22.6 1.3 collective-permute-start.17
  23.9 1.3 collective-permute-done.12
  25.2 7.9 %collective-permute-start.13 = (f32[256,256]{1,0:T(8,128)S(1)}, f32[256,256]{1,0:T(8,128)S(1)}, u32[]{:S(2)}, u32[]{:S(2)}) collective-permute-start(f32[256,256]{1,0:T(8,128)S(1)} %broadcast_select_fusion.6), channel_id=1, source_target_pairs={{0,2},{1,3},{2,0},{3,1},{4,6},{5,7},{6,4},{7,5},{8,10},{9,11},{10,... | collective-permute-start | bytes 786440 | tf_op jit(solution)/shard_map/ppermute | solution.py:333
  33.2 0.1 collective-permute-start.21
  33.3 4.0 %collective-permute-done.13 = f32[256,256]{1,0:T(8,128)S(1)} collective-permute-done((f32[256,256]{1,0:T(8,128)S(1)}, f32[256,256]{1,0:T(8,128)S(1)}, u32[]{:S(2)}, u32[]{:S(2)}) %collective-permute-start.13) | collective-permute-done | bytes 262176 | tf_op jit(solution)/shard_map/ppermute | solution.py:333
  37.4 2.7 %collective-permute-start.14 = (f32[256,256]{1,0:T(8,128)S(1)}, f32[256,256]{1,0:T(8,128)}, u32[]{:S(2)}, u32[]{:S(2)}) collective-permute-start(f32[256,256]{1,0:T(8,128)S(1)} %broadcast_select_fusion.7), channel_id=1, source_target_pairs={{0,16},{1,17},{2,18},{3,19},{4,20},{5,21},{6,22},{7,23},{8,24},{9,... | collective-permute-start | bytes 786440 | tf_op jit(solution)/shard_map/ppermute | solution.py:333
  40.1 7.6 %collective-permute-done.17 = f32[2,256,256]{2,1,0:T(8,128)} collective-permute-done((f32[2,256,256]{2,1,0:T(8,128)S(1)}, f32[2,256,256]{2,1,0:T(8,128)}, u32[]{:S(2)}, u32[]{:S(2)}) %collective-permute-start.17) | collective-permute-done | bytes 524320 | tf_op jit(solution)/shard_map/ppermute | solution.py:333
  47.7 8.0 %collective-permute-start.23 = (f32[2,256,256]{2,1,0:T(8,128)}, f32[2,256,256]{2,1,0:T(8,128)S(1)}, u32[]{:S(2)}, u32[]{:S(2)}) collective-permute-start(f32[2,256,256]{2,1,0:T(8,128)} %collective-permute-done.22), channel_id=1, source_target_pairs={{0,2},{1,3},{2,0},{3,1},{4,6},{5,7},{6,4},{7,5},{8,10},{9,11},{10,... | collective-permute-start | bytes 1572872 | tf_op jit(solution)/shard_map/ppermute | solution.py:333
  55.6 1.1 broadcast_select_fusion.2
  56.8 0.1 collective-permute-start.18
  56.8 1.1 broadcast_select_fusion.1.a_ref
  58.0 2.8 %collective-permute-start.24 = (f32[2,256,256]{2,1,0:T(8,128)S(1)}, f32[2,256,256]{2,1,0:T(8,128)S(1)}, u32[]{:S(2)}, u32[]{:S(2)}) collective-permute-start(f32[2,256,256]{2,1,0:T(8,128)S(1)} %broadcast_select_fusion.1.a_ref), channel_id=1, source_target_pairs={{0,8},{1,9},{2,10},{3,11},{4,12},{5,13},{6,14},{7,15},{8,0},{9,1},... | collective-permute-start | bytes 1572872 | tf_op jit(solution)/shard_map/ppermute | solution.py:333
  60.8 4.8 %collective-permute-done.23 = f32[2,256,256]{2,1,0:T(8,128)S(1)} collective-permute-done((f32[2,256,256]{2,1,0:T(8,128)}, f32[2,256,256]{2,1,0:T(8,128)S(1)}, u32[]{:S(2)}, u32[]{:S(2)}) %collective-permute-start.23) | collective-permute-done | bytes 524320 | tf_op jit(solution)/shard_map/ppermute | solution.py:333
  65.6 0.1 broadcast_select_fusion.b_ref
  65.7 11.2 %collective-permute-done.18 = f32[2,256,256]{2,1,0:T(8,128)S(1)} collective-permute-done((f32[2,256,256]{2,1,0:T(8,128)S(1)}, f32[2,256,256]{2,1,0:T(8,128)S(1)}, u32[]{:S(2)}, u32[]{:S(2)}) %collective-permute-start.18) | collective-permute-done | bytes 524320 | tf_op jit(solution)/shard_map/ppermute | solution.py:333
  77.0 3.0 %collective-permute-start.25 = (f32[2,256,256]{2,1,0:T(8,128)S(1)}, f32[2,256,256]{2,1,0:T(8,128)S(1)}, u32[]{:S(2)}, u32[]{:S(2)}) collective-permute-start(f32[2,256,256]{2,1,0:T(8,128)S(1)} %broadcast_select_fusion.b_ref), channel_id=1, source_target_pairs={{0,8},{1,9},{2,10},{3,11},{4,12},{5,13},{6,14},{7,15},{8,0},{9,1},... | collective-permute-start | bytes 1572872 | tf_op jit(solution)/shard_map/ppermute | solution.py:333
  80.0 0.1 broadcast_select_fusion.3.a_ref
  80.1 0.1 collective-permute-start.19
  80.2 0.5 collective-permute-start.15
  80.8 1.8 %collective-permute-done.15.b_ref = f32[256,256]{1,0:T(8,128)S(1)} collective-permute-done((f32[256,256]{1,0:T(8,128)S(1)}, f32[256,256]{1,0:T(8,128)S(1)}, u32[]{:S(2)}, u32[]{:S(2)}) %collective-permute-start.15) | collective-permute-done | bytes 262176 | tf_op jit(solution)/shard_map/ppermute | solution.py:333
  82.6 1.7 %collective-permute-start.2 = (f32[2,256,256]{2,1,0:T(8,128)}, f32[2,256,256]{2,1,0:T(8,128)S(1)}, u32[]{:S(2)}, u32[]{:S(2)}) collective-permute-start(f32[2,256,256]{2,1,0:T(8,128)} %copy-done.9), channel_id=1, source_target_pairs={{0,0},{1,1},{2,2},{3,3},{4,5},{5,4},{6,7},{7,6},{8,8},{9,9},{10,10... | collective-permute-start | bytes 1572872 | tf_op jit(solution)/shard_map/ppermute | solution.py:333
  84.3 0.4 collective-permute-start.7
  84.8 0.1 collective-permute-start.9
  84.9 0.4 collective-permute-start.8
  85.3 0.1 collective-permute-start.10
  85.4 0.7 pad_add_fusion.pos_ref.refs_0_
  86.1 7.7 %chain0.1 = (f32[256,256]{1,0:T(8,128)}, bf16[256,768]{1,0:T(8,128)(2,1)}, bf16[256,768]{1,0:T(8,128)(2,1)}) custom-call(s32[2]{0:T(128)} %pad_add_fusion.pos_ref.refs_0_, f32[256,256]{1,0:T(8,128)} %copy-done.8, f32[256,256]{1,0:T(8,128)} %copy-done.15), custom_call_target="tpu_custom_call" | custom-call | tf_op jit(solution)/shard_map/chain0/pallas_call | solution.py:150
  93.8 8.8 %chain1.1 = (f32[256,512]{1,0:T(8,128)}, bf16[256,768]{1,0:T(8,128)(2,1)}, bf16[256,768]{1,0:T(8,128)(2,1)}) custom-call(s32[2]{0:T(128)} %pad_add_fusion.pos_ref.refs_0_, f32[2,256,256]{2,1,0:T(8,128)} %copy-done.7, f32[2,256,256]{2,1,0:T(8,128)} %collective-permute-done.19.b_ref, bf16[256,768]{1,0:T(8,128)(2,1)} %get-tuple-element.17.refs_0_.refs_14_, ...), custom_call_target="tpu_custom_call" | custom-call | tf_op jit(solution)/shard_map/chain1/pallas_call | solution.py:150
  102.5 10.3 %chain2.1 = (f32[256,768]{1,0:T(8,128)}, bf16[256,768]{1,0:T(8,128)(2,1)}, bf16[256,1536]{1,0:T(8,128)(2,1)}) custom-call(s32[2]{0:T(128)} %pad_add_fusion.pos_ref.refs_0_, f32[2,256,256]{2,1,0:T(8,128)} %copy-done.2, f32[2,256,256]{2,1,0:T(8,128)} %copy-done.3, f32[2,256,256]{2,1,0:T(8,128)} %copy-done.5, f32[2,256,256]{2,1,0:T(8,128)} %copy-done.6, ...), custom_call_target="tpu_custom_call" | custom-call | tf_op jit(solution)/shard_map/chain2/pallas_call | solution.py:150
  112.8 11.8 %chain3.1 = (f32[256,1024]{1,0:T(8,128)}, bf16[256,768]{1,0:T(8,128)(2,1)}, bf16[256,2304]{1,0:T(8,128)(2,1)}) custom-call(s32[2]{0:T(128)} %pad_add_fusion.pos_ref.refs_0_, f32[2,256,256]{2,1,0:T(8,128)} %copy-done.2, f32[2,256,256]{2,1,0:T(8,128)} %copy-done.3, f32[2,256,256]{2,1,0:T(8,128)} %copy-done.5, f32[2,256,256]{2,1,0:T(8,128)} %copy-done.6, ...), custom_call_target="tpu_custom_call" | custom-call | tf_op jit(solution)/shard_map/chain3/pallas_call | solution.py:150
  124.7 0.8 copy-done.10
  125.4 0.2 copy-done.11
  125.6 0.2 copy-done.12
  125.8 0.2 copy-done.13
  126.0 0.2 copy-done.14
  126.2 13.8 %tile.1 = f32[512,256]{1,0:T(8,128)} custom-call(s32[2]{0:T(128)} %pad_add_fusion.pos_ref.refs_0_, f32[512,256]{1,0:T(8,128)} %refs_1_.1, f32[2,256,256]{2,1,0:T(8,128)} %copy-done.1, f32[2,256,256]{2,1,0:T(8,128)} %collective-permute-done.refs_3_, f32[2,256,256]{2,1,0:T(8,128)} %copy-done.9, f32[2,256,256]{2,1,0:T(8,128)} %copy-done.10, ...), custom_call_target="tpu_custom_call" | custom-call | tf_op jit(solution)/shard_map/tile/pallas_call | solution.py:423
  (54 shorter events, 0.3 us)
Async XLA Ops:
  0.0 1.3 copy-start
  1.4 20.9 %copy-start.1 = (f32[2,256,256]{2,1,0:T(8,128)}, f32[2,256,256]{2,1,0:T(8,128)S(1)}, u32[]{:S(2)}) copy-start(f32[2,256,256]{2,1,0:T(8,128)S(1)} %broadcast_select_fusion.4.refs_2_) | copy-start | bytes 1572868
  1.4 15.7 %collective-permute-start.3 = (f32[2,256,256]{2,1,0:T(8,128)S(1)}, f32[2,256,256]{2,1,0:T(8,128)S(1)}, u32[]{:S(2)}, u32[]{:S(2)}) collective-permute-start(f32[2,256,256]{2,1,0:T(8,128)S(1)} %broadcast_select_fusion.4.refs_2_), channel_id=1, source_target_pairs={{0,16},{1,17},{2,18},{3,19},{4,20},{5,21},{6,22},{7,23},{8,24},{9,... | collective-permute-start | bytes 1572872 | tf_op jit(solution)/shard_map/ppermute | solution.py:333
  1.7 19.4 %collective-permute-start.16 = (f32[2,256,256]{2,1,0:T(8,128)S(1)}, f32[2,256,256]{2,1,0:T(8,128)S(1)}, u32[]{:S(2)}, u32[]{:S(2)}) collective-permute-start(f32[2,256,256]{2,1,0:T(8,128)S(1)} %broadcast_select_fusion.4.refs_2_), channel_id=1, source_target_pairs={{0,0},{1,21},{2,2},{3,3},{4,4},{5,5},{6,6},{7,7},{8,8},{9,9},{10,1... | collective-permute-start | bytes 1572872 | tf_op jit(solution)/shard_map/ppermute | solution.py:333
  2.4 18.7 %collective-permute-start.20 = (f32[2,256,256]{2,1,0:T(8,128)S(1)}, f32[2,256,256]{2,1,0:T(8,128)}, u32[]{:S(2)}, u32[]{:S(2)}) collective-permute-start(f32[2,256,256]{2,1,0:T(8,128)S(1)} %broadcast_select_fusion.4.refs_2_), channel_id=1, source_target_pairs={{0,0},{1,1},{2,22},{3,23},{4,4},{5,5},{6,6},{7,7},{8,8},{9,9},{10,... | collective-permute-start | bytes 1572872 | tf_op jit(solution)/shard_map/ppermute | solution.py:333
  3.9 1.4 %collective-permute-start.11 = (f32[256,256]{1,0:T(8,128)S(1)}, f32[256,256]{1,0:T(8,128)S(1)}, u32[]{:S(2)}, u32[]{:S(2)}) collective-permute-start(f32[256,256]{1,0:T(8,128)S(1)} %slice.4), channel_id=1, source_target_pairs={{0,20},{1,1},{2,2},{3,3},{4,4},{5,5},{6,6},{7,7},{8,8},{9,9},{10,1... | collective-permute-start | bytes 786440 | tf_op jit(solution)/shard_map/ppermute | solution.py:333
  4.6 28.6 %collective-permute-start.1 = (f32[2,256,256]{2,1,0:T(8,128)S(1)}, f32[2,256,256]{2,1,0:T(8,128)S(1)}, u32[]{:S(2)}, u32[]{:S(2)}) collective-permute-start(f32[2,256,256]{2,1,0:T(8,128)S(1)} %broadcast_select_fusion.4.refs_2_), channel_id=1, source_target_pairs={{0,0},{1,1},{2,2},{3,3},{4,6},{5,7},{6,4},{7,5},{8,8},{9,9},{10,10... | collective-permute-start | bytes 1572872 | tf_op jit(solution)/shard_map/ppermute | solution.py:333
  5.3 27.9 %collective-permute-start = (f32[2,256,256]{2,1,0:T(8,128)S(1)}, f32[2,256,256]{2,1,0:T(8,128)}, u32[]{:S(2)}, u32[]{:S(2)}) collective-permute-start(f32[2,256,256]{2,1,0:T(8,128)S(1)} %broadcast_select_fusion.4.refs_2_), channel_id=1, source_target_pairs={{0,0},{1,1},{2,2},{3,3},{4,5},{5,4},{6,7},{7,6},{8,8},{9,9},{10,10... | collective-permute-start | bytes 1572872 | tf_op jit(solution)/shard_map/ppermute | solution.py:333
  17.1 67.2 %copy-start.4 = (f32[2,256,256]{2,1,0:T(8,128)}, f32[2,256,256]{2,1,0:T(8,128)S(1)}, u32[]{:S(2)}) copy-start(f32[2,256,256]{2,1,0:T(8,128)S(1)} %collective-permute-done.3.refs_6_) | copy-start | bytes 1572868
  17.1 8.1 %collective-permute-start.12 = (f32[256,256]{1,0:T(8,128)S(1)}, f32[256,256]{1,0:T(8,128)S(1)}, u32[]{:S(2)}, u32[]{:S(2)}) collective-permute-start(f32[256,256]{1,0:T(8,128)S(1)} %broadcast_select_fusion.5), channel_id=1, source_target_pairs={{0,1},{1,0},{2,3},{3,2},{4,5},{5,4},{6,7},{7,6},{8,9},{9,8},{10,11... | collective-permute-start | bytes 786440 | tf_op jit(solution)/shard_map/ppermute | solution.py:333
  22.3 15.0 %collective-permute-start.22 = (f32[2,256,256]{2,1,0:T(8,128)S(1)}, f32[2,256,256]{2,1,0:T(8,128)}, u32[]{:S(2)}, u32[]{:S(2)}) collective-permute-start(f32[2,256,256]{2,1,0:T(8,128)S(1)} %get-tuple-element.29), channel_id=1, source_target_pairs={{0,1},{1,0},{2,3},{3,2},{4,5},{5,4},{6,7},{7,6},{8,9},{9,8},{10,11... | collective-permute-start | bytes 1572872 | tf_op jit(solution)/shard_map/ppermute | solution.py:333
  22.6 25.0 %collective-permute-start.17 = (f32[2,256,256]{2,1,0:T(8,128)S(1)}, f32[2,256,256]{2,1,0:T(8,128)}, u32[]{:S(2)}, u32[]{:S(2)}) collective-permute-start(f32[2,256,256]{2,1,0:T(8,128)S(1)} %get-tuple-element.30), channel_id=1, source_target_pairs={{0,1},{1,0},{2,3},{3,2},{4,5},{5,4},{6,7},{7,6},{8,9},{9,8},{10,11... | collective-permute-start | bytes 1572872 | tf_op jit(solution)/shard_map/ppermute | solution.py:333
  25.2 12.1 %collective-permute-start.13 = (f32[256,256]{1,0:T(8,128)S(1)}, f32[256,256]{1,0:T(8,128)S(1)}, u32[]{:S(2)}, u32[]{:S(2)}) collective-permute-start(f32[256,256]{1,0:T(8,128)S(1)} %broadcast_select_fusion.6), channel_id=1, source_target_pairs={{0,2},{1,3},{2,0},{3,1},{4,6},{5,7},{6,4},{7,5},{8,10},{9,11},{10,... | collective-permute-start | bytes 786440 | tf_op jit(solution)/shard_map/ppermute | solution.py:333
  33.2 32.5 %copy-start.9 = (f32[2,256,256]{2,1,0:T(8,128)}, f32[2,256,256]{2,1,0:T(8,128)S(1)}, u32[]{:S(2)}) copy-start(f32[2,256,256]{2,1,0:T(8,128)S(1)} %collective-permute-done.1.refs_4_) | copy-start | bytes 1572868
  33.2 23.6 %collective-permute-start.21 = (f32[2,256,256]{2,1,0:T(8,128)S(1)}, f32[2,256,256]{2,1,0:T(8,128)}, u32[]{:S(2)}, u32[]{:S(2)}) collective-permute-start(f32[2,256,256]{2,1,0:T(8,128)S(1)} %get-tuple-element.29), channel_id=1, source_target_pairs={{0,2},{1,3},{2,0},{3,1},{4,6},{5,7},{6,4},{7,5},{8,10},{9,11},{10,... | collective-permute-start | bytes 1572872 | tf_op jit(solution)/shard_map/ppermute | solution.py:333
  33.3 24.7 %collective-permute-start.5 = (f32[2,256,256]{2,1,0:T(8,128)S(1)}, f32[2,256,256]{2,1,0:T(8,128)}, u32[]{:S(2)}, u32[]{:S(2)}) collective-permute-start(f32[2,256,256]{2,1,0:T(8,128)S(1)} %collective-permute-done.1.refs_4_), channel_id=1, source_target_pairs={{0,16},{1,17},{2,18},{3,19},{4,20},{5,21},{6,22},{7,23},{8,24},{9,... | collective-permute-start | bytes 1572872 | tf_op jit(solution)/shard_map/ppermute | solution.py:333
  37.3 42.9 %collective-permute-start.4 = (f32[2,256,256]{2,1,0:T(8,128)}, f32[2,256,256]{2,1,0:T(8,128)}, u32[]{:S(2)}, u32[]{:S(2)}) collective-permute-start(f32[2,256,256]{2,1,0:T(8,128)} %collective-permute-done.refs_3_), channel_id=1, source_target_pairs={{0,16},{1,17},{2,18},{3,19},{4,20},{5,21},{6,22},{7,23},{8,24},{9,... | collective-permute-start | bytes 1572872 | tf_op jit(solution)/shard_map/ppermute | solution.py:333
  37.4 42.7 %collective-permute-start.14 = (f32[256,256]{1,0:T(8,128)S(1)}, f32[256,256]{1,0:T(8,128)}, u32[]{:S(2)}, u32[]{:S(2)}) collective-permute-start(f32[256,256]{1,0:T(8,128)S(1)} %broadcast_select_fusion.7), channel_id=1, source_target_pairs={{0,16},{1,17},{2,18},{3,19},{4,20},{5,21},{6,22},{7,23},{8,24},{9,... | collective-permute-start | bytes 786440 | tf_op jit(solution)/shard_map/ppermute | solution.py:333
  47.7 18.0 %collective-permute-start.23 = (f32[2,256,256]{2,1,0:T(8,128)}, f32[2,256,256]{2,1,0:T(8,128)S(1)}, u32[]{:S(2)}, u32[]{:S(2)}) collective-permute-start(f32[2,256,256]{2,1,0:T(8,128)} %collective-permute-done.22), channel_id=1, source_target_pairs={{0,2},{1,3},{2,0},{3,1},{4,6},{5,7},{6,4},{7,5},{8,10},{9,11},{10,... | collective-permute-start | bytes 1572872 | tf_op jit(solution)/shard_map/ppermute | solution.py:333
  56.8 20.2 %collective-permute-start.18 = (f32[2,256,256]{2,1,0:T(8,128)S(1)}, f32[2,256,256]{2,1,0:T(8,128)S(1)}, u32[]{:S(2)}, u32[]{:S(2)}) collective-permute-start(f32[2,256,256]{2,1,0:T(8,128)S(1)} %broadcast_select_fusion.2), channel_id=1, source_target_pairs={{0,2},{1,3},{2,0},{3,1},{4,6},{5,7},{6,4},{7,5},{8,10},{9,11},{10,... | collective-permute-start | bytes 1572872 | tf_op jit(solution)/shard_map/ppermute | solution.py:333
  58.0 22.1 %copy-start.2 = (f32[2,256,256]{2,1,0:T(8,128)}, f32[2,256,256]{2,1,0:T(8,128)S(1)}, u32[]{:S(2)}) copy-start(f32[2,256,256]{2,1,0:T(8,128)S(1)} %broadcast_select_fusion.1.a_ref) | copy-start | bytes 1572868
  58.0 26.3 %collective-permute-start.24 = (f32[2,256,256]{2,1,0:T(8,128)S(1)}, f32[2,256,256]{2,1,0:T(8,128)S(1)}, u32[]{:S(2)}, u32[]{:S(2)}) collective-permute-start(f32[2,256,256]{2,1,0:T(8,128)S(1)} %broadcast_select_fusion.1.a_ref), channel_id=1, source_target_pairs={{0,8},{1,9},{2,10},{3,11},{4,12},{5,13},{6,14},{7,15},{8,0},{9,1},... | collective-permute-start | bytes 1572872 | tf_op jit(solution)/shard_map/ppermute | solution.py:333
  65.6 19.2 %collective-permute-start.6 = (f32[2,256,256]{2,1,0:T(8,128)}, f32[2,256,256]{2,1,0:T(8,128)}, u32[]{:S(2)}, u32[]{:S(2)}) collective-permute-start(f32[2,256,256]{2,1,0:T(8,128)} %collective-permute-done.5.refs_8_), channel_id=1, source_target_pairs={{0,1},{1,0},{2,3},{3,2},{4,5},{5,4},{6,7},{7,6},{8,9},{9,8},{10,11... | collective-permute-start | bytes 1572872 | tf_op jit(solution)/shard_map/ppermute | solution.py:333
  65.7 14.5 %copy-start.3 = (f32[2,256,256]{2,1,0:T(8,128)}, f32[2,256,256]{2,1,0:T(8,128)S(1)}, u32[]{:S(2)}) copy-start(f32[2,256,256]{2,1,0:T(8,128)S(1)} %broadcast_select_fusion.b_ref) | copy-start | bytes 1572868
  77.0 8.0 %collective-permute-start.25 = (f32[2,256,256]{2,1,0:T(8,128)S(1)}, f32[2,256,256]{2,1,0:T(8,128)S(1)}, u32[]{:S(2)}, u32[]{:S(2)}) collective-permute-start(f32[2,256,256]{2,1,0:T(8,128)S(1)} %broadcast_select_fusion.b_ref), channel_id=1, source_target_pairs={{0,8},{1,9},{2,10},{3,11},{4,12},{5,13},{6,14},{7,15},{8,0},{9,1},... | collective-permute-start | bytes 1572872 | tf_op jit(solution)/shard_map/ppermute | solution.py:333
  80.0 13.7 %copy-start.7 = (f32[2,256,256]{2,1,0:T(8,128)}, f32[2,256,256]{2,1,0:T(8,128)S(1)}, u32[]{:S(2)}) copy-start(f32[2,256,256]{2,1,0:T(8,128)S(1)} %broadcast_select_fusion.3.a_ref) | copy-start | bytes 1572868
  80.1 5.2 %collective-permute-start.19 = (f32[2,256,256]{2,1,0:T(8,128)S(1)}, f32[2,256,256]{2,1,0:T(8,128)}, u32[]{:S(2)}, u32[]{:S(2)}) collective-permute-start(f32[2,256,256]{2,1,0:T(8,128)S(1)} %broadcast_select_fusion.3.a_ref), channel_id=1, source_target_pairs={{0,8},{1,9},{2,10},{3,11},{4,12},{5,13},{6,14},{7,15},{8,0},{9,1},... | collective-permute-start | bytes 1572872 | tf_op jit(solution)/shard_map/ppermute | solution.py:333
  80.2 5.9 %copy-start.8 = (f32[256,256]{1,0:T(8,128)}, f32[256,256]{1,0:T(8,128)S(1)}, u32[]{:S(2)}) copy-start(f32[256,256]{1,0:T(8,128)S(1)} %broadcast_select_fusion.8.a_ref) | copy-start | bytes 786436
  80.2 2.4 %collective-permute-start.15 = (f32[256,256]{1,0:T(8,128)S(1)}, f32[256,256]{1,0:T(8,128)S(1)}, u32[]{:S(2)}, u32[]{:S(2)}) collective-permute-start(f32[256,256]{1,0:T(8,128)S(1)} %broadcast_select_fusion.8.a_ref), channel_id=1, source_target_pairs={{0,8},{1,9},{2,10},{3,11},{4,12},{5,13},{6,14},{7,15},{8,0},{9,1},... | collective-permute-start | bytes 786440 | tf_op jit(solution)/shard_map/ppermute | solution.py:333
  82.6 3.5 %copy-start.15 = (f32[256,256]{1,0:T(8,128)}, f32[256,256]{1,0:T(8,128)S(1)}, u32[]{:S(2)}) copy-start(f32[256,256]{1,0:T(8,128)S(1)} %collective-permute-done.15.b_ref) | copy-start | bytes 786436
  82.6 42.0 %collective-permute-start.2 = (f32[2,256,256]{2,1,0:T(8,128)}, f32[2,256,256]{2,1,0:T(8,128)S(1)}, u32[]{:S(2)}, u32[]{:S(2)}) collective-permute-start(f32[2,256,256]{2,1,0:T(8,128)} %copy-done.9), channel_id=1, source_target_pairs={{0,0},{1,1},{2,2},{3,3},{4,5},{5,4},{6,7},{7,6},{8,8},{9,9},{10,10... | collective-permute-start | bytes 1572872 | tf_op jit(solution)/shard_map/ppermute | solution.py:333
  84.3 18.2 %copy-start.5 = (f32[2,256,256]{2,1,0:T(8,128)}, f32[2,256,256]{2,1,0:T(8,128)S(1)}, u32[]{:S(2)}) copy-start(f32[2,256,256]{2,1,0:T(8,128)S(1)} %collective-permute-done.24.a_other) | copy-start | bytes 1572868
  84.3 40.3 %collective-permute-start.7 = (f32[2,256,256]{2,1,0:T(8,128)S(1)}, f32[2,256,256]{2,1,0:T(8,128)S(1)}, u32[]{:S(2)}, u32[]{:S(2)}) collective-permute-start(f32[2,256,256]{2,1,0:T(8,128)S(1)} %collective-permute-done.3.refs_6_), channel_id=1, source_target_pairs={{0,8},{1,9},{2,10},{3,11},{4,12},{5,13},{6,14},{7,15},{8,0},{9,1},... | collective-permute-start | bytes 1572872 | tf_op jit(solution)/shard_map/ppermute | solution.py:333
  84.8 39.8 %collective-permute-start.9 = (f32[2,256,256]{2,1,0:T(8,128)}, f32[2,256,256]{2,1,0:T(8,128)S(1)}, u32[]{:S(2)}, u32[]{:S(2)}) collective-permute-start(f32[2,256,256]{2,1,0:T(8,128)} %collective-permute-done.5.refs_8_), channel_id=1, source_target_pairs={{0,8},{1,9},{2,10},{3,11},{4,12},{5,13},{6,14},{7,15},{8,0},{9,1},... | collective-permute-start | bytes 1572872 | tf_op jit(solution)/shard_map/ppermute | solution.py:333
  84.9 17.6 %copy-start.6 = (f32[2,256,256]{2,1,0:T(8,128)}, f32[2,256,256]{2,1,0:T(8,128)S(1)}, u32[]{:S(2)}) copy-start(f32[2,256,256]{2,1,0:T(8,128)S(1)} %collective-permute-done.25.b_other) | copy-start | bytes 1572868
  84.9 39.7 %collective-permute-start.8 = (f32[2,256,256]{2,1,0:T(8,128)}, f32[2,256,256]{2,1,0:T(8,128)S(1)}, u32[]{:S(2)}, u32[]{:S(2)}) collective-permute-start(f32[2,256,256]{2,1,0:T(8,128)} %collective-permute-done.4.refs_7_), channel_id=1, source_target_pairs={{0,8},{1,9},{2,10},{3,11},{4,12},{5,13},{6,14},{7,15},{8,0},{9,1},... | collective-permute-start | bytes 1572872 | tf_op jit(solution)/shard_map/ppermute | solution.py:333
  85.3 39.4 %collective-permute-start.10 = (f32[2,256,256]{2,1,0:T(8,128)}, f32[2,256,256]{2,1,0:T(8,128)S(1)}, u32[]{:S(2)}, u32[]{:S(2)}) collective-permute-start(f32[2,256,256]{2,1,0:T(8,128)} %collective-permute-done.6.refs_9_), channel_id=1, source_target_pairs={{0,8},{1,9},{2,10},{3,11},{4,12},{5,13},{6,14},{7,15},{8,0},{9,1},... | collective-permute-start | bytes 1572872 | tf_op jit(solution)/shard_map/ppermute | solution.py:333
  124.6 0.9 copy-start.10
  124.6 1.0 copy-start.11
  124.6 1.2 copy-start.12
  124.6 1.3 copy-start.13
  124.7 1.5 %copy-start.14 = (f32[2,256,256]{2,1,0:T(8,128)}, f32[2,256,256]{2,1,0:T(8,128)S(1)}, u32[]{:S(2)}) copy-start(f32[2,256,256]{2,1,0:T(8,128)S(1)} %collective-permute-done.10.refs_13_) | copy-start | bytes 1572868

commit v2 on v1

--- a/solution.py
+++ b/solution.py
@@ -14,7 +14,9 @@
 bf16 = jnp.bfloat16
 VMEM = pl.BlockSpec(memory_space=pltpu.VMEM)
 SMEM = pl.BlockSpec(memory_space=pltpu.SMEM)
-PARAMS = pltpu.CompilerParams(vmem_limit_bytes=56 * 2**20)
+PARAMS = pltpu.CompilerParams(vmem_limit_bytes=16 * 2**20)
+TILE_PARAMS = pltpu.CompilerParams(vmem_limit_bytes=36 * 2**20)
+COST = pl.CostEstimate(flops=1000, bytes_accessed=1024, transcendentals=0)
 
 
 def lane_copy(tile, lane):
@@ -107,7 +109,7 @@
     return jnp.where(row >= col, x, 0.0)
 
 
-def factor_block(block, factor_ref, inv_ref, col):
+def factor_block(block, factor_ref, col):
     h = LANES
     up_a, inv_a = factor_half(block[:h, :h])
     inv_a = lower(inv_a)
@@ -120,8 +122,7 @@
     factor_ref[:h, col + h : col + 2 * h] = zero
     factor_ref[h:, col : col + h] = low
     factor_ref[h:, col + h : col + 2 * h] = lower(up_b.T)
-    inv = jnp.concatenate([jnp.concatenate([inv_a, zero], 1), jnp.concatenate([inv_low, inv_b], 1)], 0)
-    inv_ref[...] = as_right(inv)
+    return jnp.concatenate([jnp.concatenate([inv_a, zero], 1), jnp.concatenate([inv_low, inv_b], 1)], 0)
 
 
 def chain_body(take, k, width, refs):
@@ -141,7 +142,7 @@
         block = block - dot_t(left[:, : 3 * w * k], right_ref[:, : 3 * w * k])
     else:
         right_ref[...] = jnp.zeros_like(right_ref)
-    factor_block(block, factor_ref, inv_ref, w * k)
+    inv_ref[...] = as_right(factor_block(block, factor_ref, w * k))
 
 
 def chain_call(kernel, k, width, inputs, specs, state):
@@ -158,6 +159,7 @@
         out_specs=[VMEM] * 3,
         scratch_shapes=[pltpu.VMEM((width, wide), bf16)],
         compiler_params=PARAMS,
+        cost_estimate=COST,
         name=f"chain{k}",
     )(*inputs, *invs, *rights)
     return factor, (invs + [inv], rights + [right])
@@ -233,7 +235,8 @@
         in_specs=[SMEM] + [VMEM] * (len(inputs) - 1 + 3 * SNODES),
         out_specs=VMEM,
         scratch_shapes=[pltpu.VMEM((rows + width, wide), bf16), pltpu.VMEM((width, wide), bf16)],
-        compiler_params=PARAMS,
+        compiler_params=TILE_PARAMS,
+        cost_estimate=COST,
         name="tile",
     )(*inputs, *invs, *rights, *factors)
 
@@ -262,33 +265,20 @@
     )
 
 
-def chain_first(width, pos_ref, a_ref, b_ref, *refs):
+def chain_early(k, width, pos_ref, a_ref, b_ref, *refs):
     even = (pos_ref[0] % 2) == 0
-    chain_body(lambda j: jnp.where(even, a_ref[...], b_ref[...]), 0, width, refs)
-
-
-def chain_second(width, pos_ref, a_ref, b_ref, *refs):
-    even = (pos_ref[0] % 2) == 0
-    chain_body(lambda j: jnp.where(even, a_ref[j], b_ref[j]), 1, width, refs)
-
-
-def chain_later(k, width, pos_ref, a_ref, b_ref, a_other, b_other, *refs):
+    chain_body(lambda j: jnp.where(even, a_ref[k + j], b_ref[k + j]), k, width, refs)
+
+
+def chain_later(k, width, pos_ref, a_ref, b_ref, *refs):
     core = pos_ref[0] % 2
-    first = (pos_ref[1] % 2) == k % 2
-
-    def take(j):
-        own = core == j // 2
-        mine = jnp.where(own, a_ref[j % 2], a_other[j % 2])
-        other = jnp.where(own, b_ref[j % 2], b_other[j % 2])
-        return jnp.where(first, mine, other)
-
-    chain_body(take, k, width, refs)
+    chain_body(lambda j: jnp.where(core == j // 2, a_ref[j % 2], b_ref[j % 2]), k, width, refs)
 
 
 def box_tile(width, *refs):
     pos_ref, tile_ref = refs[:2]
-    below, crossed, other = refs[2:6], refs[6:10], refs[10:14]
-    rest = refs[14:]
+    below, crossed, other = refs[2:6], refs[6], refs[7]
+    rest = refs[8:]
     n = SNODES
     inv_refs, right_refs, factor_refs = rest[:n], rest[n : 2 * n], rest[2 * n : 3 * n]
     out_ref, left, right, work = rest[3 * n :]
@@ -299,25 +289,23 @@
     @pl.when((row_index >= 2) & (col_index < n))
     def _():
         for m in range(4):
-            for k in range(n):
-
-                @pl.when((col_index ^ m) == k)
-                def _():
-                    work[k, :w, :] = below[m][0]
-                    work[k, w : 2 * w, :] = below[m][1]
+            k = col_index ^ m
+            work[k, :w, :] = below[m][0]
+            work[k, w : 2 * w, :] = below[m][1]
 
     @pl.when((row_index >= 2) & (col_index >= n))
     def _():
-        for k in range(n):
-            for place in range(3):
-                want = col_index if place == 2 else n + 2 * core + place
-                for m in range(4):
-
-                    @pl.when((col_index ^ m) == want)
-                    def _():
-                        work[k, place * w : (place + 1) * w, :] = jnp.where(
-                            core == k // 2, crossed[m][k % 2], other[m][k % 2]
-                        )
+        for m in range(4):
+            column = (col_index ^ m) - n
+
+            def place(at):
+                for k in range(n):
+                    work[k, at * w : (at + 1) * w, :] = jnp.where(core == k // 2, crossed[m, k % 2], other[m, k % 2])
+
+            if m == 0:
+                place(2)
+            for at in range(2):
+                pl.when(column == 2 * core + at)(functools.partial(place, at))
 
     write_tile(
         pos_ref, lambda k: work[k], tile_ref, inv_refs, right_refs, factor_refs, out_ref, left, right, width
@@ -329,19 +317,9 @@
     for r in range(4):
         for c in range(8):
             pr, pc = pair(r, c)
-            perm.append((r * 8 + c, pr * 8 + pc))
+            if (pr, pc) != (r, c):
+                perm.append((r * 8 + c, pr * 8 + pc))
     return lax.ppermute(x, ("row", "col"), perm)
-
-
-def across(members):
-    def pair(r, c):
-        if r < 2 and c < 4 and members(r, c):
-            return r + 2, c + 4
-        if r >= 2 and c >= 4 and members(r - 2, c - 4):
-            return r - 2, c - 4
-        return r, c
-
-    return pair
 
 
 def core_pair(r, c):
@@ -360,12 +338,17 @@
     return r, c ^ 2
 
 
-def mixed(r, c):
-    return (r >= 2) != (c >= 4)
+def after(x, *others):
+    return lax.optimization_barrier((x, *others))[0]
 
 
 def some(pair, members):
     return lambda r, c: pair(r, c) if members(r, c) else (r, c)
+
+
+def chosen(pairs):
+    table = {a: b for p, q in pairs for a, b in ((p, q), (q, p))}
+    return lambda r, c: table.get((r, c), (r, c))
 
 
 def box_mesh(stiffness):
@@ -373,53 +356,74 @@
     r, c = lax.axis_index("row"), lax.axis_index("col")
     pos = jnp.stack([r, c]).astype(jnp.int32)
     blocks = stiffness.reshape(2, width, width)
-    first = (r == 0) & (c == 0)
-
-    d = blocks[0]
-    d = jnp.where((r == 2) & (c == 4), swap(d, across(lambda r, c: (r, c) == (0, 0))), d)
+    even, near = c % 2 == 0, (c // 2) % 2 == 0
+    schur, corner = (r >= 2) & (c >= 4), (r < 2) & (c >= 4)
     q = jnp.where(r < 2, blocks.transpose(0, 2, 1), blocks)
-    d = jnp.where(c % 2 == 0, d, swap(d, y_pair))
-    d = jnp.where((c // 2) % 2 == 0, d, swap(d, z_pair))
-    d = jnp.where((r >= 2) & (c < 4), swap(d, x_pair), d)
-    d_other = swap(d, core_pair)
-
+
+    beside = [((r, c), (r, c + 1)) for r in (0, 1) for c in (4, 6)]
+    below = [((r, c), (r, c + 1)) for r in (2, 3) for c in (0, 2)]
+    hop = swap(q, chosen([((0, 0), (2, 4)), ((0, 1), (2, 5))] + beside))
+    hop_far = swap(q, chosen([((0, 0), (2, 6)), ((0, 1), (2, 7))] + below))
+    zq = swap(q, lambda r, c: z_pair(r, c) if (r < 2 or c < 4) and not (r == 1 and c < 2) else (r, c))
     xq = swap(q, x_pair)
-    e = swap(q, across(lambda r, c: (r, c) == (0, 1)))
-    e = jnp.where(r < 2, q, jnp.where(c < 4, xq, e))
-    e = jnp.where(c % 2 == 1, e, swap(e, y_pair))
-    e = jnp.where((c // 2) % 2 == 0, e, swap(e, z_pair))
-    e_other = swap(e, core_pair)
-
-    g = swap(q, across(lambda r, c: c >= 2))
-    g = jnp.where(r < 2, q, jnp.where(c < 4, xq, g))
-    gy = swap(g, y_pair)
-    odd = (c // 2) % 2 == 1
-    g = jnp.where(odd, g, swap(g, z_pair))
-    gy = jnp.where(odd, gy, swap(gy, z_pair))
-    g_other, gy_other = swap(g, core_pair), swap(gy, core_pair)
-
-    yq, zq = swap(q, some(y_pair, mixed)), swap(q, some(z_pair, mixed))
-    yzq = swap(zq, some(y_pair, mixed))
-    xzq, xyq = swap(zq, x_pair), swap(yq, x_pair)
-    xyzq = swap(xzq, y_pair)
-    crossed = [xq, xyq, xzq, xyzq]
-    other = [swap(v, core_pair) for v in crossed]
+    hop_late = swap(xq, chosen([((r, c), (r, c + 4)) for r in (2, 3) for c in (2, 3)]))
+    hop_later = swap(xq, chosen([((r, c), (r, c + 2)) for r in (2, 3) for c in (2, 3)]))
+    xz = swap(zq, x_pair)
+    to_schur = some(x_pair, lambda r, c: c >= 4)
+    xy = swap(hop, to_schur)
+
+    def held(on_near, on_far):
+        return jnp.where(near, on_near, on_far)
+
+    m = held(
+        jnp.where(schur, hop, jnp.where(r < 2, q, xq)),
+        jnp.where(schur, hop_far, zq),
+    )
+    m = after(jnp.where(corner, zq, m), hop_late)
+    ym = swap(m, some(y_pair, lambda r, c: (r < 2 and c >= 4) or r == 0 or (r == 2 and c not in (2, 3))))
+    n = jnp.concatenate([jnp.where(even, m[:1], ym[:1]), jnp.where(even, ym, m)], 0)
+    late = chosen([((0, c), (2, c)) for c in (2, 3)])
+    n = jnp.where((r == 2) & (c < 4) & jnp.logical_not(near), swap(n, late), n)
+    n = after(n, hop_later, xz)
+    n_other = swap(n, core_pair)
 
     state, factors = ([], []), []
-    for k in range(SNODES):
-        if k == 0:
-            kernel, inputs = chain_first, [pos, d, d_other]
-        elif k == 1:
-            kernel, inputs = chain_second, [pos, e, e_other]
-        else:
-            kernel, inputs = functools.partial(chain_later, k), [pos, g, gy, g_other, gy_other]
-        factor, state = chain_call(
-            functools.partial(kernel, width), k, width, inputs, [SMEM] + [VMEM] * (len(inputs) - 1), state
-        )
-        factors.append(factor)
+    factor, state = chain_call(
+        functools.partial(chain_early, 0, width), 0, width, [pos, n, n_other], [SMEM, VMEM, VMEM], state
+    )
+    factors.append(factor)
+
+    cross = swap(
+        jnp.where(corner, ym, zq),
+        lambda r, c: x_pair(r, c) if c >= 4 else y_pair(r, c) if r >= 2 else (r, c),
+    )
+    g_near = after(hop_later, factor)
+    g = held(
+        jnp.where(schur, g_near, jnp.where(r < 2, zq, xz)),
+        jnp.where(schur, hop_late, jnp.where(r < 2, q, xq)),
+    )
+    yg = swap(g, some(y_pair, lambda r, c: r >= 2 or c < 4))
+    factor, state = chain_call(
+        functools.partial(chain_early, 1, width), 1, width, [pos, after(n, g), n_other], [SMEM, VMEM, VMEM], state
+    )
+    factors.append(factor)
+    yg = after(yg, factor)
+    g2, g3 = jnp.where(even, g, yg), jnp.where(even, yg, g)
+    g2_other, g3_other = swap(g2, core_pair), swap(g3, core_pair)
+    g2 = after(g2, xy, g3_other)
+    factor, state = chain_call(
+        functools.partial(chain_later, 2, width), 2, width, [pos, g2, g2_other], [SMEM, VMEM, VMEM], state
+    )
+    factors.append(factor)
+    crossed = jnp.stack([xq, xy, xz, after(cross, factor)])
+    other = swap(crossed, some(core_pair, lambda r, c: r >= 2 and c >= 4))
+    factor, state = chain_call(
+        functools.partial(chain_later, 3, width), 3, width, [pos, g3, g3_other], [SMEM, VMEM, VMEM], state
+    )
+    factors.append(factor)
     invs, rights = state
     wide = 3 * width * SNODES
-    inputs = [pos, stiffness, q, yq, zq, yzq, *crossed, *other]
+    inputs = [pos, stiffness, blocks, hop_far, zq, cross, crossed, other]
     return pl.pallas_call(
         functools.partial(box_tile, width),
         out_shape=jax.ShapeDtypeStruct((rows, width), f32),
@@ -430,7 +434,8 @@
             pltpu.VMEM((width, wide), bf16),
             pltpu.VMEM((SNODES, rows + width, width), f32),
         ],
-        compiler_params=PARAMS,
+        compiler_params=TILE_PARAMS,
+        cost_estimate=COST,
         name="tile",
     )(*inputs, *invs, *rights, *factors)
 

time: 141 us -> 122 us (0.87)
  the two profiles are of different devices: /device:TPU:19 before, /device:TPU:14 now
where the time goes in v2:
time: 122 us
  waiting for transfers between devices  52 us (43%)
  Pallas kernels  37.1 us (30%)
  starting transfers between devices  23.8 us (20%)
  other arithmetic  7.29 us (6%)
  local copies, waits for them, and re-layouts  1.26 us (1%)
    ppermute x16, waiting for transfers between devices, swap(): return lax.ppermute(x, ('row', 'col'), perm)  52 us
    pallas_call x4, Pallas kernels, chain_call(): pl.pallas_call(kernel, out_shape=[jax.ShapeDtypeStruct((width, (k + 1) *...  28.9 us
    ppermute x16, starting transfers between devices, swap(): return lax.ppermute(x, ('row', 'col'), perm)  23.8 us
    pallas_call x1, Pallas kernels, box_mesh(): pl.pallas_call(functools.partial(box_tile, width), out_shape=jax.ShapeDty...  8.15 us
  transfers between devices with their start and end apart: 16, of which 8 were waited for; matrix products, arithmetic and copies ran while one was open for 1% of the time, Pallas kernels for 19%

profile of v2, /device:TPU:14, one launch (start us, length us, event | category | flops | bytes accessed | tf_op | source)
XLA Modules:
  0.0 121.8 jit_solution(4953183589068722309)
XLA Ops:
  0.0 1.2 %copy.2 = f32[2,256,256]{2,1,0:T(8,128)S(1)} copy(f32[2,256,256]{1,2,0:T(8,128)} %bitcast.9) | data formatting | bytes 1048576 | tf_op jit(solution)/shard_map/transpose | solution.py:361
  1.2 1.1 broadcast_select_fusion.6
  2.4 0.1 collective-permute-start.3
  2.4 0.7 collective-permute-start.2
  3.1 2.4 %collective-permute-start.1 = (f32[2,256,256]{2,1,0:T(8,128)S(1)}, f32[2,256,256]{2,1,0:T(8,128)S(1)}, u32[]{:S(2)}, u32[]{:S(2)}) collective-permute-start(f32[2,256,256]{2,1,0:T(8,128)S(1)} %broadcast_select_fusion.6), channel_id=1, source_target_pairs={{0,2},{1,3},{2,0},{3,1},{4,6},{5,7},{6,4},{7,5},{10,8},{11,9},{12,... | collective-permute-start | bytes 1572872 | tf_op jit(solution)/shard_map/ppermute | solution.py:322
  5.5 2.4 %collective-permute-start = (f32[2,256,256]{2,1,0:T(8,128)S(1)}, f32[2,256,256]{2,1,0:T(8,128)S(1)}, u32[]{:S(2)}, u32[]{:S(2)}) collective-permute-start(f32[2,256,256]{2,1,0:T(8,128)S(1)} %broadcast_select_fusion.6), channel_id=1, source_target_pairs={{0,22},{1,23},{16,17},{17,16},{18,19},{19,18},{22,0},{23,1},{24,25... | collective-permute-start | bytes 1572872 | tf_op jit(solution)/shard_map/ppermute | solution.py:322
  7.9 8.2 %collective-permute-done.3 = f32[2,256,256]{2,1,0:T(8,128)S(1)} collective-permute-done((f32[2,256,256]{2,1,0:T(8,128)S(1)}, f32[2,256,256]{2,1,0:T(8,128)S(1)}, u32[]{:S(2)}, u32[]{:S(2)}) %collective-permute-start.3) | collective-permute-done | bytes 524320 | tf_op jit(solution)/shard_map/ppermute | solution.py:322
  16.1 4.5 %collective-permute-start.4 = (f32[2,256,256]{2,1,0:T(8,128)S(1)}, f32[2,256,256]{2,1,0:T(8,128)}, u32[]{:S(2)}, u32[]{:S(2)}) collective-permute-start(f32[2,256,256]{2,1,0:T(8,128)S(1)} %collective-permute-done.3), channel_id=1, source_target_pairs={{18,22},{19,23},{22,18},{23,19},{26,30},{27,31},{30,26},{31,27}} | collective-permute-start | bytes 1572872 | tf_op jit(solution)/shard_map/ppermute | solution.py:322
  20.6 0.0 collective-permute-done.2
  20.6 0.0 copy-start.2
  20.7 7.3 %collective-permute-done.1.refs_4_ = f32[2,256,256]{2,1,0:T(8,128)S(1)} collective-permute-done((f32[2,256,256]{2,1,0:T(8,128)S(1)}, f32[2,256,256]{2,1,0:T(8,128)S(1)}, u32[]{:S(2)}, u32[]{:S(2)}) %collective-permute-start.1) | collective-permute-done | bytes 524320 | tf_op jit(solution)/shard_map/ppermute | solution.py:322
  27.9 0.0 collective-permute-done.refs_3_
  27.9 0.2 select_select_fusion.1
  28.1 4.9 %collective-permute-done.4 = f32[2,256,256]{2,1,0:T(8,128)} collective-permute-done((f32[2,256,256]{2,1,0:T(8,128)S(1)}, f32[2,256,256]{2,1,0:T(8,128)}, u32[]{:S(2)}, u32[]{:S(2)}) %collective-permute-start.4) | collective-permute-done | bytes 524320 | tf_op jit(solution)/shard_map/ppermute | solution.py:322
  33.0 0.7 collective-permute-start.5
  33.7 0.0 collective-permute-done.5
  33.8 1.1 broadcast_select_fusion.3
  34.9 0.9 pad_maximum_fusion.1
  35.8 1.9 %collective-permute-start.10 = (f32[3,256,256]{2,1,0:T(8,128)}, f32[3,256,256]{2,1,0:T(8,128)}, u32[]{:S(2)}, u32[]{:S(2)}) collective-permute-start(f32[3,256,256]{2,1,0:T(8,128)} %pad_maximum_fusion.1), channel_id=1, source_target_pairs={{2,18},{3,19},{18,2},{19,3}} | collective-permute-start | bytes 2359304 | tf_op jit(solution)/shard_map/ppermute | solution.py:322
  37.8 4.4 %collective-permute-start.9 = (f32[2,256,256]{2,1,0:T(8,128)S(1)}, f32[2,256,256]{2,1,0:T(8,128)}, u32[]{:S(2)}, u32[]{:S(2)}) collective-permute-start(f32[2,256,256]{2,1,0:T(8,128)S(1)} %collective-permute-done.3), channel_id=1, source_target_pairs={{18,20},{19,21},{20,18},{21,19},{26,28},{27,29},{28,26},{29,27}} | collective-permute-start | bytes 1572872 | tf_op jit(solution)/shard_map/ppermute | solution.py:322
  42.2 0.1 collective-permute-start.8
  42.3 12.8 %collective-permute-done.10 = f32[3,256,256]{2,1,0:T(8,128)} collective-permute-done((f32[3,256,256]{2,1,0:T(8,128)}, f32[3,256,256]{2,1,0:T(8,128)}, u32[]{:S(2)}, u32[]{:S(2)}) %collective-permute-start.10) | collective-permute-done | bytes 786464 | tf_op jit(solution)/shard_map/ppermute | solution.py:322
  55.1 1.2 %broadcast_select_fusion.a_ref = f32[3,256,256]{2,1,0:T(8,128)S(1)} fusion(f32[3,256,256]{2,1,0:T(8,128)} %collective-permute-done.10, pred[]{:T(512)S(6)} %and.34, f32[2,256,256]{2,1,0:T(8,128)S(1)} %broadcast_select_fusion.3, f32[1,256,256]{2,1,0:T(8,128)S(1)} %slice_select_fusion), kind=kLoop, calls=%fused_computation.4 | loop fusion | flops 393216 | bytes 2359297 | tf_op jit(solution)/shard_map/jit(_where)/select_n | solution.py:386
  56.3 0.0 collective-permute-done.9
  56.3 4.4 %collective-permute-done.8 = f32[2,256,256]{2,1,0:T(8,128)} collective-permute-done((f32[2,256,256]{2,1,0:T(8,128)S(1)}, f32[2,256,256]{2,1,0:T(8,128)}, u32[]{:S(2)}, u32[]{:S(2)}) %collective-permute-start.8) | collective-permute-done | bytes 524320 | tf_op jit(solution)/shard_map/ppermute | solution.py:322
  60.7 0.1 pad_add_fusion.pos_ref.refs_0_
  60.8 2.2 %collective-permute-done.11.b_ref = f32[3,256,256]{2,1,0:T(8,128)S(1)} collective-permute-done((f32[3,256,256]{2,1,0:T(8,128)S(1)}, f32[3,256,256]{2,1,0:T(8,128)S(1)}, u32[]{:S(2)}, u32[]{:S(2)}) %collective-permute-start.11) | collective-permute-done | bytes 786464 | tf_op jit(solution)/shard_map/ppermute | solution.py:322
  63.0 6.3 %chain0.1 = (f32[256,256]{1,0:T(8,128)S(1)}, bf16[256,768]{1,0:T(8,128)(2,1)S(1)}, bf16[256,768]{1,0:T(8,128)(2,1)S(1)}) custom-call(s32[2]{0:T(128)S(1)} %pad_add_fusion.pos_ref.refs_0_, f32[3,256,256]{2,1,0:T(8,128)S(1)} %broadcast_select_fusion.a_ref, f32[3,256,256]{2,1,0:T(8,128)S(1)} %collective-permute-done.11.b_ref), custom_call_target="tpu_custom_call" | custom-call | flops 1000 | bytes 1024 | tf_op jit(solution)/shard_map/chain0/pallas_call | solution.py:151
  69.3 0.0 copy-start.3
  69.3 1.4 %select_select_fusion = (f32[2,256,256]{2,1,0:T(8,128)S(1)}, f32[2,256,256]{2,1,0:T(8,128)S(1)}) fusion(f32[2,256,256]{2,1,0:T(8,128)} %collective-permute-done.4, f32[2,256,256]{2,1,0:T(8,128)} %collective-permute-done.9, f32[2,256,256]{2,1,0:T(8,128)S(1)} %collective-permute-done.1.refs_4_, f32[2,256,256]{2,1,0:T(8,128)} %collective-permute-done.8, ...), kind=kLoop, calls=%fused_computation.2 | loop fusion | flops 786432 | bytes 4718596 | tf_op jit(solution)/shard_map/jit(_where)/select_n | solution.py:376
  70.6 1.9 %collective-permute-start.12 = (f32[2,256,256]{2,1,0:T(8,128)S(1)}, f32[2,256,256]{2,1,0:T(8,128)S(1)}, u32[]{:S(2)}, u32[]{:S(2)}) collective-permute-start(f32[2,256,256]{2,1,0:T(8,128)S(1)} %get-tuple-element.45), channel_id=1, source_target_pairs={{0,1},{1,0},{2,3},{3,2},{8,9},{9,8},{10,11},{11,10},{16,17},{17,16... | collective-permute-start | bytes 1572872 | tf_op jit(solution)/shard_map/ppermute | solution.py:322
  72.6 0.9 collective-permute-start.7
  73.5 6.9 %chain1.1 = (f32[256,512]{1,0:T(8,128)S(1)}, bf16[256,768]{1,0:T(8,128)(2,1)S(1)}, bf16[256,768]{1,0:T(8,128)(2,1)S(1)}) custom-call(s32[2]{0:T(128)S(1)} %pad_add_fusion.pos_ref.refs_0_, f32[3,256,256]{2,1,0:T(8,128)S(1)} %broadcast_select_fusion.a_ref, f32[3,256,256]{2,1,0:T(8,128)S(1)} %collective-permute-done.11.b_ref, ...), custom_call_target="tpu_custom_call" | custom-call | flops 1000 | bytes 1024 | tf_op jit(solution)/shard_map/chain1/pallas_call | solution.py:151
  80.4 6.1 %collective-permute-done.12 = f32[2,256,256]{2,1,0:T(8,128)S(1)} collective-permute-done((f32[2,256,256]{2,1,0:T(8,128)S(1)}, f32[2,256,256]{2,1,0:T(8,128)S(1)}, u32[]{:S(2)}, u32[]{:S(2)}) %collective-permute-start.12) | collective-permute-done | bytes 524320 | tf_op jit(solution)/shard_map/ppermute | solution.py:322
  86.5 0.1 broadcast_select_fusion.1
  86.6 0.1 collective-permute-start.13
  86.7 0.5 collective-permute-start.14
  87.2 2.2 %collective-permute-start.6 = (f32[2,256,256]{2,1,0:T(8,128)S(1)}, f32[2,256,256]{2,1,0:T(8,128)S(1)}, u32[]{:S(2)}, u32[]{:S(2)}) collective-permute-start(f32[2,256,256]{2,1,0:T(8,128)S(1)} %get-tuple-element.46), channel_id=1, source_target_pairs={{4,20},{5,21},{6,22},{7,23},{12,28},{13,29},{14,30},{15,31},{16,17... | collective-permute-start | bytes 1572872 | tf_op jit(solution)/shard_map/ppermute | solution.py:322
  89.4 0.0 collective-permute-done.7
  89.4 0.0 collective-permute-done.13.b_ref
  89.4 7.5 %chain2.1 = (f32[256,768]{1,0:T(8,128)S(1)}, bf16[256,768]{1,0:T(8,128)(2,1)S(1)}, bf16[256,1536]{1,0:T(8,128)(2,1)S(1)}) custom-call(s32[2]{0:T(128)S(1)} %pad_add_fusion.pos_ref.refs_0_, f32[2,256,256]{2,1,0:T(8,128)S(1)} %get-tuple-element.33.a_ref, f32[2,256,256]{2,1,0:T(8,128)S(1)} %collective-permute-done.14.b_ref, ...), custom_call_target="tpu_custom_call" | custom-call | flops 1000 | bytes 1024 | tf_op jit(solution)/shard_map/chain2/pallas_call | solution.py:151
  96.8 6.1 %collective-permute-done.6.refs_5_ = f32[2,256,256]{2,1,0:T(8,128)S(1)} collective-permute-done((f32[2,256,256]{2,1,0:T(8,128)S(1)}, f32[2,256,256]{2,1,0:T(8,128)S(1)}, u32[]{:S(2)}, u32[]{:S(2)}) %collective-permute-start.6) | collective-permute-done | bytes 524320 | tf_op jit(solution)/shard_map/ppermute | solution.py:322
  102.9 1.2 pad_maximum_fusion.refs_6_
  104.2 0.0 copy-start
  104.2 1.1 collective-permute-start.15
  105.3 8.3 %chain3.1 = (f32[256,1024]{1,0:T(8,128)S(1)}, bf16[256,768]{1,0:T(8,128)(2,1)S(1)}, bf16[256,2304]{1,0:T(8,128)(2,1)S(1)}) custom-call(s32[2]{0:T(128)S(1)} %pad_add_fusion.pos_ref.refs_0_, f32[2,256,256]{2,1,0:T(8,128)S(1)} %get-tuple-element.43.a_ref, f32[2,256,256]{2,1,0:T(8,128)S(1)} %collective-permute-done.13.b_ref, ...), custom_call_target="tpu_custom_call" | custom-call | flops 1000 | bytes 1024 | tf_op jit(solution)/shard_map/chain3/pallas_call | solution.py:151
  113.6 0.0 collective-permute-done.15.refs_7_
  113.6 8.1 %tile.1 = f32[512,256]{1,0:T(8,128)} custom-call(s32[2]{0:T(128)S(1)} %pad_add_fusion.pos_ref.refs_0_, f32[512,256]{1,0:T(8,128)S(1)} %copy-done, f32[2,256,256]{2,1,0:T(8,128)S(1)} %bitcast.11, f32[2,256,256]{2,1,0:T(8,128)S(1)} %collective-permute-done.refs_3_, f32[2,256,256]{2,1,0:T(8,128)S(1)} %collective-permute-done.1.refs_4_, ...), custom_call_target="tpu_custom_call" | custom-call | flops 1000 | bytes 1024 | tf_op jit(solution)/shard_map/tile/pallas_call | solution.py:427
  (8 shorter events, 0.1 us)
Async XLA Ops:
  2.4 13.7 %collective-permute-start.3 = (f32[2,256,256]{2,1,0:T(8,128)S(1)}, f32[2,256,256]{2,1,0:T(8,128)S(1)}, u32[]{:S(2)}, u32[]{:S(2)}) collective-permute-start(f32[2,256,256]{2,1,0:T(8,128)S(1)} %broadcast_select_fusion.6), channel_id=1, source_target_pairs={{0,16},{1,17},{2,18},{3,19},{4,20},{5,21},{6,22},{7,23},{8,24},{9,... | collective-permute-start | bytes 1572872 | tf_op jit(solution)/shard_map/ppermute | solution.py:322
  2.4 18.2 %collective-permute-start.2 = (f32[2,256,256]{2,1,0:T(8,128)S(1)}, f32[2,256,256]{2,1,0:T(8,128)S(1)}, u32[]{:S(2)}, u32[]{:S(2)}) collective-permute-start(f32[2,256,256]{2,1,0:T(8,128)S(1)} %broadcast_select_fusion.6), channel_id=1, source_target_pairs={{0,20},{1,21},{4,5},{5,4},{6,7},{7,6},{12,13},{13,12},{14,15},{15,... | collective-permute-start | bytes 1572872 | tf_op jit(solution)/shard_map/ppermute | solution.py:322
  3.1 24.8 %collective-permute-start.1 = (f32[2,256,256]{2,1,0:T(8,128)S(1)}, f32[2,256,256]{2,1,0:T(8,128)S(1)}, u32[]{:S(2)}, u32[]{:S(2)}) collective-permute-start(f32[2,256,256]{2,1,0:T(8,128)S(1)} %broadcast_select_fusion.6), channel_id=1, source_target_pairs={{0,2},{1,3},{2,0},{3,1},{4,6},{5,7},{6,4},{7,5},{10,8},{11,9},{12,... | collective-permute-start | bytes 1572872 | tf_op jit(solution)/shard_map/ppermute | solution.py:322
  5.5 22.4 %collective-permute-start = (f32[2,256,256]{2,1,0:T(8,128)S(1)}, f32[2,256,256]{2,1,0:T(8,128)S(1)}, u32[]{:S(2)}, u32[]{:S(2)}) collective-permute-start(f32[2,256,256]{2,1,0:T(8,128)S(1)} %broadcast_select_fusion.6), channel_id=1, source_target_pairs={{0,22},{1,23},{16,17},{17,16},{18,19},{19,18},{22,0},{23,1},{24,25... | collective-permute-start | bytes 1572872 | tf_op jit(solution)/shard_map/ppermute | solution.py:322
  16.1 16.9 %collective-permute-start.4 = (f32[2,256,256]{2,1,0:T(8,128)S(1)}, f32[2,256,256]{2,1,0:T(8,128)}, u32[]{:S(2)}, u32[]{:S(2)}) collective-permute-start(f32[2,256,256]{2,1,0:T(8,128)S(1)} %collective-permute-done.3), channel_id=1, source_target_pairs={{18,22},{19,23},{22,18},{23,19},{26,30},{27,31},{30,26},{31,27}} | collective-permute-start | bytes 1572872 | tf_op jit(solution)/shard_map/ppermute | solution.py:322
  20.6 7.4 %copy-start.2 = (f32[2,256,256]{2,1,0:T(8,128)}, f32[2,256,256]{2,1,0:T(8,128)S(1)}, u32[]{:S(2)}) copy-start(f32[2,256,256]{2,1,0:T(8,128)S(1)} %collective-permute-done.2) | copy-start | bytes 1572868
  28.1 5.6 %copy-start.1 = (f32[2,256,256]{2,1,0:T(8,128)}, f32[2,256,256]{2,1,0:T(8,128)S(1)}, u32[]{:S(2)}) copy-start(f32[2,256,256]{2,1,0:T(8,128)S(1)} %select_select_fusion.1) | copy-start | bytes 1572868
  33.0 0.7 collective-permute-start.5
  35.8 19.2 %collective-permute-start.10 = (f32[3,256,256]{2,1,0:T(8,128)}, f32[3,256,256]{2,1,0:T(8,128)}, u32[]{:S(2)}, u32[]{:S(2)}) collective-permute-start(f32[3,256,256]{2,1,0:T(8,128)} %pad_maximum_fusion.1), channel_id=1, source_target_pairs={{2,18},{3,19},{18,2},{19,3}} | collective-permute-start | bytes 2359304 | tf_op jit(solution)/shard_map/ppermute | solution.py:322
  37.8 18.6 %collective-permute-start.9 = (f32[2,256,256]{2,1,0:T(8,128)S(1)}, f32[2,256,256]{2,1,0:T(8,128)}, u32[]{:S(2)}, u32[]{:S(2)}) collective-permute-start(f32[2,256,256]{2,1,0:T(8,128)S(1)} %collective-permute-done.3), channel_id=1, source_target_pairs={{18,20},{19,21},{20,18},{21,19},{26,28},{27,29},{28,26},{29,27}} | collective-permute-start | bytes 1572872 | tf_op jit(solution)/shard_map/ppermute | solution.py:322
  42.2 18.5 %collective-permute-start.8 = (f32[2,256,256]{2,1,0:T(8,128)S(1)}, f32[2,256,256]{2,1,0:T(8,128)}, u32[]{:S(2)}, u32[]{:S(2)}) collective-permute-start(f32[2,256,256]{2,1,0:T(8,128)S(1)} %collective-permute-done.1.refs_4_), channel_id=1, source_target_pairs={{0,16},{1,17},{2,18},{3,19},{4,20},{5,21},{6,22},{7,23},{8,24},{9,... | collective-permute-start | bytes 1572872 | tf_op jit(solution)/shard_map/ppermute | solution.py:322
  60.7 2.3 %collective-permute-start.11 = (f32[3,256,256]{2,1,0:T(8,128)S(1)}, f32[3,256,256]{2,1,0:T(8,128)S(1)}, u32[]{:S(2)}, u32[]{:S(2)}) collective-permute-start(f32[3,256,256]{2,1,0:T(8,128)S(1)} %broadcast_select_fusion.a_ref), channel_id=1, source_target_pairs={{0,8},{1,9},{2,10},{3,11},{4,12},{5,13},{6,14},{7,15},{8,0},{9,1},... | collective-permute-start | bytes 2359304 | tf_op jit(solution)/shard_map/ppermute | solution.py:322
  69.3 3.3 %copy-start.3 = (f32[2,256,256]{2,1,0:T(8,128)S(1)}, f32[2,256,256]{2,1,0:T(8,128)}, u32[]{:S(2)}) copy-start(f32[2,256,256]{2,1,0:T(8,128)} %copy-done.2) | copy-start | bytes 1572868
  70.6 15.9 %collective-permute-start.12 = (f32[2,256,256]{2,1,0:T(8,128)S(1)}, f32[2,256,256]{2,1,0:T(8,128)S(1)}, u32[]{:S(2)}, u32[]{:S(2)}) collective-permute-start(f32[2,256,256]{2,1,0:T(8,128)S(1)} %get-tuple-element.45), channel_id=1, source_target_pairs={{0,1},{1,0},{2,3},{3,2},{8,9},{9,8},{10,11},{11,10},{16,17},{17,16... | collective-permute-start | bytes 1572872 | tf_op jit(solution)/shard_map/ppermute | solution.py:322
  72.6 16.8 %collective-permute-start.7 = (f32[2,256,256]{2,1,0:T(8,128)S(1)}, f32[2,256,256]{2,1,0:T(8,128)S(1)}, u32[]{:S(2)}, u32[]{:S(2)}) collective-permute-start(f32[2,256,256]{2,1,0:T(8,128)S(1)} %copy-done.3), channel_id=1, source_target_pairs={{4,20},{5,21},{6,22},{7,23},{12,28},{13,29},{14,30},{15,31},{20,4}... | collective-permute-start | bytes 1572872 | tf_op jit(solution)/shard_map/ppermute | solution.py:322
  86.6 2.8 %collective-permute-start.13 = (f32[2,256,256]{2,1,0:T(8,128)S(1)}, f32[2,256,256]{2,1,0:T(8,128)S(1)}, u32[]{:S(2)}, u32[]{:S(2)}) collective-permute-start(f32[2,256,256]{2,1,0:T(8,128)S(1)} %get-tuple-element.43.a_ref), channel_id=1, source_target_pairs={{0,8},{1,9},{2,10},{3,11},{4,12},{5,13},{6,14},{7,15},{8,0},{9,1},... | collective-permute-start | bytes 1572872 | tf_op jit(solution)/shard_map/ppermute | solution.py:322
  86.7 2.7 %collective-permute-start.14 = (f32[2,256,256]{2,1,0:T(8,128)S(1)}, f32[2,256,256]{2,1,0:T(8,128)S(1)}, u32[]{:S(2)}, u32[]{:S(2)}) collective-permute-start(f32[2,256,256]{2,1,0:T(8,128)S(1)} %get-tuple-element.33.a_ref), channel_id=1, source_target_pairs={{0,8},{1,9},{2,10},{3,11},{4,12},{5,13},{6,14},{7,15},{8,0},{9,1},... | collective-permute-start | bytes 1572872 | tf_op jit(solution)/shard_map/ppermute | solution.py:322
  87.2 15.8 %collective-permute-start.6 = (f32[2,256,256]{2,1,0:T(8,128)S(1)}, f32[2,256,256]{2,1,0:T(8,128)S(1)}, u32[]{:S(2)}, u32[]{:S(2)}) collective-permute-start(f32[2,256,256]{2,1,0:T(8,128)S(1)} %get-tuple-element.46), channel_id=1, source_target_pairs={{4,20},{5,21},{6,22},{7,23},{12,28},{13,29},{14,30},{15,31},{16,17... | collective-permute-start | bytes 1572872 | tf_op jit(solution)/shard_map/ppermute | solution.py:322
  104.2 9.5 %copy-start = (f32[512,256]{1,0:T(8,128)S(1)}, f32[512,256]{1,0:T(8,128)}, u32[]{:S(2)}) copy-start(f32[512,256]{1,0:T(8,128)} %refs_1_.1) | copy-start | bytes 1572868
  104.2 9.5 %collective-permute-start.15 = (f32[4,2,256,256]{3,2,1,0:T(8,128)S(1)}, f32[4,2,256,256]{3,2,1,0:T(8,128)S(1)}, u32[]{:S(2)}, u32[]{:S(2)}) collective-permute-start(f32[4,2,256,256]{3,2,1,0:T(8,128)S(1)} %pad_maximum_fusion.refs_6_), channel_id=1, source_target_pairs={{20,28},{21,29},{22,30},{23,31},{28,20},{29,21},{30,22},{31,23}} | collective-permute-start | bytes 6291464 | tf_op jit(solution)/shard_map/ppermute | solution.py:322

commit v3 on v2

--- a/solution.py
+++ b/solution.py
@@ -368,8 +368,9 @@
     xq = swap(q, x_pair)
     hop_late = swap(xq, chosen([((r, c), (r, c + 4)) for r in (2, 3) for c in (2, 3)]))
     hop_later = swap(xq, chosen([((r, c), (r, c + 2)) for r in (2, 3) for c in (2, 3)]))
-    xz = swap(zq, x_pair)
     to_schur = some(x_pair, lambda r, c: c >= 4)
+    near_z = swap(zq, some(x_pair, lambda r, c: c < 2))
+    xz = swap(zq, to_schur)
     xy = swap(hop, to_schur)
 
     def held(on_near, on_far):
@@ -384,7 +385,7 @@
     n = jnp.concatenate([jnp.where(even, m[:1], ym[:1]), jnp.where(even, ym, m)], 0)
     late = chosen([((0, c), (2, c)) for c in (2, 3)])
     n = jnp.where((r == 2) & (c < 4) & jnp.logical_not(near), swap(n, late), n)
-    n = after(n, hop_later, xz)
+    n = after(n, hop_later)
     n_other = swap(n, core_pair)
 
     state, factors = ([], []), []
@@ -399,12 +400,12 @@
     )
     g_near = after(hop_later, factor)
     g = held(
-        jnp.where(schur, g_near, jnp.where(r < 2, zq, xz)),
+        jnp.where(schur, g_near, jnp.where(r < 2, zq, near_z)),
         jnp.where(schur, hop_late, jnp.where(r < 2, q, xq)),
     )
     yg = swap(g, some(y_pair, lambda r, c: r >= 2 or c < 4))
     factor, state = chain_call(
-        functools.partial(chain_early, 1, width), 1, width, [pos, after(n, g), n_other], [SMEM, VMEM, VMEM], state
+        functools.partial(chain_early, 1, width), 1, width, [pos, after(n, g, xz), n_other], [SMEM, VMEM, VMEM], state
     )
     factors.append(factor)
     yg = after(yg, factor)

time: 122 us -> 115 us (0.943)
  the two profiles are of different devices: /device:TPU:14 before, /device:TPU:19 now
where the time goes in v3:
time: 115 us
  Pallas kernels  38.2 us (33%)
  starting transfers between devices  36.2 us (31%)
  waiting for transfers between devices  33.8 us (29%)
  other arithmetic  4.28 us (4%)
  local copies, waits for them, and re-layouts  1.93 us (2%)
    ppermute x17, starting transfers between devices, swap(): return lax.ppermute(x, ('row', 'col'), perm)  36.2 us
    ppermute x17, waiting for transfers between devices, swap(): return lax.ppermute(x, ('row', 'col'), perm)  33.8 us
    pallas_call x4, Pallas kernels, chain_call(): pl.pallas_call(kernel, out_shape=[jax.ShapeDtypeStruct((width, (k + 1) *...  28.9 us
    pallas_call x1, Pallas kernels, box_mesh(): pl.pallas_call(functools.partial(box_tile, width), out_shape=jax.ShapeDty...  9.26 us
  transfers between devices with their start and end apart: 17, of which 6 were waited for; matrix products, arithmetic and copies ran while one was open for 2% of the time, Pallas kernels for 25%

profile of v3, /device:TPU:19, one launch (start us, length us, event | category | flops | bytes accessed | tf_op | source)
XLA Modules:
  0.0 114.6 jit_solution(4601484522655826972)
XLA Ops:
  0.0 1.2 %copy.2 = f32[2,256,256]{2,1,0:T(8,128)S(1)} copy(f32[2,256,256]{1,2,0:T(8,128)} %bitcast.9) | data formatting | bytes 1048576 | tf_op jit(solution)/shard_map/transpose | solution.py:361
  1.2 1.1 broadcast_select_fusion.6
  2.4 0.1 collective-permute-start.3
  2.4 0.7 collective-permute-start.2
  3.1 0.7 collective-permute-start.1
  3.9 0.7 collective-permute-start
  4.6 16.3 %collective-permute-done.3 = f32[2,256,256]{2,1,0:T(8,128)S(1)} collective-permute-done((f32[2,256,256]{2,1,0:T(8,128)S(1)}, f32[2,256,256]{2,1,0:T(8,128)S(1)}, u32[]{:S(2)}, u32[]{:S(2)}) %collective-permute-start.3) | collective-permute-done | bytes 524320 | tf_op jit(solution)/shard_map/ppermute | solution.py:322
  20.8 1.5 %collective-permute-start.4 = (f32[2,256,256]{2,1,0:T(8,128)S(1)}, f32[2,256,256]{2,1,0:T(8,128)}, u32[]{:S(2)}, u32[]{:S(2)}) collective-permute-start(f32[2,256,256]{2,1,0:T(8,128)S(1)} %collective-permute-done.3), channel_id=1, source_target_pairs={{18,22},{19,23},{22,18},{23,19},{26,30},{27,31},{30,26},{31,27}} | collective-permute-start | bytes 1572872 | tf_op jit(solution)/shard_map/ppermute | solution.py:322
  22.3 0.0 collective-permute-done.2
  22.3 0.0 collective-permute-done.1.refs_4_
  22.3 0.2 select_select_fusion.1
  22.5 0.6 copy-done.2
  23.1 0.0 collective-permute-done.4
  23.1 0.7 collective-permute-start.5
  23.8 0.1 copy-done.1
  23.9 0.1 broadcast_select_fusion.3
  24.0 0.9 pad_maximum_fusion.1
  25.0 1.6 %collective-permute-start.10 = (f32[3,256,256]{2,1,0:T(8,128)}, f32[3,256,256]{2,1,0:T(8,128)}, u32[]{:S(2)}, u32[]{:S(2)}) collective-permute-start(f32[3,256,256]{2,1,0:T(8,128)} %pad_maximum_fusion.1), channel_id=1, source_target_pairs={{2,18},{3,19},{18,2},{19,3}} | collective-permute-start | bytes 2359304 | tf_op jit(solution)/shard_map/ppermute | solution.py:322
  26.6 11.0 %collective-permute-start.9 = (f32[2,256,256]{2,1,0:T(8,128)S(1)}, f32[2,256,256]{2,1,0:T(8,128)}, u32[]{:S(2)}, u32[]{:S(2)}) collective-permute-start(f32[2,256,256]{2,1,0:T(8,128)S(1)} %collective-permute-done.3), channel_id=1, source_target_pairs={{18,20},{19,21},{20,18},{21,19},{26,28},{27,29},{28,26},{29,27}} | collective-permute-start | bytes 1572872 | tf_op jit(solution)/shard_map/ppermute | solution.py:322
  37.6 0.1 broadcast_select_fusion.a_ref
  37.7 8.6 %collective-permute-done.9 = f32[2,256,256]{2,1,0:T(8,128)} collective-permute-done((f32[2,256,256]{2,1,0:T(8,128)S(1)}, f32[2,256,256]{2,1,0:T(8,128)}, u32[]{:S(2)}, u32[]{:S(2)}) %collective-permute-start.9) | collective-permute-done | bytes 524320 | tf_op jit(solution)/shard_map/ppermute | solution.py:322
  46.4 4.2 %collective-permute-start.11 = (f32[3,256,256]{2,1,0:T(8,128)S(1)}, f32[3,256,256]{2,1,0:T(8,128)S(1)}, u32[]{:S(2)}, u32[]{:S(2)}) collective-permute-start(f32[3,256,256]{2,1,0:T(8,128)S(1)} %broadcast_select_fusion.a_ref), channel_id=1, source_target_pairs={{0,8},{1,9},{2,10},{3,11},{4,12},{5,13},{6,14},{7,15},{8,0},{9,1},... | collective-permute-start | bytes 2359304 | tf_op jit(solution)/shard_map/ppermute | solution.py:322
  50.6 0.7 collective-permute-start.12
  51.3 0.1 pad_add_fusion.pos_ref.refs_0_
  51.3 1.9 %collective-permute-start.8 = (f32[2,256,256]{2,1,0:T(8,128)S(1)}, f32[2,256,256]{2,1,0:T(8,128)S(1)}, u32[]{:S(2)}, u32[]{:S(2)}) collective-permute-start(f32[2,256,256]{2,1,0:T(8,128)S(1)} %collective-permute-done.1.refs_4_), channel_id=1, source_target_pairs={{4,20},{5,21},{6,22},{7,23},{12,28},{13,29},{14,30},{15,31},{20,4}... | collective-permute-start | bytes 1572872 | tf_op jit(solution)/shard_map/ppermute | solution.py:322
  53.2 0.0 collective-permute-done.11.b_ref
  53.3 6.3 %chain0.1 = (f32[256,256]{1,0:T(8,128)S(1)}, bf16[256,768]{1,0:T(8,128)(2,1)S(1)}, bf16[256,768]{1,0:T(8,128)(2,1)S(1)}) custom-call(s32[2]{0:T(128)S(1)} %pad_add_fusion.pos_ref.refs_0_, f32[3,256,256]{2,1,0:T(8,128)S(1)} %broadcast_select_fusion.a_ref, f32[3,256,256]{2,1,0:T(8,128)S(1)} %collective-permute-done.11.b_ref), custom_call_target="tpu_custom_call" | custom-call | flops 1000 | bytes 1024 | tf_op jit(solution)/shard_map/chain0/pallas_call | solution.py:151
  59.6 0.0 copy-start.3
  59.6 1.5 %select_select_fusion = (f32[2,256,256]{2,1,0:T(8,128)S(1)}, f32[2,256,256]{2,1,0:T(8,128)S(1)}) fusion(f32[2,256,256]{2,1,0:T(8,128)} %collective-permute-done.4, f32[2,256,256]{2,1,0:T(8,128)} %collective-permute-done.9, f32[2,256,256]{2,1,0:T(8,128)S(1)} %collective-permute-done.1.refs_4_, f32[2,256,256]{2,1,0:T(8,128)S(1)} %collective-permute-done.12, ...), kind=kLoop, calls=%fused_computation.2 | loop fusion | flops 786432 | bytes 4718596 | tf_op jit(solution)/shard_map/jit(_where)/select_n | solution.py:377
  61.1 4.2 %collective-permute-start.13 = (f32[2,256,256]{2,1,0:T(8,128)S(1)}, f32[2,256,256]{2,1,0:T(8,128)S(1)}, u32[]{:S(2)}, u32[]{:S(2)}) collective-permute-start(f32[2,256,256]{2,1,0:T(8,128)S(1)} %get-tuple-element.45), channel_id=1, source_target_pairs={{0,1},{1,0},{2,3},{3,2},{8,9},{9,8},{10,11},{11,10},{16,17},{17,16... | collective-permute-start | bytes 1572872 | tf_op jit(solution)/shard_map/ppermute | solution.py:322
  65.3 2.1 %collective-permute-start.7 = (f32[2,256,256]{2,1,0:T(8,128)S(1)}, f32[2,256,256]{2,1,0:T(8,128)S(1)}, u32[]{:S(2)}, u32[]{:S(2)}) collective-permute-start(f32[2,256,256]{2,1,0:T(8,128)S(1)} %copy-done.3), channel_id=1, source_target_pairs={{4,20},{5,21},{6,22},{7,23},{12,28},{13,29},{14,30},{15,31},{20,4}... | collective-permute-start | bytes 1572872 | tf_op jit(solution)/shard_map/ppermute | solution.py:322
  67.4 0.0 collective-permute-done.8
  67.4 6.9 %chain1.1 = (f32[256,512]{1,0:T(8,128)S(1)}, bf16[256,768]{1,0:T(8,128)(2,1)S(1)}, bf16[256,768]{1,0:T(8,128)(2,1)S(1)}) custom-call(s32[2]{0:T(128)S(1)} %pad_add_fusion.pos_ref.refs_0_, f32[3,256,256]{2,1,0:T(8,128)S(1)} %broadcast_select_fusion.a_ref, f32[3,256,256]{2,1,0:T(8,128)S(1)} %collective-permute-done.11.b_ref, ...), custom_call_target="tpu_custom_call" | custom-call | flops 1000 | bytes 1024 | tf_op jit(solution)/shard_map/chain1/pallas_call | solution.py:151
  74.3 3.3 %collective-permute-done.13 = f32[2,256,256]{2,1,0:T(8,128)S(1)} collective-permute-done((f32[2,256,256]{2,1,0:T(8,128)S(1)}, f32[2,256,256]{2,1,0:T(8,128)S(1)}, u32[]{:S(2)}, u32[]{:S(2)}) %collective-permute-start.13) | collective-permute-done | bytes 524320 | tf_op jit(solution)/shard_map/ppermute | solution.py:322
  77.6 0.1 broadcast_select_fusion.1
  77.6 0.6 collective-permute-start.14
  78.3 0.1 collective-permute-start.15
  78.4 1.9 %collective-permute-start.6 = (f32[2,256,256]{2,1,0:T(8,128)S(1)}, f32[2,256,256]{2,1,0:T(8,128)S(1)}, u32[]{:S(2)}, u32[]{:S(2)}) collective-permute-start(f32[2,256,256]{2,1,0:T(8,128)S(1)} %get-tuple-element.46), channel_id=1, source_target_pairs={{4,20},{5,21},{6,22},{7,23},{12,28},{13,29},{14,30},{15,31},{16,17... | collective-permute-start | bytes 1572872 | tf_op jit(solution)/shard_map/ppermute | solution.py:322
  80.3 0.1 collective-permute-done.7
  80.4 0.0 collective-permute-done.14.b_ref
  80.4 0.1 collective-permute-done.15.b_ref
  80.6 7.4 %chain2.1 = (f32[256,768]{1,0:T(8,128)S(1)}, bf16[256,768]{1,0:T(8,128)(2,1)S(1)}, bf16[256,1536]{1,0:T(8,128)(2,1)S(1)}) custom-call(s32[2]{0:T(128)S(1)} %pad_add_fusion.pos_ref.refs_0_, f32[2,256,256]{2,1,0:T(8,128)S(1)} %get-tuple-element.33.a_ref, f32[2,256,256]{2,1,0:T(8,128)S(1)} %collective-permute-done.15.b_ref, ...), custom_call_target="tpu_custom_call" | custom-call | flops 1000 | bytes 1024 | tf_op jit(solution)/shard_map/chain2/pallas_call | solution.py:151
  88.0 5.3 %collective-permute-done.6.refs_5_ = f32[2,256,256]{2,1,0:T(8,128)S(1)} collective-permute-done((f32[2,256,256]{2,1,0:T(8,128)S(1)}, f32[2,256,256]{2,1,0:T(8,128)S(1)}, u32[]{:S(2)}, u32[]{:S(2)}) %collective-permute-start.6) | collective-permute-done | bytes 524320 | tf_op jit(solution)/shard_map/ppermute | solution.py:322
  93.3 0.2 pad_maximum_fusion.refs_6_
  93.5 0.0 copy-start
  93.5 3.5 %collective-permute-start.16 = (f32[4,2,256,256]{3,2,1,0:T(8,128)S(1)}, f32[4,2,256,256]{3,2,1,0:T(8,128)S(1)}, u32[]{:S(2)}, u32[]{:S(2)}) collective-permute-start(f32[4,2,256,256]{3,2,1,0:T(8,128)S(1)} %pad_maximum_fusion.refs_6_), channel_id=1, source_target_pairs={{20,28},{21,29},{22,30},{23,31},{28,20},{29,21},{30,22},{31,23}} | collective-permute-start | bytes 6291464 | tf_op jit(solution)/shard_map/ppermute | solution.py:322
  97.0 8.3 %chain3.1 = (f32[256,1024]{1,0:T(8,128)S(1)}, bf16[256,768]{1,0:T(8,128)(2,1)S(1)}, bf16[256,2304]{1,0:T(8,128)(2,1)S(1)}) custom-call(s32[2]{0:T(128)S(1)} %pad_add_fusion.pos_ref.refs_0_, f32[2,256,256]{2,1,0:T(8,128)S(1)} %get-tuple-element.43.a_ref, f32[2,256,256]{2,1,0:T(8,128)S(1)} %collective-permute-done.14.b_ref, ...), custom_call_target="tpu_custom_call" | custom-call | flops 1000 | bytes 1024 | tf_op jit(solution)/shard_map/chain3/pallas_call | solution.py:151
  105.4 9.3 %tile.1 = f32[512,256]{1,0:T(8,128)} custom-call(s32[2]{0:T(128)S(1)} %pad_add_fusion.pos_ref.refs_0_, f32[512,256]{1,0:T(8,128)S(1)} %copy-done, f32[2,256,256]{2,1,0:T(8,128)S(1)} %bitcast.11, f32[2,256,256]{2,1,0:T(8,128)S(1)} %collective-permute-done.refs_3_, f32[2,256,256]{2,1,0:T(8,128)S(1)} %collective-permute-done.1.refs_4_, ...), custom_call_target="tpu_custom_call" | custom-call | flops 1000 | bytes 1024 | tf_op jit(solution)/shard_map/tile/pallas_call | solution.py:428
  (10 shorter events, 0.1 us)
Async XLA Ops:
  2.4 18.5 %collective-permute-start.3 = (f32[2,256,256]{2,1,0:T(8,128)S(1)}, f32[2,256,256]{2,1,0:T(8,128)S(1)}, u32[]{:S(2)}, u32[]{:S(2)}) collective-permute-start(f32[2,256,256]{2,1,0:T(8,128)S(1)} %broadcast_select_fusion.6), channel_id=1, source_target_pairs={{0,16},{1,17},{2,18},{3,19},{4,20},{5,21},{6,22},{7,23},{8,24},{9,... | collective-permute-start | bytes 1572872 | tf_op jit(solution)/shard_map/ppermute | solution.py:322
  2.4 19.9 %collective-permute-start.2 = (f32[2,256,256]{2,1,0:T(8,128)S(1)}, f32[2,256,256]{2,1,0:T(8,128)S(1)}, u32[]{:S(2)}, u32[]{:S(2)}) collective-permute-start(f32[2,256,256]{2,1,0:T(8,128)S(1)} %broadcast_select_fusion.6), channel_id=1, source_target_pairs={{0,20},{1,21},{4,5},{5,4},{6,7},{7,6},{12,13},{13,12},{14,15},{15,... | collective-permute-start | bytes 1572872 | tf_op jit(solution)/shard_map/ppermute | solution.py:322
  3.1 19.2 %collective-permute-start.1 = (f32[2,256,256]{2,1,0:T(8,128)S(1)}, f32[2,256,256]{2,1,0:T(8,128)S(1)}, u32[]{:S(2)}, u32[]{:S(2)}) collective-permute-start(f32[2,256,256]{2,1,0:T(8,128)S(1)} %broadcast_select_fusion.6), channel_id=1, source_target_pairs={{0,2},{1,3},{2,0},{3,1},{4,6},{5,7},{6,4},{7,5},{10,8},{11,9},{12,... | collective-permute-start | bytes 1572872 | tf_op jit(solution)/shard_map/ppermute | solution.py:322
  3.9 18.5 %collective-permute-start = (f32[2,256,256]{2,1,0:T(8,128)S(1)}, f32[2,256,256]{2,1,0:T(8,128)S(1)}, u32[]{:S(2)}, u32[]{:S(2)}) collective-permute-start(f32[2,256,256]{2,1,0:T(8,128)S(1)} %broadcast_select_fusion.6), channel_id=1, source_target_pairs={{0,22},{1,23},{16,17},{17,16},{18,19},{19,18},{22,0},{23,1},{24,25... | collective-permute-start | bytes 1572872 | tf_op jit(solution)/shard_map/ppermute | solution.py:322
  20.8 2.3 %collective-permute-start.4 = (f32[2,256,256]{2,1,0:T(8,128)S(1)}, f32[2,256,256]{2,1,0:T(8,128)}, u32[]{:S(2)}, u32[]{:S(2)}) collective-permute-start(f32[2,256,256]{2,1,0:T(8,128)S(1)} %collective-permute-done.3), channel_id=1, source_target_pairs={{18,22},{19,23},{22,18},{23,19},{26,30},{27,31},{30,26},{31,27}} | collective-permute-start | bytes 1572872 | tf_op jit(solution)/shard_map/ppermute | solution.py:322
  22.3 0.8 copy-start.2
  23.1 0.8 copy-start.1
  23.1 0.7 collective-permute-start.5
  25.0 12.7 %collective-permute-start.10 = (f32[3,256,256]{2,1,0:T(8,128)}, f32[3,256,256]{2,1,0:T(8,128)}, u32[]{:S(2)}, u32[]{:S(2)}) collective-permute-start(f32[3,256,256]{2,1,0:T(8,128)} %pad_maximum_fusion.1), channel_id=1, source_target_pairs={{2,18},{3,19},{18,2},{19,3}} | collective-permute-start | bytes 2359304 | tf_op jit(solution)/shard_map/ppermute | solution.py:322
  26.6 19.8 %collective-permute-start.9 = (f32[2,256,256]{2,1,0:T(8,128)S(1)}, f32[2,256,256]{2,1,0:T(8,128)}, u32[]{:S(2)}, u32[]{:S(2)}) collective-permute-start(f32[2,256,256]{2,1,0:T(8,128)S(1)} %collective-permute-done.3), channel_id=1, source_target_pairs={{18,20},{19,21},{20,18},{21,19},{26,28},{27,29},{28,26},{29,27}} | collective-permute-start | bytes 1572872 | tf_op jit(solution)/shard_map/ppermute | solution.py:322
  46.4 6.9 %collective-permute-start.11 = (f32[3,256,256]{2,1,0:T(8,128)S(1)}, f32[3,256,256]{2,1,0:T(8,128)S(1)}, u32[]{:S(2)}, u32[]{:S(2)}) collective-permute-start(f32[3,256,256]{2,1,0:T(8,128)S(1)} %broadcast_select_fusion.a_ref), channel_id=1, source_target_pairs={{0,8},{1,9},{2,10},{3,11},{4,12},{5,13},{6,14},{7,15},{8,0},{9,1},... | collective-permute-start | bytes 2359304 | tf_op jit(solution)/shard_map/ppermute | solution.py:322
  50.6 9.0 %collective-permute-start.12 = (f32[2,256,256]{2,1,0:T(8,128)S(1)}, f32[2,256,256]{2,1,0:T(8,128)S(1)}, u32[]{:S(2)}, u32[]{:S(2)}) collective-permute-start(f32[2,256,256]{2,1,0:T(8,128)S(1)} %collective-permute-done.1.refs_4_), channel_id=1, source_target_pairs={{0,16},{1,17},{8,24},{9,25},{16,0},{17,1},{24,8},{25,9}} | collective-permute-start | bytes 1572872 | tf_op jit(solution)/shard_map/ppermute | solution.py:322
  51.3 16.1 %collective-permute-start.8 = (f32[2,256,256]{2,1,0:T(8,128)S(1)}, f32[2,256,256]{2,1,0:T(8,128)S(1)}, u32[]{:S(2)}, u32[]{:S(2)}) collective-permute-start(f32[2,256,256]{2,1,0:T(8,128)S(1)} %collective-permute-done.1.refs_4_), channel_id=1, source_target_pairs={{4,20},{5,21},{6,22},{7,23},{12,28},{13,29},{14,30},{15,31},{20,4}... | collective-permute-start | bytes 1572872 | tf_op jit(solution)/shard_map/ppermute | solution.py:322
  59.6 5.7 %copy-start.3 = (f32[2,256,256]{2,1,0:T(8,128)S(1)}, f32[2,256,256]{2,1,0:T(8,128)}, u32[]{:S(2)}) copy-start(f32[2,256,256]{2,1,0:T(8,128)} %copy-done.2) | copy-start | bytes 1572868
  61.1 16.5 %collective-permute-start.13 = (f32[2,256,256]{2,1,0:T(8,128)S(1)}, f32[2,256,256]{2,1,0:T(8,128)S(1)}, u32[]{:S(2)}, u32[]{:S(2)}) collective-permute-start(f32[2,256,256]{2,1,0:T(8,128)S(1)} %get-tuple-element.45), channel_id=1, source_target_pairs={{0,1},{1,0},{2,3},{3,2},{8,9},{9,8},{10,11},{11,10},{16,17},{17,16... | collective-permute-start | bytes 1572872 | tf_op jit(solution)/shard_map/ppermute | solution.py:322
  65.3 15.1 %collective-permute-start.7 = (f32[2,256,256]{2,1,0:T(8,128)S(1)}, f32[2,256,256]{2,1,0:T(8,128)S(1)}, u32[]{:S(2)}, u32[]{:S(2)}) collective-permute-start(f32[2,256,256]{2,1,0:T(8,128)S(1)} %copy-done.3), channel_id=1, source_target_pairs={{4,20},{5,21},{6,22},{7,23},{12,28},{13,29},{14,30},{15,31},{20,4}... | collective-permute-start | bytes 1572872 | tf_op jit(solution)/shard_map/ppermute | solution.py:322
  77.6 2.8 %collective-permute-start.14 = (f32[2,256,256]{2,1,0:T(8,128)S(1)}, f32[2,256,256]{2,1,0:T(8,128)S(1)}, u32[]{:S(2)}, u32[]{:S(2)}) collective-permute-start(f32[2,256,256]{2,1,0:T(8,128)S(1)} %get-tuple-element.43.a_ref), channel_id=1, source_target_pairs={{0,8},{1,9},{2,10},{3,11},{4,12},{5,13},{6,14},{7,15},{8,0},{9,1},... | collective-permute-start | bytes 1572872 | tf_op jit(solution)/shard_map/ppermute | solution.py:322
  78.3 2.3 %collective-permute-start.15 = (f32[2,256,256]{2,1,0:T(8,128)S(1)}, f32[2,256,256]{2,1,0:T(8,128)S(1)}, u32[]{:S(2)}, u32[]{:S(2)}) collective-permute-start(f32[2,256,256]{2,1,0:T(8,128)S(1)} %get-tuple-element.33.a_ref), channel_id=1, source_target_pairs={{0,8},{1,9},{2,10},{3,11},{4,12},{5,13},{6,14},{7,15},{8,0},{9,1},... | collective-permute-start | bytes 1572872 | tf_op jit(solution)/shard_map/ppermute | solution.py:322
  78.4 14.9 %collective-permute-start.6 = (f32[2,256,256]{2,1,0:T(8,128)S(1)}, f32[2,256,256]{2,1,0:T(8,128)S(1)}, u32[]{:S(2)}, u32[]{:S(2)}) collective-permute-start(f32[2,256,256]{2,1,0:T(8,128)S(1)} %get-tuple-element.46), channel_id=1, source_target_pairs={{4,20},{5,21},{6,22},{7,23},{12,28},{13,29},{14,30},{15,31},{16,17... | collective-permute-start | bytes 1572872 | tf_op jit(solution)/shard_map/ppermute | solution.py:322
  93.5 11.9 %copy-start = (f32[512,256]{1,0:T(8,128)S(1)}, f32[512,256]{1,0:T(8,128)}, u32[]{:S(2)}) copy-start(f32[512,256]{1,0:T(8,128)} %refs_1_.1) | copy-start | bytes 1572868
  93.5 11.8 %collective-permute-start.16 = (f32[4,2,256,256]{3,2,1,0:T(8,128)S(1)}, f32[4,2,256,256]{3,2,1,0:T(8,128)S(1)}, u32[]{:S(2)}, u32[]{:S(2)}) collective-permute-start(f32[4,2,256,256]{3,2,1,0:T(8,128)S(1)} %pad_maximum_fusion.refs_6_), channel_id=1, source_target_pairs={{20,28},{21,29},{22,30},{23,31},{28,20},{29,21},{30,22},{31,23}} | collective-permute-start | bytes 6291464 | tf_op jit(solution)/shard_map/ppermute | solution.py:322

commit v4 on v3

--- a/solution.py
+++ b/solution.py
@@ -165,9 +165,10 @@
     return factor, (invs + [inv], rights + [right])
 
 
-def solve_rows(take, rows, extra, inv_refs, right_refs, left, right, factor_rows, width):
+def solve_rows(take, rows, last, inv_refs, right_refs, left, right, factor_rows, width):
     w = width
-    for k in range(SNODES):
+
+    def step(k):
         rest = take(k)
         if k > 0:
             rest = rest - dot_t(left[:, : 3 * w * k], right_refs[k][:, : 3 * w * k])
@@ -176,6 +177,9 @@
         right[:, 3 * w * k : 3 * w * (k + 1)] = as_right(row[rows:])
         factor_rows(k, row[:rows])
 
+    for k in range(SNODES):
+        pl.when(last >= k)(functools.partial(step, k))
+
 
 def write_tile(pos_ref, take, tile_ref, inv_refs, right_refs, factor_refs, out_ref, left, right, width):
     row_index, col_index = pos_ref[0], pos_ref[1]
@@ -191,7 +195,7 @@
             def _():
                 out_ref[...] = value
 
-        solve_rows(take, rows, width, inv_refs, right_refs, left, right, factor_rows, width)
+        solve_rows(take, rows, col_index, inv_refs, right_refs, left, right, factor_rows, width)
 
         @pl.when(col_index >= SNODES)
         def _():
@@ -360,9 +364,8 @@
     schur, corner = (r >= 2) & (c >= 4), (r < 2) & (c >= 4)
     q = jnp.where(r < 2, blocks.transpose(0, 2, 1), blocks)
 
-    beside = [((r, c), (r, c + 1)) for r in (0, 1) for c in (4, 6)]
     below = [((r, c), (r, c + 1)) for r in (2, 3) for c in (0, 2)]
-    hop = swap(q, chosen([((0, 0), (2, 4)), ((0, 1), (2, 5))] + beside))
+    hop = swap(q, chosen([((0, 0), (2, 4)), ((0, 1), (2, 5))]))
     hop_far = swap(q, chosen([((0, 0), (2, 6)), ((0, 1), (2, 7))] + below))
     zq = swap(q, lambda r, c: z_pair(r, c) if (r < 2 or c < 4) and not (r == 1 and c < 2) else (r, c))
     xq = swap(q, x_pair)
@@ -371,7 +374,7 @@
     to_schur = some(x_pair, lambda r, c: c >= 4)
     near_z = swap(zq, some(x_pair, lambda r, c: c < 2))
     xz = swap(zq, to_schur)
-    xy = swap(hop, to_schur)
+    xy = swap(xq, some(y_pair, lambda r, c: r >= 2 and c >= 4))
 
     def held(on_near, on_far):
         return jnp.where(near, on_near, on_far)
@@ -405,13 +408,13 @@
     )
     yg = swap(g, some(y_pair, lambda r, c: r >= 2 or c < 4))
     factor, state = chain_call(
-        functools.partial(chain_early, 1, width), 1, width, [pos, after(n, g, xz), n_other], [SMEM, VMEM, VMEM], state
+        functools.partial(chain_early, 1, width), 1, width, [pos, after(n, g, xz, xy), n_other], [SMEM, VMEM, VMEM], state
     )
     factors.append(factor)
     yg = after(yg, factor)
     g2, g3 = jnp.where(even, g, yg), jnp.where(even, yg, g)
     g2_other, g3_other = swap(g2, core_pair), swap(g3, core_pair)
-    g2 = after(g2, xy, g3_other)
+    g2 = after(g2, cross, g3_other)
     factor, state = chain_call(
         functools.partial(chain_later, 2, width), 2, width, [pos, g2, g2_other], [SMEM, VMEM, VMEM], state
     )

time: 115 us -> 114 us (level)
  starting transfers between devices: 36.2 us -> 37.6 us
  waiting for transfers between devices: 33.8 us -> 32.5 us
    ppermute x17, starting transfers between devices: 36.2 us -> 37.6 us  [swap(): return lax.ppermute(x, ('row', 'col'), perm)]
    ppermute x17, waiting for transfers between devices: 33.8 us -> 32.5 us  [swap(): return lax.ppermute(x, ('row', 'col'), perm)]
    pallas_call x1, Pallas kernels: 9.26 us -> 8.07 us  [box_mesh(): pl.pallas_call(functools.partial(box_tile, width), out_shape=jax.ShapeDty...]
  transfers between devices with their start and end apart: 17 -> 17, of which waited for: 6 -> 6; matrix products, arithmetic and copies ran while one was open for 2% -> 2% of each run, Pallas kernels for 25% -> 19%
where the time goes in v4:
time: 114 us; the launch traced here: 113 us
  starting transfers between devices  37.6 us (33%)
  Pallas kernels  37.2 us (33%)
  waiting for transfers between devices  32.5 us (29%)
  other arithmetic  4.21 us (4%)
  local copies, waits for them, and re-layouts  1.3 us (1%)
    ppermute x17, starting transfers between devices, swap(): return lax.ppermute(x, ('row', 'col'), perm)  37.6 us
    ppermute x17, waiting for transfers between devices, swap(): return lax.ppermute(x, ('row', 'col'), perm)  32.5 us
    pallas_call x4, Pallas kernels, chain_call(): pl.pallas_call(kernel, out_shape=[jax.ShapeDtypeStruct((width, (k + 1) *...  29.1 us
    pallas_call x1, Pallas kernels, box_mesh(): pl.pallas_call(functools.partial(box_tile, width), out_shape=jax.ShapeDty...  8.07 us
  transfers between devices with their start and end apart: 17, of which 6 were waited for; matrix products, arithmetic and copies ran while one was open for 2% of the time, Pallas kernels for 19%

profile of v4, /device:TPU:19, one launch (start us, length us, event | category | flops | bytes accessed | tf_op | source)
XLA Modules:
  0.0 113.1 jit_solution(11879016499314197479)
XLA Ops:
  0.0 1.2 %copy.2 = f32[2,256,256]{2,1,0:T(8,128)S(1)} copy(f32[2,256,256]{1,2,0:T(8,128)} %bitcast.9) | data formatting | bytes 1048576 | tf_op jit(solution)/shard_map/transpose | solution.py:365
  1.2 1.1 broadcast_select_fusion.6
  2.4 0.1 collective-permute-start.3
  2.4 0.7 collective-permute-start.2
  3.1 0.7 collective-permute-start.1
  3.9 0.7 collective-permute-start
  4.6 16.3 %collective-permute-done.3 = f32[2,256,256]{2,1,0:T(8,128)S(1)} collective-permute-done((f32[2,256,256]{2,1,0:T(8,128)S(1)}, f32[2,256,256]{2,1,0:T(8,128)S(1)}, u32[]{:S(2)}, u32[]{:S(2)}) %collective-permute-start.3) | collective-permute-done | bytes 524320 | tf_op jit(solution)/shard_map/ppermute | solution.py:326
  20.8 1.5 %collective-permute-start.4 = (f32[2,256,256]{2,1,0:T(8,128)S(1)}, f32[2,256,256]{2,1,0:T(8,128)}, u32[]{:S(2)}, u32[]{:S(2)}) collective-permute-start(f32[2,256,256]{2,1,0:T(8,128)S(1)} %collective-permute-done.3), channel_id=1, source_target_pairs={{18,22},{19,23},{22,18},{23,19},{26,30},{27,31},{30,26},{31,27}} | collective-permute-start | bytes 1572872 | tf_op jit(solution)/shard_map/ppermute | solution.py:326
  22.3 0.0 collective-permute-done.2
  22.3 0.0 collective-permute-done.1.refs_4_
  22.3 0.0 collective-permute-done.refs_3_
  22.3 0.2 select_select_fusion.1
  22.5 0.0 copy-start.1
  22.5 0.7 collective-permute-start.5
  23.2 0.0 collective-permute-done.5
  23.2 0.0 copy-done.1
  23.3 0.1 broadcast_select_fusion.3
  23.4 0.9 pad_maximum_fusion.1
  24.4 1.6 %collective-permute-start.10 = (f32[3,256,256]{2,1,0:T(8,128)}, f32[3,256,256]{2,1,0:T(8,128)}, u32[]{:S(2)}, u32[]{:S(2)}) collective-permute-start(f32[3,256,256]{2,1,0:T(8,128)} %pad_maximum_fusion.1), channel_id=1, source_target_pairs={{2,18},{3,19},{18,2},{19,3}} | collective-permute-start | bytes 2359304 | tf_op jit(solution)/shard_map/ppermute | solution.py:326
  25.9 11.6 %collective-permute-start.9 = (f32[2,256,256]{2,1,0:T(8,128)S(1)}, f32[2,256,256]{2,1,0:T(8,128)}, u32[]{:S(2)}, u32[]{:S(2)}) collective-permute-start(f32[2,256,256]{2,1,0:T(8,128)S(1)} %collective-permute-done.3), channel_id=1, source_target_pairs={{18,20},{19,21},{20,18},{21,19},{26,28},{27,29},{28,26},{29,27}} | collective-permute-start | bytes 1572872 | tf_op jit(solution)/shard_map/ppermute | solution.py:326
  37.6 0.0 collective-permute-done.10
  37.6 0.1 broadcast_select_fusion.a_ref
  37.7 9.1 %collective-permute-done.9 = f32[2,256,256]{2,1,0:T(8,128)} collective-permute-done((f32[2,256,256]{2,1,0:T(8,128)S(1)}, f32[2,256,256]{2,1,0:T(8,128)}, u32[]{:S(2)}, u32[]{:S(2)}) %collective-permute-start.9) | collective-permute-done | bytes 524320 | tf_op jit(solution)/shard_map/ppermute | solution.py:326
  46.8 3.7 %collective-permute-start.11 = (f32[3,256,256]{2,1,0:T(8,128)S(1)}, f32[3,256,256]{2,1,0:T(8,128)S(1)}, u32[]{:S(2)}, u32[]{:S(2)}) collective-permute-start(f32[3,256,256]{2,1,0:T(8,128)S(1)} %broadcast_select_fusion.a_ref), channel_id=1, source_target_pairs={{0,8},{1,9},{2,10},{3,11},{4,12},{5,13},{6,14},{7,15},{8,0},{9,1},... | collective-permute-start | bytes 2359304 | tf_op jit(solution)/shard_map/ppermute | solution.py:326
  50.5 0.7 collective-permute-start.12
  51.2 0.1 pad_add_fusion.pos_ref.refs_0_
  51.3 4.2 %collective-permute-start.7 = (f32[2,256,256]{2,1,0:T(8,128)S(1)}, f32[2,256,256]{2,1,0:T(8,128)S(1)}, u32[]{:S(2)}, u32[]{:S(2)}) collective-permute-start(f32[2,256,256]{2,1,0:T(8,128)S(1)} %collective-permute-done.3), channel_id=1, source_target_pairs={{20,21},{21,20},{22,23},{23,22},{28,29},{29,28},{30,31},{31,30}} | collective-permute-start | bytes 1572872 | tf_op jit(solution)/shard_map/ppermute | solution.py:326
  55.5 1.9 %collective-permute-start.8 = (f32[2,256,256]{2,1,0:T(8,128)S(1)}, f32[2,256,256]{2,1,0:T(8,128)S(1)}, u32[]{:S(2)}, u32[]{:S(2)}) collective-permute-start(f32[2,256,256]{2,1,0:T(8,128)S(1)} %collective-permute-done.1.refs_4_), channel_id=1, source_target_pairs={{4,20},{5,21},{6,22},{7,23},{12,28},{13,29},{14,30},{15,31},{20,4}... | collective-permute-start | bytes 1572872 | tf_op jit(solution)/shard_map/ppermute | solution.py:326
  57.4 6.3 %chain0.1 = (f32[256,256]{1,0:T(8,128)S(1)}, bf16[256,768]{1,0:T(8,128)(2,1)S(1)}, bf16[256,768]{1,0:T(8,128)(2,1)S(1)}) custom-call(s32[2]{0:T(128)S(1)} %pad_add_fusion.pos_ref.refs_0_, f32[3,256,256]{2,1,0:T(8,128)S(1)} %broadcast_select_fusion.a_ref, f32[3,256,256]{2,1,0:T(8,128)S(1)} %collective-permute-done.11.b_ref), custom_call_target="tpu_custom_call" | custom-call | flops 1000 | bytes 1024 | tf_op jit(solution)/shard_map/chain0/pallas_call | solution.py:151
  63.7 1.5 %select_select_fusion = (f32[2,256,256]{2,1,0:T(8,128)S(1)}, f32[2,256,256]{2,1,0:T(8,128)S(1)}) fusion(f32[2,256,256]{2,1,0:T(8,128)} %collective-permute-done.4, f32[2,256,256]{2,1,0:T(8,128)} %collective-permute-done.9, f32[2,256,256]{2,1,0:T(8,128)S(1)} %collective-permute-done.1.refs_4_, f32[2,256,256]{2,1,0:T(8,128)S(1)} %collective-permute-done.12, ...), kind=kLoop, calls=%fused_computation.2 | loop fusion | flops 786432 | bytes 4718596 | tf_op jit(solution)/shard_map/jit(_where)/select_n | solution.py:380
  65.2 1.9 %collective-permute-start.13 = (f32[2,256,256]{2,1,0:T(8,128)S(1)}, f32[2,256,256]{2,1,0:T(8,128)S(1)}, u32[]{:S(2)}, u32[]{:S(2)}) collective-permute-start(f32[2,256,256]{2,1,0:T(8,128)S(1)} %get-tuple-element.45), channel_id=1, source_target_pairs={{0,1},{1,0},{2,3},{3,2},{8,9},{9,8},{10,11},{11,10},{16,17},{17,16... | collective-permute-start | bytes 1572872 | tf_op jit(solution)/shard_map/ppermute | solution.py:326
  67.1 0.7 collective-permute-done.7
  67.8 2.8 %collective-permute-done.8 = f32[2,256,256]{2,1,0:T(8,128)S(1)} collective-permute-done((f32[2,256,256]{2,1,0:T(8,128)S(1)}, f32[2,256,256]{2,1,0:T(8,128)S(1)}, u32[]{:S(2)}, u32[]{:S(2)}) %collective-permute-start.8) | collective-permute-done | bytes 524320 | tf_op jit(solution)/shard_map/ppermute | solution.py:326
  70.6 2.4 %collective-permute-start.6 = (f32[2,256,256]{2,1,0:T(8,128)S(1)}, f32[2,256,256]{2,1,0:T(8,128)S(1)}, u32[]{:S(2)}, u32[]{:S(2)}) collective-permute-start(f32[2,256,256]{2,1,0:T(8,128)S(1)} %get-tuple-element.46), channel_id=1, source_target_pairs={{4,20},{5,21},{6,22},{7,23},{12,28},{13,29},{14,30},{15,31},{16,17... | collective-permute-start | bytes 1572872 | tf_op jit(solution)/shard_map/ppermute | solution.py:326
  73.0 6.9 %chain1.1 = (f32[256,512]{1,0:T(8,128)S(1)}, bf16[256,768]{1,0:T(8,128)(2,1)S(1)}, bf16[256,768]{1,0:T(8,128)(2,1)S(1)}) custom-call(s32[2]{0:T(128)S(1)} %pad_add_fusion.pos_ref.refs_0_, f32[3,256,256]{2,1,0:T(8,128)S(1)} %broadcast_select_fusion.a_ref, f32[3,256,256]{2,1,0:T(8,128)S(1)} %collective-permute-done.11.b_ref, ...), custom_call_target="tpu_custom_call" | custom-call | flops 1000 | bytes 1024 | tf_op jit(solution)/shard_map/chain1/pallas_call | solution.py:151
  79.9 0.4 collective-permute-done.13
  80.3 0.1 broadcast_select_fusion.1
  80.4 1.2 %collective-permute-start.14 = (f32[2,256,256]{2,1,0:T(8,128)S(1)}, f32[2,256,256]{2,1,0:T(8,128)S(1)}, u32[]{:S(2)}, u32[]{:S(2)}) collective-permute-start(f32[2,256,256]{2,1,0:T(8,128)S(1)} %get-tuple-element.43.a_ref), channel_id=1, source_target_pairs={{0,8},{1,9},{2,10},{3,11},{4,12},{5,13},{6,14},{7,15},{8,0},{9,1},... | collective-permute-start | bytes 1572872 | tf_op jit(solution)/shard_map/ppermute | solution.py:326
  81.5 0.1 collective-permute-start.15
  81.6 3.2 %collective-permute-done.6.refs_5_ = f32[2,256,256]{2,1,0:T(8,128)S(1)} collective-permute-done((f32[2,256,256]{2,1,0:T(8,128)S(1)}, f32[2,256,256]{2,1,0:T(8,128)S(1)}, u32[]{:S(2)}, u32[]{:S(2)}) %collective-permute-start.6) | collective-permute-done | bytes 524320 | tf_op jit(solution)/shard_map/ppermute | solution.py:326
  84.8 0.0 collective-permute-done.14.b_ref
  84.8 0.0 collective-permute-done.15.b_ref
  84.8 7.7 %chain2.1 = (f32[256,768]{1,0:T(8,128)S(1)}, bf16[256,768]{1,0:T(8,128)(2,1)S(1)}, bf16[256,1536]{1,0:T(8,128)(2,1)S(1)}) custom-call(s32[2]{0:T(128)S(1)} %pad_add_fusion.pos_ref.refs_0_, f32[2,256,256]{2,1,0:T(8,128)S(1)} %get-tuple-element.33.a_ref, f32[2,256,256]{2,1,0:T(8,128)S(1)} %collective-permute-done.15.b_ref, ...), custom_call_target="tpu_custom_call" | custom-call | flops 1000 | bytes 1024 | tf_op jit(solution)/shard_map/chain2/pallas_call | solution.py:151
  92.5 0.2 pad_maximum_fusion.refs_6_
  92.6 0.0 copy-start
  92.7 4.1 %collective-permute-start.16 = (f32[4,2,256,256]{3,2,1,0:T(8,128)S(1)}, f32[4,2,256,256]{3,2,1,0:T(8,128)S(1)}, u32[]{:S(2)}, u32[]{:S(2)}) collective-permute-start(f32[4,2,256,256]{3,2,1,0:T(8,128)S(1)} %pad_maximum_fusion.refs_6_), channel_id=1, source_target_pairs={{20,28},{21,29},{22,30},{23,31},{28,20},{29,21},{30,22},{31,23}} | collective-permute-start | bytes 6291464 | tf_op jit(solution)/shard_map/ppermute | solution.py:326
  96.7 8.3 %chain3.1 = (f32[256,1024]{1,0:T(8,128)S(1)}, bf16[256,768]{1,0:T(8,128)(2,1)S(1)}, bf16[256,2304]{1,0:T(8,128)(2,1)S(1)}) custom-call(s32[2]{0:T(128)S(1)} %pad_add_fusion.pos_ref.refs_0_, f32[2,256,256]{2,1,0:T(8,128)S(1)} %get-tuple-element.43.a_ref, f32[2,256,256]{2,1,0:T(8,128)S(1)} %collective-permute-done.14.b_ref, ...), custom_call_target="tpu_custom_call" | custom-call | flops 1000 | bytes 1024 | tf_op jit(solution)/shard_map/chain3/pallas_call | solution.py:151
  105.0 8.1 %tile.1 = f32[512,256]{1,0:T(8,128)} custom-call(s32[2]{0:T(128)S(1)} %pad_add_fusion.pos_ref.refs_0_, f32[512,256]{1,0:T(8,128)S(1)} %copy-done, f32[2,256,256]{2,1,0:T(8,128)S(1)} %bitcast.11, f32[2,256,256]{2,1,0:T(8,128)S(1)} %collective-permute-done.refs_3_, f32[2,256,256]{2,1,0:T(8,128)S(1)} %collective-permute-done.1.refs_4_, ...), custom_call_target="tpu_custom_call" | custom-call | flops 1000 | bytes 1024 | tf_op jit(solution)/shard_map/tile/pallas_call | solution.py:431
  (6 shorter events, 0.0 us)
Async XLA Ops:
  2.4 18.5 %collective-permute-start.3 = (f32[2,256,256]{2,1,0:T(8,128)S(1)}, f32[2,256,256]{2,1,0:T(8,128)S(1)}, u32[]{:S(2)}, u32[]{:S(2)}) collective-permute-start(f32[2,256,256]{2,1,0:T(8,128)S(1)} %broadcast_select_fusion.6), channel_id=1, source_target_pairs={{0,16},{1,17},{2,18},{3,19},{4,20},{5,21},{6,22},{7,23},{8,24},{9,... | collective-permute-start | bytes 1572872 | tf_op jit(solution)/shard_map/ppermute | solution.py:326
  2.4 19.9 %collective-permute-start.2 = (f32[2,256,256]{2,1,0:T(8,128)S(1)}, f32[2,256,256]{2,1,0:T(8,128)S(1)}, u32[]{:S(2)}, u32[]{:S(2)}) collective-permute-start(f32[2,256,256]{2,1,0:T(8,128)S(1)} %broadcast_select_fusion.6), channel_id=1, source_target_pairs={{0,20},{1,21},{20,0},{21,1}} | collective-permute-start | bytes 1572872 | tf_op jit(solution)/shard_map/ppermute | solution.py:326
  3.1 19.2 %collective-permute-start.1 = (f32[2,256,256]{2,1,0:T(8,128)S(1)}, f32[2,256,256]{2,1,0:T(8,128)S(1)}, u32[]{:S(2)}, u32[]{:S(2)}) collective-permute-start(f32[2,256,256]{2,1,0:T(8,128)S(1)} %broadcast_select_fusion.6), channel_id=1, source_target_pairs={{0,2},{1,3},{2,0},{3,1},{4,6},{5,7},{6,4},{7,5},{10,8},{11,9},{12,... | collective-permute-start | bytes 1572872 | tf_op jit(solution)/shard_map/ppermute | solution.py:326
  3.9 18.5 %collective-permute-start = (f32[2,256,256]{2,1,0:T(8,128)S(1)}, f32[2,256,256]{2,1,0:T(8,128)S(1)}, u32[]{:S(2)}, u32[]{:S(2)}) collective-permute-start(f32[2,256,256]{2,1,0:T(8,128)S(1)} %broadcast_select_fusion.6), channel_id=1, source_target_pairs={{0,22},{1,23},{16,17},{17,16},{18,19},{19,18},{22,0},{23,1},{24,25... | collective-permute-start | bytes 1572872 | tf_op jit(solution)/shard_map/ppermute | solution.py:326
  20.8 1.7 %collective-permute-start.4 = (f32[2,256,256]{2,1,0:T(8,128)S(1)}, f32[2,256,256]{2,1,0:T(8,128)}, u32[]{:S(2)}, u32[]{:S(2)}) collective-permute-start(f32[2,256,256]{2,1,0:T(8,128)S(1)} %collective-permute-done.3), channel_id=1, source_target_pairs={{18,22},{19,23},{22,18},{23,19},{26,30},{27,31},{30,26},{31,27}} | collective-permute-start | bytes 1572872 | tf_op jit(solution)/shard_map/ppermute | solution.py:326
  22.5 0.8 copy-start.1
  22.5 0.7 collective-permute-start.5
  24.4 13.2 %collective-permute-start.10 = (f32[3,256,256]{2,1,0:T(8,128)}, f32[3,256,256]{2,1,0:T(8,128)}, u32[]{:S(2)}, u32[]{:S(2)}) collective-permute-start(f32[3,256,256]{2,1,0:T(8,128)} %pad_maximum_fusion.1), channel_id=1, source_target_pairs={{2,18},{3,19},{18,2},{19,3}} | collective-permute-start | bytes 2359304 | tf_op jit(solution)/shard_map/ppermute | solution.py:326
  25.9 20.9 %collective-permute-start.9 = (f32[2,256,256]{2,1,0:T(8,128)S(1)}, f32[2,256,256]{2,1,0:T(8,128)}, u32[]{:S(2)}, u32[]{:S(2)}) collective-permute-start(f32[2,256,256]{2,1,0:T(8,128)S(1)} %collective-permute-done.3), channel_id=1, source_target_pairs={{18,20},{19,21},{20,18},{21,19},{26,28},{27,29},{28,26},{29,27}} | collective-permute-start | bytes 1572872 | tf_op jit(solution)/shard_map/ppermute | solution.py:326
  46.8 10.6 %collective-permute-start.11 = (f32[3,256,256]{2,1,0:T(8,128)S(1)}, f32[3,256,256]{2,1,0:T(8,128)S(1)}, u32[]{:S(2)}, u32[]{:S(2)}) collective-permute-start(f32[3,256,256]{2,1,0:T(8,128)S(1)} %broadcast_select_fusion.a_ref), channel_id=1, source_target_pairs={{0,8},{1,9},{2,10},{3,11},{4,12},{5,13},{6,14},{7,15},{8,0},{9,1},... | collective-permute-start | bytes 2359304 | tf_op jit(solution)/shard_map/ppermute | solution.py:326
  50.5 13.2 %collective-permute-start.12 = (f32[2,256,256]{2,1,0:T(8,128)S(1)}, f32[2,256,256]{2,1,0:T(8,128)S(1)}, u32[]{:S(2)}, u32[]{:S(2)}) collective-permute-start(f32[2,256,256]{2,1,0:T(8,128)S(1)} %collective-permute-done.1.refs_4_), channel_id=1, source_target_pairs={{0,16},{1,17},{8,24},{9,25},{16,0},{17,1},{24,8},{25,9}} | collective-permute-start | bytes 1572872 | tf_op jit(solution)/shard_map/ppermute | solution.py:326
  51.3 16.5 %collective-permute-start.7 = (f32[2,256,256]{2,1,0:T(8,128)S(1)}, f32[2,256,256]{2,1,0:T(8,128)S(1)}, u32[]{:S(2)}, u32[]{:S(2)}) collective-permute-start(f32[2,256,256]{2,1,0:T(8,128)S(1)} %collective-permute-done.3), channel_id=1, source_target_pairs={{20,21},{21,20},{22,23},{23,22},{28,29},{29,28},{30,31},{31,30}} | collective-permute-start | bytes 1572872 | tf_op jit(solution)/shard_map/ppermute | solution.py:326
  55.5 15.1 %collective-permute-start.8 = (f32[2,256,256]{2,1,0:T(8,128)S(1)}, f32[2,256,256]{2,1,0:T(8,128)S(1)}, u32[]{:S(2)}, u32[]{:S(2)}) collective-permute-start(f32[2,256,256]{2,1,0:T(8,128)S(1)} %collective-permute-done.1.refs_4_), channel_id=1, source_target_pairs={{4,20},{5,21},{6,22},{7,23},{12,28},{13,29},{14,30},{15,31},{20,4}... | collective-permute-start | bytes 1572872 | tf_op jit(solution)/shard_map/ppermute | solution.py:326
  65.2 15.1 %collective-permute-start.13 = (f32[2,256,256]{2,1,0:T(8,128)S(1)}, f32[2,256,256]{2,1,0:T(8,128)S(1)}, u32[]{:S(2)}, u32[]{:S(2)}) collective-permute-start(f32[2,256,256]{2,1,0:T(8,128)S(1)} %get-tuple-element.45), channel_id=1, source_target_pairs={{0,1},{1,0},{2,3},{3,2},{8,9},{9,8},{10,11},{11,10},{16,17},{17,16... | collective-permute-start | bytes 1572872 | tf_op jit(solution)/shard_map/ppermute | solution.py:326
  70.6 14.2 %collective-permute-start.6 = (f32[2,256,256]{2,1,0:T(8,128)S(1)}, f32[2,256,256]{2,1,0:T(8,128)S(1)}, u32[]{:S(2)}, u32[]{:S(2)}) collective-permute-start(f32[2,256,256]{2,1,0:T(8,128)S(1)} %get-tuple-element.46), channel_id=1, source_target_pairs={{4,20},{5,21},{6,22},{7,23},{12,28},{13,29},{14,30},{15,31},{16,17... | collective-permute-start | bytes 1572872 | tf_op jit(solution)/shard_map/ppermute | solution.py:326
  80.4 4.4 %collective-permute-start.14 = (f32[2,256,256]{2,1,0:T(8,128)S(1)}, f32[2,256,256]{2,1,0:T(8,128)S(1)}, u32[]{:S(2)}, u32[]{:S(2)}) collective-permute-start(f32[2,256,256]{2,1,0:T(8,128)S(1)} %get-tuple-element.43.a_ref), channel_id=1, source_target_pairs={{0,8},{1,9},{2,10},{3,11},{4,12},{5,13},{6,14},{7,15},{8,0},{9,1},... | collective-permute-start | bytes 1572872 | tf_op jit(solution)/shard_map/ppermute | solution.py:326
  81.5 3.3 %collective-permute-start.15 = (f32[2,256,256]{2,1,0:T(8,128)S(1)}, f32[2,256,256]{2,1,0:T(8,128)S(1)}, u32[]{:S(2)}, u32[]{:S(2)}) collective-permute-start(f32[2,256,256]{2,1,0:T(8,128)S(1)} %get-tuple-element.33.a_ref), channel_id=1, source_target_pairs={{0,8},{1,9},{2,10},{3,11},{4,12},{5,13},{6,14},{7,15},{8,0},{9,1},... | collective-permute-start | bytes 1572872 | tf_op jit(solution)/shard_map/ppermute | solution.py:326
  92.6 12.4 %copy-start = (f32[512,256]{1,0:T(8,128)S(1)}, f32[512,256]{1,0:T(8,128)}, u32[]{:S(2)}) copy-start(f32[512,256]{1,0:T(8,128)} %refs_1_.1) | copy-start | bytes 1572868
  92.7 12.4 %collective-permute-start.16 = (f32[4,2,256,256]{3,2,1,0:T(8,128)S(1)}, f32[4,2,256,256]{3,2,1,0:T(8,128)S(1)}, u32[]{:S(2)}, u32[]{:S(2)}) collective-permute-start(f32[4,2,256,256]{3,2,1,0:T(8,128)S(1)} %pad_maximum_fusion.refs_6_), channel_id=1, source_target_pairs={{20,28},{21,29},{22,30},{23,31},{28,20},{29,21},{30,22},{31,23}} | collective-permute-start | bytes 6291464 | tf_op jit(solution)/shard_map/ppermute | solution.py:326

commit v5 on v4

--- a/solution.py
+++ b/solution.py
@@ -350,6 +350,12 @@
     return lambda r, c: pair(r, c) if members(r, c) else (r, c)
 
 
+def turn_blocks(pos_ref, block_ref, out_ref):
+    top = pos_ref[0] < 2
+    for b in range(2):
+        out_ref[b] = jnp.where(top, block_ref[b].T, block_ref[b])
+
+
 def chosen(pairs):
     table = {a: b for p, q in pairs for a, b in ((p, q), (q, p))}
     return lambda r, c: table.get((r, c), (r, c))
@@ -362,7 +368,15 @@
     blocks = stiffness.reshape(2, width, width)
     even, near = c % 2 == 0, (c // 2) % 2 == 0
     schur, corner = (r >= 2) & (c >= 4), (r < 2) & (c >= 4)
-    q = jnp.where(r < 2, blocks.transpose(0, 2, 1), blocks)
+    q = pl.pallas_call(
+        turn_blocks,
+        out_shape=jax.ShapeDtypeStruct(blocks.shape, f32),
+        in_specs=[SMEM, VMEM],
+        out_specs=VMEM,
+        compiler_params=PARAMS,
+        cost_estimate=COST,
+        name="turn",
+    )(pos, blocks)
 
     below = [((r, c), (r, c + 1)) for r in (2, 3) for c in (0, 2)]
     hop = swap(q, chosen([((0, 0), (2, 4)), ((0, 1), (2, 5))]))

time: 114 us -> 113 us (level)
    transpose x1 -> x0, local copies, waits for them, and re-layouts: 1.24 us -> none  [box_mesh(): q = jnp.where(r < 2, blocks.transpose(0, 2, 1), blocks)]
where the time goes in v5:
time: 113 us
  starting transfers between devices  38.4 us (34%)
  Pallas kernels  37.9 us (34%)
  waiting for transfers between devices  31.7 us (28%)
  other arithmetic  3.19 us (3%)
    ppermute x17, starting transfers between devices, swap(): return lax.ppermute(x, ('row', 'col'), perm)  38.4 us
    ppermute x17, waiting for transfers between devices, swap(): return lax.ppermute(x, ('row', 'col'), perm)  31.7 us
    pallas_call x4, Pallas kernels, chain_call(): pl.pallas_call(kernel, out_shape=[jax.ShapeDtypeStruct((width, (k + 1) *...  29.1 us
    pallas_call x1, Pallas kernels, box_mesh(): pl.pallas_call(functools.partial(box_tile, width), out_shape=jax.ShapeDty...  8.09 us
  transfers between devices with their start and end apart: 17, of which 6 were waited for; matrix products, arithmetic and copies ran while one was open for 2% of the time, Pallas kernels for 19%

profile of v5, /device:TPU:19, one launch (start us, length us, event | category | flops | bytes accessed | tf_op | source)
XLA Modules:
  0.0 112.6 jit_solution(5576614247698041689)
XLA Ops:
  0.0 0.1 pad_add_fusion.pos_ref.refs_0_
  0.1 1.0 copy-done
  1.1 0.7 turn.1
  1.9 0.3 collective-permute-start.3
  2.2 0.7 collective-permute-start.2
  2.9 0.7 collective-permute-start.1
  3.6 0.7 collective-permute-start
  4.3 16.1 %collective-permute-done.3 = f32[2,256,256]{2,1,0:T(8,128)S(1)} collective-permute-done((f32[2,256,256]{2,1,0:T(8,128)S(1)}, f32[2,256,256]{2,1,0:T(8,128)S(1)}, u32[]{:S(2)}, u32[]{:S(2)}) %collective-permute-start.3) | collective-permute-done | bytes 524320 | tf_op jit(solution)/shard_map/ppermute | solution.py:326
  20.3 1.5 %collective-permute-start.4 = (f32[2,256,256]{2,1,0:T(8,128)S(1)}, f32[2,256,256]{2,1,0:T(8,128)}, u32[]{:S(2)}, u32[]{:S(2)}) collective-permute-start(f32[2,256,256]{2,1,0:T(8,128)S(1)} %collective-permute-done.3), channel_id=1, source_target_pairs={{18,22},{19,23},{22,18},{23,19},{26,30},{27,31},{30,26},{31,27}} | collective-permute-start | bytes 1572872 | tf_op jit(solution)/shard_map/ppermute | solution.py:326
  21.8 0.0 collective-permute-done.2
  21.8 0.0 collective-permute-done.refs_3_
  21.8 0.2 select_select_fusion.1
  22.0 0.0 copy-start.2
  22.0 0.0 collective-permute-done.4
  22.0 0.7 collective-permute-start.5
  22.7 0.0 collective-permute-done.5
  22.7 0.0 copy-done.2
  22.8 0.1 broadcast_select_fusion.3
  22.9 0.9 pad_maximum_fusion.1
  23.9 1.6 %collective-permute-start.10 = (f32[3,256,256]{2,1,0:T(8,128)}, f32[3,256,256]{2,1,0:T(8,128)}, u32[]{:S(2)}, u32[]{:S(2)}) collective-permute-start(f32[3,256,256]{2,1,0:T(8,128)} %pad_maximum_fusion.1), channel_id=1, source_target_pairs={{2,18},{3,19},{18,2},{19,3}} | collective-permute-start | bytes 2359304 | tf_op jit(solution)/shard_map/ppermute | solution.py:326
  25.5 11.6 %collective-permute-start.9 = (f32[2,256,256]{2,1,0:T(8,128)S(1)}, f32[2,256,256]{2,1,0:T(8,128)}, u32[]{:S(2)}, u32[]{:S(2)}) collective-permute-start(f32[2,256,256]{2,1,0:T(8,128)S(1)} %collective-permute-done.3), channel_id=1, source_target_pairs={{18,20},{19,21},{20,18},{21,19},{26,28},{27,29},{28,26},{29,27}} | collective-permute-start | bytes 1572872 | tf_op jit(solution)/shard_map/ppermute | solution.py:326
  37.1 0.0 collective-permute-done.10
  37.1 0.2 broadcast_select_fusion.a_ref
  37.3 8.6 %collective-permute-done.9 = f32[2,256,256]{2,1,0:T(8,128)} collective-permute-done((f32[2,256,256]{2,1,0:T(8,128)S(1)}, f32[2,256,256]{2,1,0:T(8,128)}, u32[]{:S(2)}, u32[]{:S(2)}) %collective-permute-start.9) | collective-permute-done | bytes 524320 | tf_op jit(solution)/shard_map/ppermute | solution.py:326
  45.8 4.2 %collective-permute-start.11 = (f32[3,256,256]{2,1,0:T(8,128)S(1)}, f32[3,256,256]{2,1,0:T(8,128)S(1)}, u32[]{:S(2)}, u32[]{:S(2)}) collective-permute-start(f32[3,256,256]{2,1,0:T(8,128)S(1)} %broadcast_select_fusion.a_ref), channel_id=1, source_target_pairs={{0,8},{1,9},{2,10},{3,11},{4,12},{5,13},{6,14},{7,15},{8,0},{9,1},... | collective-permute-start | bytes 2359304 | tf_op jit(solution)/shard_map/ppermute | solution.py:326
  50.1 0.7 collective-permute-start.12
  50.7 4.2 %collective-permute-start.7 = (f32[2,256,256]{2,1,0:T(8,128)S(1)}, f32[2,256,256]{2,1,0:T(8,128)S(1)}, u32[]{:S(2)}, u32[]{:S(2)}) collective-permute-start(f32[2,256,256]{2,1,0:T(8,128)S(1)} %collective-permute-done.3), channel_id=1, source_target_pairs={{20,21},{21,20},{22,23},{23,22},{28,29},{29,28},{30,31},{31,30}} | collective-permute-start | bytes 1572872 | tf_op jit(solution)/shard_map/ppermute | solution.py:326
  54.9 1.9 %collective-permute-start.8 = (f32[2,256,256]{2,1,0:T(8,128)S(1)}, f32[2,256,256]{2,1,0:T(8,128)S(1)}, u32[]{:S(2)}, u32[]{:S(2)}) collective-permute-start(f32[2,256,256]{2,1,0:T(8,128)S(1)} %collective-permute-done.1.refs_4_), channel_id=1, source_target_pairs={{4,20},{5,21},{6,22},{7,23},{12,28},{13,29},{14,30},{15,31},{20,4}... | collective-permute-start | bytes 1572872 | tf_op jit(solution)/shard_map/ppermute | solution.py:326
  56.9 0.0 collective-permute-done.11.b_ref
  56.9 6.3 %chain0.1 = (f32[256,256]{1,0:T(8,128)S(1)}, bf16[256,768]{1,0:T(8,128)(2,1)S(1)}, bf16[256,768]{1,0:T(8,128)(2,1)S(1)}) custom-call(s32[2]{0:T(128)S(1)} %pad_add_fusion.pos_ref.refs_0_, f32[3,256,256]{2,1,0:T(8,128)S(1)} %broadcast_select_fusion.a_ref, f32[3,256,256]{2,1,0:T(8,128)S(1)} %collective-permute-done.11.b_ref), custom_call_target="tpu_custom_call" | custom-call | flops 1000 | bytes 1024 | tf_op jit(solution)/shard_map/chain0/pallas_call | solution.py:151
  63.2 0.0 collective-permute-done.12
  63.2 1.5 %select_select_fusion = (f32[2,256,256]{2,1,0:T(8,128)S(1)}, f32[2,256,256]{2,1,0:T(8,128)S(1)}) fusion(f32[2,256,256]{2,1,0:T(8,128)} %collective-permute-done.4, f32[2,256,256]{2,1,0:T(8,128)} %collective-permute-done.9, f32[2,256,256]{2,1,0:T(8,128)S(1)} %collective-permute-done.1.refs_4_, f32[2,256,256]{2,1,0:T(8,128)S(1)} %collective-permute-done.12, ...), kind=kLoop, calls=%fused_computation.2 | loop fusion | flops 786432 | bytes 4718596 | tf_op jit(solution)/shard_map/jit(_where)/select_n | solution.py:394
  64.7 1.9 %collective-permute-start.13 = (f32[2,256,256]{2,1,0:T(8,128)S(1)}, f32[2,256,256]{2,1,0:T(8,128)S(1)}, u32[]{:S(2)}, u32[]{:S(2)}) collective-permute-start(f32[2,256,256]{2,1,0:T(8,128)S(1)} %get-tuple-element.45), channel_id=1, source_target_pairs={{0,1},{1,0},{2,3},{3,2},{8,9},{9,8},{10,11},{11,10},{16,17},{17,16... | collective-permute-start | bytes 1572872 | tf_op jit(solution)/shard_map/ppermute | solution.py:326
  66.6 0.6 collective-permute-done.7
  67.2 2.8 %collective-permute-done.8 = f32[2,256,256]{2,1,0:T(8,128)S(1)} collective-permute-done((f32[2,256,256]{2,1,0:T(8,128)S(1)}, f32[2,256,256]{2,1,0:T(8,128)S(1)}, u32[]{:S(2)}, u32[]{:S(2)}) %collective-permute-start.8) | collective-permute-done | bytes 524320 | tf_op jit(solution)/shard_map/ppermute | solution.py:326
  70.1 2.4 %collective-permute-start.6 = (f32[2,256,256]{2,1,0:T(8,128)S(1)}, f32[2,256,256]{2,1,0:T(8,128)S(1)}, u32[]{:S(2)}, u32[]{:S(2)}) collective-permute-start(f32[2,256,256]{2,1,0:T(8,128)S(1)} %get-tuple-element.46), channel_id=1, source_target_pairs={{4,20},{5,21},{6,22},{7,23},{12,28},{13,29},{14,30},{15,31},{16,17... | collective-permute-start | bytes 1572872 | tf_op jit(solution)/shard_map/ppermute | solution.py:326
  72.5 6.9 %chain1.1 = (f32[256,512]{1,0:T(8,128)S(1)}, bf16[256,768]{1,0:T(8,128)(2,1)S(1)}, bf16[256,768]{1,0:T(8,128)(2,1)S(1)}) custom-call(s32[2]{0:T(128)S(1)} %pad_add_fusion.pos_ref.refs_0_, f32[3,256,256]{2,1,0:T(8,128)S(1)} %broadcast_select_fusion.a_ref, f32[3,256,256]{2,1,0:T(8,128)S(1)} %collective-permute-done.11.b_ref, ...), custom_call_target="tpu_custom_call" | custom-call | flops 1000 | bytes 1024 | tf_op jit(solution)/shard_map/chain1/pallas_call | solution.py:151
  79.4 0.4 collective-permute-done.13
  79.8 0.1 broadcast_select_fusion.1
  79.9 1.2 %collective-permute-start.14 = (f32[2,256,256]{2,1,0:T(8,128)S(1)}, f32[2,256,256]{2,1,0:T(8,128)S(1)}, u32[]{:S(2)}, u32[]{:S(2)}) collective-permute-start(f32[2,256,256]{2,1,0:T(8,128)S(1)} %get-tuple-element.43.a_ref), channel_id=1, source_target_pairs={{0,8},{1,9},{2,10},{3,11},{4,12},{5,13},{6,14},{7,15},{8,0},{9,1},... | collective-permute-start | bytes 1572872 | tf_op jit(solution)/shard_map/ppermute | solution.py:326
  81.0 0.1 collective-permute-start.15
  81.1 3.1 %collective-permute-done.6.refs_5_ = f32[2,256,256]{2,1,0:T(8,128)S(1)} collective-permute-done((f32[2,256,256]{2,1,0:T(8,128)S(1)}, f32[2,256,256]{2,1,0:T(8,128)S(1)}, u32[]{:S(2)}, u32[]{:S(2)}) %collective-permute-start.6) | collective-permute-done | bytes 524320 | tf_op jit(solution)/shard_map/ppermute | solution.py:326
  84.3 7.7 %chain2.1 = (f32[256,768]{1,0:T(8,128)S(1)}, bf16[256,768]{1,0:T(8,128)(2,1)S(1)}, bf16[256,1536]{1,0:T(8,128)(2,1)S(1)}) custom-call(s32[2]{0:T(128)S(1)} %pad_add_fusion.pos_ref.refs_0_, f32[2,256,256]{2,1,0:T(8,128)S(1)} %get-tuple-element.33.a_ref, f32[2,256,256]{2,1,0:T(8,128)S(1)} %collective-permute-done.15.b_ref, ...), custom_call_target="tpu_custom_call" | custom-call | flops 1000 | bytes 1024 | tf_op jit(solution)/shard_map/chain2/pallas_call | solution.py:151
  91.9 0.1 pad_maximum_fusion.refs_6_
  92.1 0.0 copy-start.1
  92.1 4.1 %collective-permute-start.16 = (f32[4,2,256,256]{3,2,1,0:T(8,128)S(1)}, f32[4,2,256,256]{3,2,1,0:T(8,128)S(1)}, u32[]{:S(2)}, u32[]{:S(2)}) collective-permute-start(f32[4,2,256,256]{3,2,1,0:T(8,128)S(1)} %pad_maximum_fusion.refs_6_), channel_id=1, source_target_pairs={{20,28},{21,29},{22,30},{23,31},{28,20},{29,21},{30,22},{31,23}} | collective-permute-start | bytes 6291464 | tf_op jit(solution)/shard_map/ppermute | solution.py:326
  96.2 8.3 %chain3.1 = (f32[256,1024]{1,0:T(8,128)S(1)}, bf16[256,768]{1,0:T(8,128)(2,1)S(1)}, bf16[256,2304]{1,0:T(8,128)(2,1)S(1)}) custom-call(s32[2]{0:T(128)S(1)} %pad_add_fusion.pos_ref.refs_0_, f32[2,256,256]{2,1,0:T(8,128)S(1)} %get-tuple-element.43.a_ref, f32[2,256,256]{2,1,0:T(8,128)S(1)} %collective-permute-done.14.b_ref, ...), custom_call_target="tpu_custom_call" | custom-call | flops 1000 | bytes 1024 | tf_op jit(solution)/shard_map/chain3/pallas_call | solution.py:151
  104.5 8.1 %tile.1 = f32[512,256]{1,0:T(8,128)} custom-call(s32[2]{0:T(128)S(1)} %pad_add_fusion.pos_ref.refs_0_, f32[512,256]{1,0:T(8,128)S(1)} %copy-done.1, f32[2,256,256]{2,1,0:T(8,128)S(1)} %bitcast.8, f32[2,256,256]{2,1,0:T(8,128)S(1)} %collective-permute-done.refs_3_, f32[2,256,256]{2,1,0:T(8,128)S(1)} %collective-permute-done.1.refs_4_, ...), custom_call_target="tpu_custom_call" | custom-call | flops 1000 | bytes 1024 | tf_op jit(solution)/shard_map/tile/pallas_call | solution.py:445
  (7 shorter events, 0.0 us)
Async XLA Ops:
  0.1 1.0 copy-start
  1.9 18.5 %collective-permute-start.3 = (f32[2,256,256]{2,1,0:T(8,128)S(1)}, f32[2,256,256]{2,1,0:T(8,128)S(1)}, u32[]{:S(2)}, u32[]{:S(2)}) collective-permute-start(f32[2,256,256]{2,1,0:T(8,128)S(1)} %turn.1), channel_id=1, source_target_pairs={{0,16},{1,17},{2,18},{3,19},{4,20},{5,21},{6,22},{7,23},{8,24},{9,... | collective-permute-start | bytes 1572872 | tf_op jit(solution)/shard_map/ppermute | solution.py:326
  2.2 19.6 %collective-permute-start.2 = (f32[2,256,256]{2,1,0:T(8,128)S(1)}, f32[2,256,256]{2,1,0:T(8,128)S(1)}, u32[]{:S(2)}, u32[]{:S(2)}) collective-permute-start(f32[2,256,256]{2,1,0:T(8,128)S(1)} %turn.1), channel_id=1, source_target_pairs={{0,20},{1,21},{20,0},{21,1}} | collective-permute-start | bytes 1572872 | tf_op jit(solution)/shard_map/ppermute | solution.py:326
  2.9 18.9 %collective-permute-start.1 = (f32[2,256,256]{2,1,0:T(8,128)S(1)}, f32[2,256,256]{2,1,0:T(8,128)S(1)}, u32[]{:S(2)}, u32[]{:S(2)}) collective-permute-start(f32[2,256,256]{2,1,0:T(8,128)S(1)} %turn.1), channel_id=1, source_target_pairs={{0,2},{1,3},{2,0},{3,1},{4,6},{5,7},{6,4},{7,5},{10,8},{11,9},{12,... | collective-permute-start | bytes 1572872 | tf_op jit(solution)/shard_map/ppermute | solution.py:326
  3.6 18.2 %collective-permute-start = (f32[2,256,256]{2,1,0:T(8,128)S(1)}, f32[2,256,256]{2,1,0:T(8,128)S(1)}, u32[]{:S(2)}, u32[]{:S(2)}) collective-permute-start(f32[2,256,256]{2,1,0:T(8,128)S(1)} %turn.1), channel_id=1, source_target_pairs={{0,22},{1,23},{16,17},{17,16},{18,19},{19,18},{22,0},{23,1},{24,25... | collective-permute-start | bytes 1572872 | tf_op jit(solution)/shard_map/ppermute | solution.py:326
  20.3 1.7 %collective-permute-start.4 = (f32[2,256,256]{2,1,0:T(8,128)S(1)}, f32[2,256,256]{2,1,0:T(8,128)}, u32[]{:S(2)}, u32[]{:S(2)}) collective-permute-start(f32[2,256,256]{2,1,0:T(8,128)S(1)} %collective-permute-done.3), channel_id=1, source_target_pairs={{18,22},{19,23},{22,18},{23,19},{26,30},{27,31},{30,26},{31,27}} | collective-permute-start | bytes 1572872 | tf_op jit(solution)/shard_map/ppermute | solution.py:326
  22.0 0.8 copy-start.2
  22.0 0.7 collective-permute-start.5
  23.9 13.2 %collective-permute-start.10 = (f32[3,256,256]{2,1,0:T(8,128)}, f32[3,256,256]{2,1,0:T(8,128)}, u32[]{:S(2)}, u32[]{:S(2)}) collective-permute-start(f32[3,256,256]{2,1,0:T(8,128)} %pad_maximum_fusion.1), channel_id=1, source_target_pairs={{2,18},{3,19},{18,2},{19,3}} | collective-permute-start | bytes 2359304 | tf_op jit(solution)/shard_map/ppermute | solution.py:326
  25.5 20.4 %collective-permute-start.9 = (f32[2,256,256]{2,1,0:T(8,128)S(1)}, f32[2,256,256]{2,1,0:T(8,128)}, u32[]{:S(2)}, u32[]{:S(2)}) collective-permute-start(f32[2,256,256]{2,1,0:T(8,128)S(1)} %collective-permute-done.3), channel_id=1, source_target_pairs={{18,20},{19,21},{20,18},{21,19},{26,28},{27,29},{28,26},{29,27}} | collective-permute-start | bytes 1572872 | tf_op jit(solution)/shard_map/ppermute | solution.py:326
  45.8 11.0 %collective-permute-start.11 = (f32[3,256,256]{2,1,0:T(8,128)S(1)}, f32[3,256,256]{2,1,0:T(8,128)S(1)}, u32[]{:S(2)}, u32[]{:S(2)}) collective-permute-start(f32[3,256,256]{2,1,0:T(8,128)S(1)} %broadcast_select_fusion.a_ref), channel_id=1, source_target_pairs={{0,8},{1,9},{2,10},{3,11},{4,12},{5,13},{6,14},{7,15},{8,0},{9,1},... | collective-permute-start | bytes 2359304 | tf_op jit(solution)/shard_map/ppermute | solution.py:326
  50.1 13.1 %collective-permute-start.12 = (f32[2,256,256]{2,1,0:T(8,128)S(1)}, f32[2,256,256]{2,1,0:T(8,128)S(1)}, u32[]{:S(2)}, u32[]{:S(2)}) collective-permute-start(f32[2,256,256]{2,1,0:T(8,128)S(1)} %collective-permute-done.1.refs_4_), channel_id=1, source_target_pairs={{0,16},{1,17},{8,24},{9,25},{16,0},{17,1},{24,8},{25,9}} | collective-permute-start | bytes 1572872 | tf_op jit(solution)/shard_map/ppermute | solution.py:326
  50.7 16.5 %collective-permute-start.7 = (f32[2,256,256]{2,1,0:T(8,128)S(1)}, f32[2,256,256]{2,1,0:T(8,128)S(1)}, u32[]{:S(2)}, u32[]{:S(2)}) collective-permute-start(f32[2,256,256]{2,1,0:T(8,128)S(1)} %collective-permute-done.3), channel_id=1, source_target_pairs={{20,21},{21,20},{22,23},{23,22},{28,29},{29,28},{30,31},{31,30}} | collective-permute-start | bytes 1572872 | tf_op jit(solution)/shard_map/ppermute | solution.py:326
  54.9 15.1 %collective-permute-start.8 = (f32[2,256,256]{2,1,0:T(8,128)S(1)}, f32[2,256,256]{2,1,0:T(8,128)S(1)}, u32[]{:S(2)}, u32[]{:S(2)}) collective-permute-start(f32[2,256,256]{2,1,0:T(8,128)S(1)} %collective-permute-done.1.refs_4_), channel_id=1, source_target_pairs={{4,20},{5,21},{6,22},{7,23},{12,28},{13,29},{14,30},{15,31},{20,4}... | collective-permute-start | bytes 1572872 | tf_op jit(solution)/shard_map/ppermute | solution.py:326
  64.7 15.1 %collective-permute-start.13 = (f32[2,256,256]{2,1,0:T(8,128)S(1)}, f32[2,256,256]{2,1,0:T(8,128)S(1)}, u32[]{:S(2)}, u32[]{:S(2)}) collective-permute-start(f32[2,256,256]{2,1,0:T(8,128)S(1)} %get-tuple-element.45), channel_id=1, source_target_pairs={{0,1},{1,0},{2,3},{3,2},{8,9},{9,8},{10,11},{11,10},{16,17},{17,16... | collective-permute-start | bytes 1572872 | tf_op jit(solution)/shard_map/ppermute | solution.py:326
  70.1 14.2 %collective-permute-start.6 = (f32[2,256,256]{2,1,0:T(8,128)S(1)}, f32[2,256,256]{2,1,0:T(8,128)S(1)}, u32[]{:S(2)}, u32[]{:S(2)}) collective-permute-start(f32[2,256,256]{2,1,0:T(8,128)S(1)} %get-tuple-element.46), channel_id=1, source_target_pairs={{4,20},{5,21},{6,22},{7,23},{12,28},{13,29},{14,30},{15,31},{16,17... | collective-permute-start | bytes 1572872 | tf_op jit(solution)/shard_map/ppermute | solution.py:326
  79.9 4.4 %collective-permute-start.14 = (f32[2,256,256]{2,1,0:T(8,128)S(1)}, f32[2,256,256]{2,1,0:T(8,128)S(1)}, u32[]{:S(2)}, u32[]{:S(2)}) collective-permute-start(f32[2,256,256]{2,1,0:T(8,128)S(1)} %get-tuple-element.43.a_ref), channel_id=1, source_target_pairs={{0,8},{1,9},{2,10},{3,11},{4,12},{5,13},{6,14},{7,15},{8,0},{9,1},... | collective-permute-start | bytes 1572872 | tf_op jit(solution)/shard_map/ppermute | solution.py:326
  81.0 3.2 %collective-permute-start.15 = (f32[2,256,256]{2,1,0:T(8,128)S(1)}, f32[2,256,256]{2,1,0:T(8,128)S(1)}, u32[]{:S(2)}, u32[]{:S(2)}) collective-permute-start(f32[2,256,256]{2,1,0:T(8,128)S(1)} %get-tuple-element.33.a_ref), channel_id=1, source_target_pairs={{0,8},{1,9},{2,10},{3,11},{4,12},{5,13},{6,14},{7,15},{8,0},{9,1},... | collective-permute-start | bytes 1572872 | tf_op jit(solution)/shard_map/ppermute | solution.py:326
  92.1 12.4 %copy-start.1 = (f32[512,256]{1,0:T(8,128)S(1)}, f32[512,256]{1,0:T(8,128)}, u32[]{:S(2)}) copy-start(f32[512,256]{1,0:T(8,128)} %refs_1_.1) | copy-start | bytes 1572868
  92.1 12.4 %collective-permute-start.16 = (f32[4,2,256,256]{3,2,1,0:T(8,128)S(1)}, f32[4,2,256,256]{3,2,1,0:T(8,128)S(1)}, u32[]{:S(2)}, u32[]{:S(2)}) collective-permute-start(f32[4,2,256,256]{3,2,1,0:T(8,128)S(1)} %pad_maximum_fusion.refs_6_), channel_id=1, source_target_pairs={{20,28},{21,29},{22,30},{23,31},{28,20},{29,21},{30,22},{31,23}} | collective-permute-start | bytes 6291464 | tf_op jit(solution)/shard_map/ppermute | solution.py:326

commit v6 on v5

--- a/solution.py
+++ b/solution.py
@@ -15,7 +15,7 @@
 VMEM = pl.BlockSpec(memory_space=pltpu.VMEM)
 SMEM = pl.BlockSpec(memory_space=pltpu.SMEM)
 PARAMS = pltpu.CompilerParams(vmem_limit_bytes=16 * 2**20)
-TILE_PARAMS = pltpu.CompilerParams(vmem_limit_bytes=36 * 2**20)
+TILE_PARAMS = pltpu.CompilerParams(vmem_limit_bytes=28 * 2**20)
 COST = pl.CostEstimate(flops=1000, bytes_accessed=1024, transcendentals=0)
 
 

time: 113 us -> 113 us (level)
  no operation moved by 1% of the time
where the time goes in v6:
time: 113 us
  starting transfers between devices  38.4 us (34%)
  Pallas kernels  37.9 us (34%)
  waiting for transfers between devices  31.7 us (28%)
  other arithmetic  3.19 us (3%)
    ppermute x17, starting transfers between devices, swap(): return lax.ppermute(x, ('row', 'col'), perm)  38.4 us
    ppermute x17, waiting for transfers between devices, swap(): return lax.ppermute(x, ('row', 'col'), perm)  31.7 us
    pallas_call x4, Pallas kernels, chain_call(): pl.pallas_call(kernel, out_shape=[jax.ShapeDtypeStruct((width, (k + 1) *...  29.1 us
    pallas_call x1, Pallas kernels, box_mesh(): pl.pallas_call(functools.partial(box_tile, width), out_shape=jax.ShapeDty...  8.09 us
  transfers between devices with their start and end apart: 17, of which 6 were waited for; matrix products, arithmetic and copies ran while one was open for 2% of the time, Pallas kernels for 19%

profile of v6, /device:TPU:19, one launch (start us, length us, event | category | flops | bytes accessed | tf_op | source)
XLA Modules:
  0.0 112.6 jit_solution(17448630806688984011)
XLA Ops:
  0.0 0.1 pad_add_fusion.pos_ref.refs_0_
  0.1 1.0 copy-done
  1.1 0.7 turn.1
  1.9 0.3 collective-permute-start.3
  2.2 0.7 collective-permute-start.2
  2.9 0.7 collective-permute-start.1
  3.6 0.7 collective-permute-start
  4.3 16.1 %collective-permute-done.3 = f32[2,256,256]{2,1,0:T(8,128)S(1)} collective-permute-done((f32[2,256,256]{2,1,0:T(8,128)S(1)}, f32[2,256,256]{2,1,0:T(8,128)S(1)}, u32[]{:S(2)}, u32[]{:S(2)}) %collective-permute-start.3) | collective-permute-done | bytes 524320 | tf_op jit(solution)/shard_map/ppermute | solution.py:326
  20.3 1.5 %collective-permute-start.4 = (f32[2,256,256]{2,1,0:T(8,128)S(1)}, f32[2,256,256]{2,1,0:T(8,128)}, u32[]{:S(2)}, u32[]{:S(2)}) collective-permute-start(f32[2,256,256]{2,1,0:T(8,128)S(1)} %collective-permute-done.3), channel_id=1, source_target_pairs={{18,22},{19,23},{22,18},{23,19},{26,30},{27,31},{30,26},{31,27}} | collective-permute-start | bytes 1572872 | tf_op jit(solution)/shard_map/ppermute | solution.py:326
  21.8 0.0 collective-permute-done.2
  21.8 0.0 collective-permute-done.refs_3_
  21.8 0.2 select_select_fusion.1
  22.0 0.0 copy-start.2
  22.0 0.0 collective-permute-done.4
  22.0 0.7 collective-permute-start.5
  22.7 0.0 collective-permute-done.5
  22.7 0.0 copy-done.2
  22.8 0.1 broadcast_select_fusion.3
  22.9 0.9 pad_maximum_fusion.1
  23.9 1.6 %collective-permute-start.10 = (f32[3,256,256]{2,1,0:T(8,128)}, f32[3,256,256]{2,1,0:T(8,128)}, u32[]{:S(2)}, u32[]{:S(2)}) collective-permute-start(f32[3,256,256]{2,1,0:T(8,128)} %pad_maximum_fusion.1), channel_id=1, source_target_pairs={{2,18},{3,19},{18,2},{19,3}} | collective-permute-start | bytes 2359304 | tf_op jit(solution)/shard_map/ppermute | solution.py:326
  25.5 11.6 %collective-permute-start.9 = (f32[2,256,256]{2,1,0:T(8,128)S(1)}, f32[2,256,256]{2,1,0:T(8,128)}, u32[]{:S(2)}, u32[]{:S(2)}) collective-permute-start(f32[2,256,256]{2,1,0:T(8,128)S(1)} %collective-permute-done.3), channel_id=1, source_target_pairs={{18,20},{19,21},{20,18},{21,19},{26,28},{27,29},{28,26},{29,27}} | collective-permute-start | bytes 1572872 | tf_op jit(solution)/shard_map/ppermute | solution.py:326
  37.1 0.0 collective-permute-done.10
  37.1 0.2 broadcast_select_fusion.a_ref
  37.3 8.6 %collective-permute-done.9 = f32[2,256,256]{2,1,0:T(8,128)} collective-permute-done((f32[2,256,256]{2,1,0:T(8,128)S(1)}, f32[2,256,256]{2,1,0:T(8,128)}, u32[]{:S(2)}, u32[]{:S(2)}) %collective-permute-start.9) | collective-permute-done | bytes 524320 | tf_op jit(solution)/shard_map/ppermute | solution.py:326
  45.8 4.2 %collective-permute-start.11 = (f32[3,256,256]{2,1,0:T(8,128)S(1)}, f32[3,256,256]{2,1,0:T(8,128)S(1)}, u32[]{:S(2)}, u32[]{:S(2)}) collective-permute-start(f32[3,256,256]{2,1,0:T(8,128)S(1)} %broadcast_select_fusion.a_ref), channel_id=1, source_target_pairs={{0,8},{1,9},{2,10},{3,11},{4,12},{5,13},{6,14},{7,15},{8,0},{9,1},... | collective-permute-start | bytes 2359304 | tf_op jit(solution)/shard_map/ppermute | solution.py:326
  50.1 0.7 collective-permute-start.12
  50.7 4.2 %collective-permute-start.7 = (f32[2,256,256]{2,1,0:T(8,128)S(1)}, f32[2,256,256]{2,1,0:T(8,128)S(1)}, u32[]{:S(2)}, u32[]{:S(2)}) collective-permute-start(f32[2,256,256]{2,1,0:T(8,128)S(1)} %collective-permute-done.3), channel_id=1, source_target_pairs={{20,21},{21,20},{22,23},{23,22},{28,29},{29,28},{30,31},{31,30}} | collective-permute-start | bytes 1572872 | tf_op jit(solution)/shard_map/ppermute | solution.py:326
  54.9 1.9 %collective-permute-start.8 = (f32[2,256,256]{2,1,0:T(8,128)S(1)}, f32[2,256,256]{2,1,0:T(8,128)S(1)}, u32[]{:S(2)}, u32[]{:S(2)}) collective-permute-start(f32[2,256,256]{2,1,0:T(8,128)S(1)} %collective-permute-done.1.refs_4_), channel_id=1, source_target_pairs={{4,20},{5,21},{6,22},{7,23},{12,28},{13,29},{14,30},{15,31},{20,4}... | collective-permute-start | bytes 1572872 | tf_op jit(solution)/shard_map/ppermute | solution.py:326
  56.9 0.0 collective-permute-done.11.b_ref
  56.9 6.3 %chain0.1 = (f32[256,256]{1,0:T(8,128)S(1)}, bf16[256,768]{1,0:T(8,128)(2,1)S(1)}, bf16[256,768]{1,0:T(8,128)(2,1)S(1)}) custom-call(s32[2]{0:T(128)S(1)} %pad_add_fusion.pos_ref.refs_0_, f32[3,256,256]{2,1,0:T(8,128)S(1)} %broadcast_select_fusion.a_ref, f32[3,256,256]{2,1,0:T(8,128)S(1)} %collective-permute-done.11.b_ref), custom_call_target="tpu_custom_call" | custom-call | flops 1000 | bytes 1024 | tf_op jit(solution)/shard_map/chain0/pallas_call | solution.py:151
  63.2 0.0 collective-permute-done.12
  63.2 1.5 %select_select_fusion = (f32[2,256,256]{2,1,0:T(8,128)S(1)}, f32[2,256,256]{2,1,0:T(8,128)S(1)}) fusion(f32[2,256,256]{2,1,0:T(8,128)} %collective-permute-done.4, f32[2,256,256]{2,1,0:T(8,128)} %collective-permute-done.9, f32[2,256,256]{2,1,0:T(8,128)S(1)} %collective-permute-done.1.refs_4_, f32[2,256,256]{2,1,0:T(8,128)S(1)} %collective-permute-done.12, ...), kind=kLoop, calls=%fused_computation.2 | loop fusion | flops 786432 | bytes 4718596 | tf_op jit(solution)/shard_map/jit(_where)/select_n | solution.py:394
  64.7 1.9 %collective-permute-start.13 = (f32[2,256,256]{2,1,0:T(8,128)S(1)}, f32[2,256,256]{2,1,0:T(8,128)S(1)}, u32[]{:S(2)}, u32[]{:S(2)}) collective-permute-start(f32[2,256,256]{2,1,0:T(8,128)S(1)} %get-tuple-element.45), channel_id=1, source_target_pairs={{0,1},{1,0},{2,3},{3,2},{8,9},{9,8},{10,11},{11,10},{16,17},{17,16... | collective-permute-start | bytes 1572872 | tf_op jit(solution)/shard_map/ppermute | solution.py:326
  66.6 0.6 collective-permute-done.7
  67.2 2.8 %collective-permute-done.8 = f32[2,256,256]{2,1,0:T(8,128)S(1)} collective-permute-done((f32[2,256,256]{2,1,0:T(8,128)S(1)}, f32[2,256,256]{2,1,0:T(8,128)S(1)}, u32[]{:S(2)}, u32[]{:S(2)}) %collective-permute-start.8) | collective-permute-done | bytes 524320 | tf_op jit(solution)/shard_map/ppermute | solution.py:326
  70.1 2.4 %collective-permute-start.6 = (f32[2,256,256]{2,1,0:T(8,128)S(1)}, f32[2,256,256]{2,1,0:T(8,128)S(1)}, u32[]{:S(2)}, u32[]{:S(2)}) collective-permute-start(f32[2,256,256]{2,1,0:T(8,128)S(1)} %get-tuple-element.46), channel_id=1, source_target_pairs={{4,20},{5,21},{6,22},{7,23},{12,28},{13,29},{14,30},{15,31},{16,17... | collective-permute-start | bytes 1572872 | tf_op jit(solution)/shard_map/ppermute | solution.py:326
  72.5 6.9 %chain1.1 = (f32[256,512]{1,0:T(8,128)S(1)}, bf16[256,768]{1,0:T(8,128)(2,1)S(1)}, bf16[256,768]{1,0:T(8,128)(2,1)S(1)}) custom-call(s32[2]{0:T(128)S(1)} %pad_add_fusion.pos_ref.refs_0_, f32[3,256,256]{2,1,0:T(8,128)S(1)} %broadcast_select_fusion.a_ref, f32[3,256,256]{2,1,0:T(8,128)S(1)} %collective-permute-done.11.b_ref, ...), custom_call_target="tpu_custom_call" | custom-call | flops 1000 | bytes 1024 | tf_op jit(solution)/shard_map/chain1/pallas_call | solution.py:151
  79.4 0.4 collective-permute-done.13
  79.8 0.1 broadcast_select_fusion.1
  79.9 1.2 %collective-permute-start.14 = (f32[2,256,256]{2,1,0:T(8,128)S(1)}, f32[2,256,256]{2,1,0:T(8,128)S(1)}, u32[]{:S(2)}, u32[]{:S(2)}) collective-permute-start(f32[2,256,256]{2,1,0:T(8,128)S(1)} %get-tuple-element.43.a_ref), channel_id=1, source_target_pairs={{0,8},{1,9},{2,10},{3,11},{4,12},{5,13},{6,14},{7,15},{8,0},{9,1},... | collective-permute-start | bytes 1572872 | tf_op jit(solution)/shard_map/ppermute | solution.py:326
  81.0 0.1 collective-permute-start.15
  81.1 3.1 %collective-permute-done.6.refs_5_ = f32[2,256,256]{2,1,0:T(8,128)S(1)} collective-permute-done((f32[2,256,256]{2,1,0:T(8,128)S(1)}, f32[2,256,256]{2,1,0:T(8,128)S(1)}, u32[]{:S(2)}, u32[]{:S(2)}) %collective-permute-start.6) | collective-permute-done | bytes 524320 | tf_op jit(solution)/shard_map/ppermute | solution.py:326
  84.3 7.7 %chain2.1 = (f32[256,768]{1,0:T(8,128)S(1)}, bf16[256,768]{1,0:T(8,128)(2,1)S(1)}, bf16[256,1536]{1,0:T(8,128)(2,1)S(1)}) custom-call(s32[2]{0:T(128)S(1)} %pad_add_fusion.pos_ref.refs_0_, f32[2,256,256]{2,1,0:T(8,128)S(1)} %get-tuple-element.33.a_ref, f32[2,256,256]{2,1,0:T(8,128)S(1)} %collective-permute-done.15.b_ref, ...), custom_call_target="tpu_custom_call" | custom-call | flops 1000 | bytes 1024 | tf_op jit(solution)/shard_map/chain2/pallas_call | solution.py:151
  91.9 0.1 pad_maximum_fusion.refs_6_
  92.1 0.0 copy-start.1
  92.1 4.1 %collective-permute-start.16 = (f32[4,2,256,256]{3,2,1,0:T(8,128)S(1)}, f32[4,2,256,256]{3,2,1,0:T(8,128)S(1)}, u32[]{:S(2)}, u32[]{:S(2)}) collective-permute-start(f32[4,2,256,256]{3,2,1,0:T(8,128)S(1)} %pad_maximum_fusion.refs_6_), channel_id=1, source_target_pairs={{20,28},{21,29},{22,30},{23,31},{28,20},{29,21},{30,22},{31,23}} | collective-permute-start | bytes 6291464 | tf_op jit(solution)/shard_map/ppermute | solution.py:326
  96.2 8.3 %chain3.1 = (f32[256,1024]{1,0:T(8,128)S(1)}, bf16[256,768]{1,0:T(8,128)(2,1)S(1)}, bf16[256,2304]{1,0:T(8,128)(2,1)S(1)}) custom-call(s32[2]{0:T(128)S(1)} %pad_add_fusion.pos_ref.refs_0_, f32[2,256,256]{2,1,0:T(8,128)S(1)} %get-tuple-element.43.a_ref, f32[2,256,256]{2,1,0:T(8,128)S(1)} %collective-permute-done.14.b_ref, ...), custom_call_target="tpu_custom_call" | custom-call | flops 1000 | bytes 1024 | tf_op jit(solution)/shard_map/chain3/pallas_call | solution.py:151
  104.5 8.1 %tile.1 = f32[512,256]{1,0:T(8,128)} custom-call(s32[2]{0:T(128)S(1)} %pad_add_fusion.pos_ref.refs_0_, f32[512,256]{1,0:T(8,128)S(1)} %copy-done.1, f32[2,256,256]{2,1,0:T(8,128)S(1)} %bitcast.8, f32[2,256,256]{2,1,0:T(8,128)S(1)} %collective-permute-done.refs_3_, f32[2,256,256]{2,1,0:T(8,128)S(1)} %collective-permute-done.1.refs_4_, ...), custom_call_target="tpu_custom_call" | custom-call | flops 1000 | bytes 1024 | tf_op jit(solution)/shard_map/tile/pallas_call | solution.py:445
  (7 shorter events, 0.0 us)
Async XLA Ops:
  0.1 1.0 copy-start
  1.9 18.5 %collective-permute-start.3 = (f32[2,256,256]{2,1,0:T(8,128)S(1)}, f32[2,256,256]{2,1,0:T(8,128)S(1)}, u32[]{:S(2)}, u32[]{:S(2)}) collective-permute-start(f32[2,256,256]{2,1,0:T(8,128)S(1)} %turn.1), channel_id=1, source_target_pairs={{0,16},{1,17},{2,18},{3,19},{4,20},{5,21},{6,22},{7,23},{8,24},{9,... | collective-permute-start | bytes 1572872 | tf_op jit(solution)/shard_map/ppermute | solution.py:326
  2.2 19.6 %collective-permute-start.2 = (f32[2,256,256]{2,1,0:T(8,128)S(1)}, f32[2,256,256]{2,1,0:T(8,128)S(1)}, u32[]{:S(2)}, u32[]{:S(2)}) collective-permute-start(f32[2,256,256]{2,1,0:T(8,128)S(1)} %turn.1), channel_id=1, source_target_pairs={{0,20},{1,21},{20,0},{21,1}} | collective-permute-start | bytes 1572872 | tf_op jit(solution)/shard_map/ppermute | solution.py:326
  2.9 18.9 %collective-permute-start.1 = (f32[2,256,256]{2,1,0:T(8,128)S(1)}, f32[2,256,256]{2,1,0:T(8,128)S(1)}, u32[]{:S(2)}, u32[]{:S(2)}) collective-permute-start(f32[2,256,256]{2,1,0:T(8,128)S(1)} %turn.1), channel_id=1, source_target_pairs={{0,2},{1,3},{2,0},{3,1},{4,6},{5,7},{6,4},{7,5},{10,8},{11,9},{12,... | collective-permute-start | bytes 1572872 | tf_op jit(solution)/shard_map/ppermute | solution.py:326
  3.6 18.2 %collective-permute-start = (f32[2,256,256]{2,1,0:T(8,128)S(1)}, f32[2,256,256]{2,1,0:T(8,128)S(1)}, u32[]{:S(2)}, u32[]{:S(2)}) collective-permute-start(f32[2,256,256]{2,1,0:T(8,128)S(1)} %turn.1), channel_id=1, source_target_pairs={{0,22},{1,23},{16,17},{17,16},{18,19},{19,18},{22,0},{23,1},{24,25... | collective-permute-start | bytes 1572872 | tf_op jit(solution)/shard_map/ppermute | solution.py:326
  20.3 1.7 %collective-permute-start.4 = (f32[2,256,256]{2,1,0:T(8,128)S(1)}, f32[2,256,256]{2,1,0:T(8,128)}, u32[]{:S(2)}, u32[]{:S(2)}) collective-permute-start(f32[2,256,256]{2,1,0:T(8,128)S(1)} %collective-permute-done.3), channel_id=1, source_target_pairs={{18,22},{19,23},{22,18},{23,19},{26,30},{27,31},{30,26},{31,27}} | collective-permute-start | bytes 1572872 | tf_op jit(solution)/shard_map/ppermute | solution.py:326
  22.0 0.8 copy-start.2
  22.0 0.7 collective-permute-start.5
  23.9 13.2 %collective-permute-start.10 = (f32[3,256,256]{2,1,0:T(8,128)}, f32[3,256,256]{2,1,0:T(8,128)}, u32[]{:S(2)}, u32[]{:S(2)}) collective-permute-start(f32[3,256,256]{2,1,0:T(8,128)} %pad_maximum_fusion.1), channel_id=1, source_target_pairs={{2,18},{3,19},{18,2},{19,3}} | collective-permute-start | bytes 2359304 | tf_op jit(solution)/shard_map/ppermute | solution.py:326
  25.5 20.4 %collective-permute-start.9 = (f32[2,256,256]{2,1,0:T(8,128)S(1)}, f32[2,256,256]{2,1,0:T(8,128)}, u32[]{:S(2)}, u32[]{:S(2)}) collective-permute-start(f32[2,256,256]{2,1,0:T(8,128)S(1)} %collective-permute-done.3), channel_id=1, source_target_pairs={{18,20},{19,21},{20,18},{21,19},{26,28},{27,29},{28,26},{29,27}} | collective-permute-start | bytes 1572872 | tf_op jit(solution)/shard_map/ppermute | solution.py:326
  45.8 11.0 %collective-permute-start.11 = (f32[3,256,256]{2,1,0:T(8,128)S(1)}, f32[3,256,256]{2,1,0:T(8,128)S(1)}, u32[]{:S(2)}, u32[]{:S(2)}) collective-permute-start(f32[3,256,256]{2,1,0:T(8,128)S(1)} %broadcast_select_fusion.a_ref), channel_id=1, source_target_pairs={{0,8},{1,9},{2,10},{3,11},{4,12},{5,13},{6,14},{7,15},{8,0},{9,1},... | collective-permute-start | bytes 2359304 | tf_op jit(solution)/shard_map/ppermute | solution.py:326
  50.1 13.1 %collective-permute-start.12 = (f32[2,256,256]{2,1,0:T(8,128)S(1)}, f32[2,256,256]{2,1,0:T(8,128)S(1)}, u32[]{:S(2)}, u32[]{:S(2)}) collective-permute-start(f32[2,256,256]{2,1,0:T(8,128)S(1)} %collective-permute-done.1.refs_4_), channel_id=1, source_target_pairs={{0,16},{1,17},{8,24},{9,25},{16,0},{17,1},{24,8},{25,9}} | collective-permute-start | bytes 1572872 | tf_op jit(solution)/shard_map/ppermute | solution.py:326
  50.7 16.5 %collective-permute-start.7 = (f32[2,256,256]{2,1,0:T(8,128)S(1)}, f32[2,256,256]{2,1,0:T(8,128)S(1)}, u32[]{:S(2)}, u32[]{:S(2)}) collective-permute-start(f32[2,256,256]{2,1,0:T(8,128)S(1)} %collective-permute-done.3), channel_id=1, source_target_pairs={{20,21},{21,20},{22,23},{23,22},{28,29},{29,28},{30,31},{31,30}} | collective-permute-start | bytes 1572872 | tf_op jit(solution)/shard_map/ppermute | solution.py:326
  54.9 15.1 %collective-permute-start.8 = (f32[2,256,256]{2,1,0:T(8,128)S(1)}, f32[2,256,256]{2,1,0:T(8,128)S(1)}, u32[]{:S(2)}, u32[]{:S(2)}) collective-permute-start(f32[2,256,256]{2,1,0:T(8,128)S(1)} %collective-permute-done.1.refs_4_), channel_id=1, source_target_pairs={{4,20},{5,21},{6,22},{7,23},{12,28},{13,29},{14,30},{15,31},{20,4}... | collective-permute-start | bytes 1572872 | tf_op jit(solution)/shard_map/ppermute | solution.py:326
  64.7 15.1 %collective-permute-start.13 = (f32[2,256,256]{2,1,0:T(8,128)S(1)}, f32[2,256,256]{2,1,0:T(8,128)S(1)}, u32[]{:S(2)}, u32[]{:S(2)}) collective-permute-start(f32[2,256,256]{2,1,0:T(8,128)S(1)} %get-tuple-element.45), channel_id=1, source_target_pairs={{0,1},{1,0},{2,3},{3,2},{8,9},{9,8},{10,11},{11,10},{16,17},{17,16... | collective-permute-start | bytes 1572872 | tf_op jit(solution)/shard_map/ppermute | solution.py:326
  70.1 14.2 %collective-permute-start.6 = (f32[2,256,256]{2,1,0:T(8,128)S(1)}, f32[2,256,256]{2,1,0:T(8,128)S(1)}, u32[]{:S(2)}, u32[]{:S(2)}) collective-permute-start(f32[2,256,256]{2,1,0:T(8,128)S(1)} %get-tuple-element.46), channel_id=1, source_target_pairs={{4,20},{5,21},{6,22},{7,23},{12,28},{13,29},{14,30},{15,31},{16,17... | collective-permute-start | bytes 1572872 | tf_op jit(solution)/shard_map/ppermute | solution.py:326
  79.9 4.4 %collective-permute-start.14 = (f32[2,256,256]{2,1,0:T(8,128)S(1)}, f32[2,256,256]{2,1,0:T(8,128)S(1)}, u32[]{:S(2)}, u32[]{:S(2)}) collective-permute-start(f32[2,256,256]{2,1,0:T(8,128)S(1)} %get-tuple-element.43.a_ref), channel_id=1, source_target_pairs={{0,8},{1,9},{2,10},{3,11},{4,12},{5,13},{6,14},{7,15},{8,0},{9,1},... | collective-permute-start | bytes 1572872 | tf_op jit(solution)/shard_map/ppermute | solution.py:326
  81.0 3.2 %collective-permute-start.15 = (f32[2,256,256]{2,1,0:T(8,128)S(1)}, f32[2,256,256]{2,1,0:T(8,128)S(1)}, u32[]{:S(2)}, u32[]{:S(2)}) collective-permute-start(f32[2,256,256]{2,1,0:T(8,128)S(1)} %get-tuple-element.33.a_ref), channel_id=1, source_target_pairs={{0,8},{1,9},{2,10},{3,11},{4,12},{5,13},{6,14},{7,15},{8,0},{9,1},... | collective-permute-start | bytes 1572872 | tf_op jit(solution)/shard_map/ppermute | solution.py:326
  92.1 12.4 %copy-start.1 = (f32[512,256]{1,0:T(8,128)S(1)}, f32[512,256]{1,0:T(8,128)}, u32[]{:S(2)}) copy-start(f32[512,256]{1,0:T(8,128)} %refs_1_.1) | copy-start | bytes 1572868
  92.1 12.4 %collective-permute-start.16 = (f32[4,2,256,256]{3,2,1,0:T(8,128)S(1)}, f32[4,2,256,256]{3,2,1,0:T(8,128)S(1)}, u32[]{:S(2)}, u32[]{:S(2)}) collective-permute-start(f32[4,2,256,256]{3,2,1,0:T(8,128)S(1)} %pad_maximum_fusion.refs_6_), channel_id=1, source_target_pairs={{20,28},{21,29},{22,30},{23,31},{28,20},{29,21},{30,22},{31,23}} | collective-permute-start | bytes 6291464 | tf_op jit(solution)/shard_map/ppermute | solution.py:326
